TPU v7x, 32 devices: a whole 2x2x4 slice. The times are simulated.
32 devices in a mesh: chan: 8 (over y, x, core), int: 4 (over z).
Axes of the slice: x: 2, y: 2, z: 4, core: 2. Of those that a mesh axis runs over, the one named last changes fastest.
Arguments:
- t_pp: bfloat16 [32768, 2048], P(('chan', 'int')), may hold values from -6 to 6
- interaction: bfloat16 [4, 2048, 2048], P(None, None, 'int'), may hold values from -0.125 to 0.125
- send_order: int32 [32768], P(('chan', 'int')), may hold values from 0 to 1023, as said below
- recv_order: int32 [32768], P(('chan', 'int')), may hold values from 0 to 1023, as said below
- ph_channel: int32 [32768], P('chan'), may hold values from 0 to 4, as said below
- recouple_weight: float32 [32768], P('chan'), may hold values from -1.5 to 1.5
Outputs:
- term_pp: bfloat16 [32768, 2048], P(('chan', 'int'))
Inputs may be any that keep to these rules, and one draw needn't show every extreme that they name: `send_order`: within each device's 1024 slots a permutation of its local rows. `recv_order`: within each device's 1024 slots a permutation of its received rows. `ph_channel`: non-decreasing within each device's 1024 slots; the value 4 marks empty slots, which come last; some device has no empty slot.
All inputs are finite; a program needn't handle non-finite values.
Results may differ from a plain program's by a relative error of at most 0.001.
Values may be sent and summed in bfloat16 or wider, within the bound.
No kernel may reach another device: no remote copies, remote signals or barrier semaphores. Data moves between devices by JAX's collectives and lax.ppermute only.
A program may use at most 128 MiB of HBM per device.

v0:
```python
import jax
import jax.numpy as jnp
from jax import lax
from jax.sharding import PartitionSpec as P


def channel_counts(channel_ids, channels):
    table = channel_ids[:, None] == jnp.arange(channels, dtype=jnp.int32)[None, :]
    return jnp.sum(table.astype(jnp.int32), axis=0)


def finish(product, channel_ids, scale, channels):
    live = (channel_ids < channels)[:, None]
    return jnp.where(live, scale[:, None] * product, jnp.float32(0.0)).astype(jnp.bfloat16)


def on_device(t_pp, interaction, send_order, recv_order, ph_channel, recouple_weight):
    slot_count = t_pp.shape[0]
    channels = interaction.shape[0]
    outgoing = jnp.take(t_pp, send_order, axis=0)
    arrived = lax.all_to_all(outgoing, "chan", split_axis=0, concat_axis=0, tiled=True)
    ph_rows = jnp.take(arrived, recv_order, axis=0)
    group_size = lax.axis_size("int")
    everyone = lax.all_gather(ph_rows, "int", axis=0, tiled=True)
    shares = []
    for member in range(group_size):
        member_ids = ph_channel[member * slot_count : (member + 1) * slot_count]
        member_scale = recouple_weight[member * slot_count : (member + 1) * slot_count]
        member_rows = everyone[member * slot_count : (member + 1) * slot_count]
        product = lax.ragged_dot(
            member_rows,
            interaction,
            channel_counts(member_ids, channels),
            preferred_element_type=jnp.float32,
        )
        shares.append(finish(product, member_ids, member_scale, channels))
    column_shares = jnp.concatenate(shares, axis=0)
    z_ph = lax.all_to_all(column_shares, "int", split_axis=0, concat_axis=1, tiled=True)
    back_rows = jnp.zeros_like(z_ph).at[recv_order].set(z_ph)
    returned = lax.all_to_all(back_rows, "chan", split_axis=0, concat_axis=0, tiled=True)
    return jnp.zeros_like(returned).at[send_order].set(returned)


def solution(mesh):
    in_specs = (
        P(("chan", "int"), None),
        P(None, None, "int"),
        P(("chan", "int")),
        P(("chan", "int")),
        P("chan"),
        P("chan"),
    )
    out_specs = P(("chan", "int"), None)
    return jax.shard_map(
        on_device, mesh=mesh, in_specs=in_specs, out_specs=out_specs, check_vma=False
    )
```

profile of v0, /device:TPU:0, one launch (start us, length us, event | category | flops | bytes accessed | tf_op | source)
XLA Modules:
  0.0 620.5 jit_solution(15126764704496646289)
XLA Ops:
  6.5 0.7 broadcast_clamp_fusion.1
  7.2 0.7 compare_and_fusion.1
  7.9 11.5 %gather_fusion = bf16[1024,2048]{1,0:T(8,128)(2,1)} fusion(bf16[1024,2048]{1,0:T(8,128)(2,1)} %param.8, s32[1024]{0:T(1024)S(1)} %get-tuple-element.40), kind=kCustom, calls=%fused_computation.clone | custom fusion | bytes 8392704 | tf_op jit(solution)/shard_map/jit(_take)/gather | solution.py:20
  19.5 4.6 broadcast_select_fusion.1
  24.1 0.0 copy-start.1
  24.1 5.3 all-to-all-start
  29.4 0.0 all-gather.2.cloned.1.call-start
  29.5 0.0 copy-done.1
  29.5 49.1 %all-to-all-done = bf16[8,128,2048]{2,1,0:T(8,128)(2,1)} async-done(((bf16[8,128,2048]{2,1,0:T(8,128)(2,1)}), bf16[8,128,2048]{2,1,0:T(8,128)(2,1)}, u32[]{:S(2)}, u32[]{:S(2)}) %all-to-all-start) | async-done | bytes 4194336 | tf_op jit(solution)/shard_map/all_to_all | solution.py:21
  78.6 11.5 %gather_fusion.1 = bf16[1024,2048]{1,0:T(8,128)(2,1)} fusion(bf16[1024,2048]{1,0:T(8,128)(2,1)} %bitcast.1, s32[1024]{0:T(1024)S(1)} %get-tuple-element.38), kind=kCustom, calls=%fused_computation.1.clone | custom fusion | bytes 8392704 | tf_op jit(solution)/shard_map/jit(_take)/gather | solution.py:22
  90.2 4.6 broadcast_select_fusion
  94.8 0.0 copy-start
  94.8 0.0 copy-start.2
  94.8 0.0 all-gather.2.cloned.1.call-update
  94.8 0.7 copy-done
  95.5 0.7 convert_reduce_fusion
  96.3 1.4 ragged-dot-metadata
  97.7 1.4 ragged-dot-metadata.1
  99.0 0.7 convert_reduce_fusion.2
  99.7 1.4 ragged-dot-metadata.2
  101.1 1.4 ragged-dot-metadata.3
  102.5 0.0 copy-done.2
  102.5 279.4 %all-gather.2.cloned.1.call-done = bf16[4096,2048]{1,0:T(8,128)(2,1)} async-done(((bf16[1024,2048]{1,0:T(8,128)(2,1)}), bf16[4096,2048]{1,0:T(8,128)(2,1)}) %all-gather.2.cloned.1.call-update) | async-done | bytes 16777232 | tf_op jit(solution)/shard_map/all_gather | solution.py:24
  381.9 12.4 %fusion.4 = (bf16[1024,2048]{1,0:T(8,128)(2,1)}, bf16[1024,2048]{1,0:T(8,128)(2,1)}, bf16[1024,2048]{1,0:T(8,128)(2,1)}, bf16[1024,2048]{1,0:T(8,128)(2,1)}) fusion(bf16[4096,2048]{1,0:T(8,128)(2,1)} %all-gather.2.cloned.1.call-done), kind=kLoop, calls=%fused_computation.33 | loop fusion | bytes 33554432 | tf_op jit(solution)/shard_map/slice | solution.py:29
  394.3 6.0 ragged-dot-none
  400.3 1.9 select_convert_fusion
  402.3 7.3 %ragged-dot-none.1 = f32[1024,512]{1,0:T(8,128)} custom-call(s32[1]{0:T(128)} %get-tuple-element.10, s32[5]{0:T(128)} %get-tuple-element.11, s32[7]{0:T(128)} %get-tuple-element.12, s32[7]{0:T(128)} %get-tuple-element.13, s32[1]{0:T(128)} %get-tuple-element.10, bf16[1024,2048]{1,0:T(8,128)(2,1)} %get-tuple-element.24, bf16[4,2048,512]{2,1,0:T(8,128)(2,1)} %param.9), custom_call_target="tpu_custom_call" | custom-call | flops 2147483648 | bytes 14680080 | tf_op jit(solution)/shard_map/ragged_dot_general/ragged-dot-none
  409.6 1.9 select_convert_fusion.1
  411.6 9.9 %ragged-dot-none.2 = f32[1024,512]{1,0:T(8,128)} custom-call(s32[1]{0:T(128)} %get-tuple-element.14, s32[5]{0:T(128)} %get-tuple-element.15, s32[7]{0:T(128)} %get-tuple-element.16, s32[7]{0:T(128)} %get-tuple-element.17, s32[1]{0:T(128)} %get-tuple-element.14, bf16[1024,2048]{1,0:T(8,128)(2,1)} %get-tuple-element.25, bf16[4,2048,512]{2,1,0:T(8,128)(2,1)} %param.9), custom_call_target="tpu_custom_call" | custom-call | flops 2147483648 | bytes 14680080 | tf_op jit(solution)/shard_map/ragged_dot_general/ragged-dot-none
  421.5 1.9 select_convert_fusion.2
  423.4 8.2 %ragged-dot-none.3 = f32[1024,512]{1,0:T(8,128)} custom-call(s32[1]{0:T(128)} %get-tuple-element.18, s32[5]{0:T(128)} %get-tuple-element.19, s32[7]{0:T(128)} %get-tuple-element.20, s32[7]{0:T(128)} %get-tuple-element.21, s32[1]{0:T(128)} %get-tuple-element.18, bf16[1024,2048]{1,0:T(8,128)(2,1)} %get-tuple-element.22, bf16[4,2048,512]{2,1,0:T(8,128)(2,1)} %param.9), custom_call_target="tpu_custom_call" | custom-call | flops 2147483648 | bytes 14680080 | tf_op jit(solution)/shard_map/ragged_dot_general/ragged-dot-none
  431.6 1.9 select_convert_fusion.3
  433.5 0.3 pad_maximum_fusion
  433.9 94.5 %all_to_all.43 = bf16[4,1024,512]{2,1,0:T(8,128)(2,1)S(1)} all-to-all(bf16[4,1024,512]{2,1,0:T(8,128)(2,1)S(1)} %bitcast.9), channel_id=1, replica_groups=mesh['chan'=8,'int'=4] {'int'}, dimensions={0} | all-to-all | bytes 8388608 | tf_op jit(solution)/shard_map/all_to_all | solution.py:38
  528.3 2.7 copy.10
  531.0 10.0 %scatter_custom_fusion = bf16[1024,2048]{1,0:T(8,128)(2,1)} fusion(s32[1024]{0:T(1024)S(1)} %get-tuple-element.39, bf16[1024,2048]{1,0:T(8,128)(2,1)} %bitcast.13, bf16[]{:T(256)} %constant.0.clone.1), kind=kCustom, calls=%fused_computation.13 | custom fusion | bytes 4194816 | tf_op jit(solution)/shard_map/scatter | solution.py:39
  541.0 62.5 %all_to_all.44 = bf16[8,128,2048]{2,1,0:T(8,128)(2,1)} all-to-all(bf16[8,128,2048]{2,1,0:T(8,128)(2,1)} %bitcast.10), channel_id=1, replica_groups=mesh['chan'=8,'int'=4] {'chan'}, dimensions={0} | all-to-all | bytes 8388608 | tf_op jit(solution)/shard_map/all_to_all | solution.py:40
  603.6 10.1 %scatter_custom_fusion.1 = bf16[1024,2048]{1,0:T(8,128)(2,1)} fusion(s32[1024]{0:T(1024)S(1)} %get-tuple-element.41, bf16[1024,2048]{1,0:T(8,128)(2,1)} %bitcast.12, bf16[]{:T(256)} %constant.0.clone.1), kind=kCustom, calls=%fused_computation.11 | custom fusion | bytes 4194816 | tf_op jit(solution)/shard_map/scatter | solution.py:41
  (5 shorter events, 0.0 us)
Async XLA Ops:
  24.1 5.4 copy-start.1
  24.1 54.5 %all-to-all-start = ((bf16[8,128,2048]{2,1,0:T(8,128)(2,1)}), bf16[8,128,2048]{2,1,0:T(8,128)(2,1)}, u32[]{:S(2)}, u32[]{:S(2)}) async-start(bf16[8,128,2048]{2,1,0:T(8,128)(2,1)} %bitcast.8), calls=%async_computation | async-start | bytes 8388608 | tf_op jit(solution)/shard_map/all_to_all | solution.py:21
  29.4 352.5 %all-gather.2.cloned.1.call-start = ((), (), s32[]{:S(2)}) async-start(), calls=%async_computation.3 | async-start | bytes 20971520 | tf_op jit(solution)/shard_map/all_gather | solution.py:24
  94.8 0.7 copy-start
  94.8 7.7 %copy-start.2 = (f32[4096]{0:T(1024)S(1)}, f32[4096]{0:T(1024)}, u32[]{:S(2)}) copy-start(f32[4096]{0:T(1024)} %param.13) | copy-start | bytes 49156
Sparse Core Ops, SparseCore 0:
  95.0 286.9 all-gather.1
where the time goes:
time: 621 us
  waiting for transfers between devices  329 us (53%)
  blocking collectives  157 us (25%)
  local copies, waits for them, and re-layouts  59 us (10%)
  Pallas kernels  36.9 us (6%)
  other arithmetic  20.2 us (3%)
  between operations  13.5 us (2%)
    all_gather x1, waiting for transfers between devices, on_device(): everyone = lax.all_gather(ph_rows, 'int', axis=0, tiled=True)  279 us
    all_to_all x1, blocking collectives, on_device(): lax.all_to_all(column_shares, 'int', split_axis=0, concat_axis=1, tiled=T...  94.5 us
    all_to_all x1, blocking collectives, on_device(): lax.all_to_all(back_rows, 'chan', split_axis=0, concat_axis=0, tiled=True)  62.5 us
    all_to_all x1, waiting for transfers between devices, on_device(): lax.all_to_all(outgoing, 'chan', split_axis=0, concat_axis=0, tiled=True)  49.1 us
    another operation x4, Pallas kernels  31.5 us
  transfers between devices with their start and end apart: 2, of which 2 were waited for; matrix products, arithmetic and copies ran while one was open for 0% of the time, Pallas kernels for 1%

commit v1 on v0

v1 whole, which is shorter than its diff:
```python
import functools

import jax
import jax.numpy as jnp
from jax import lax
from jax.experimental import pallas as pl
from jax.experimental.pallas import tpu as pltpu
from jax.sharding import PartitionSpec as P

VMEM_BYTES = 48 * 1024 * 1024


def multiply_body(layout, scalars, t_ref, meta_ref, *refs):
    out_ref = refs[-1]
    result = refs[-2][...]
    channel_ids = meta_ref[:, 0:1]
    scale = meta_ref[:, 1:2]
    place, used = 1, 0
    for row_counts in layout:
        channel = scalars[place].astype(jnp.float32)
        place += 1
        product = None
        for count in row_counts:
            first = pl.multiple_of(scalars[place], 256)
            part = jnp.dot(
                t_ref[:, pl.ds(first, count)], refs[used][...], preferred_element_type=jnp.float32
            )
            product = part if product is None else product + part
            place += 1
            used += 1
        result = jnp.where(channel_ids == channel, (scale * product).astype(result.dtype), result)
    out_ref[...] = result


def multiply(out, t_pp, meta, column_block, blocks):
    slots, depth = t_pp.shape
    tile = min(256, slots)
    arrays = [rows for _, parts in blocks for _, rows in parts]
    width = arrays[0].shape[1]
    layout = tuple(tuple(rows.shape[0] for _, rows in parts) for _, parts in blocks)
    scalars = [column_block]
    for channel, parts in blocks:
        scalars.append(channel)
        scalars.extend(first for first, _ in parts)
    scalars = jnp.stack([jnp.asarray(value, jnp.int32) for value in scalars])
    row_total = sum(rows.shape[0] for rows in arrays)
    grid_spec = pltpu.PrefetchScalarGridSpec(
        num_scalar_prefetch=1,
        grid=(slots // tile,),
        in_specs=[
            pl.BlockSpec((tile, depth), lambda i, s: (i, 0)),
            pl.BlockSpec((tile, meta.shape[1]), lambda i, s: (i, 0)),
            *[pl.BlockSpec(rows.shape, lambda i, s: (0, 0)) for rows in arrays],
            pl.BlockSpec((tile, width), lambda i, s: (i, s[0])),
        ],
        out_specs=pl.BlockSpec((tile, width), lambda i, s: (i, s[0])),
    )
    return pl.pallas_call(
        functools.partial(multiply_body, layout),
        grid_spec=grid_spec,
        out_shape=jax.ShapeDtypeStruct(out.shape, out.dtype),
        input_output_aliases={3 + len(arrays): 0},
        cost_estimate=pl.CostEstimate(
            flops=2 * slots * row_total * width,
            bytes_accessed=2 * (slots * depth + row_total * width + 2 * slots * width),
            transcendentals=0,
        ),
        compiler_params=pltpu.CompilerParams(vmem_limit_bytes=VMEM_BYTES),
    )(scalars, t_pp, meta, *arrays, out)


def inverse_take(order, values):
    hit = order[None, :] == jnp.arange(order.shape[0], dtype=order.dtype)[:, None]
    return [jnp.sum(jnp.where(hit, value[None, :], 0.0), axis=1) for value in values]


def row_meta(send_order, recv_order, ph_channel, recouple_weight):
    slots = send_order.shape[0]
    group = lax.axis_size("chan")
    member = lax.axis_index("int") * slots
    ids = lax.dynamic_slice(ph_channel, (member,), (slots,)).astype(jnp.float32)
    scale = lax.dynamic_slice(recouple_weight, (member,), (slots,))
    back = jnp.stack(inverse_take(recv_order, [ids, scale]), axis=0)
    back = back.reshape(2, group, slots // group).transpose(1, 0, 2)
    back = lax.all_to_all(back, "chan", split_axis=0, concat_axis=0, tiled=True)
    back = back.transpose(1, 0, 2).reshape(2, slots)
    ids, scale = inverse_take(send_order, [back[0], back[1]])
    lane = jnp.arange(128)[None, :]
    return jnp.where(lane == 0, ids[:, None], jnp.where(lane == 1, scale[:, None], 0.0))


def general_plan(t_pp, interaction, meta):
    slots, depth = t_pp.shape
    channels, _, width = interaction.shape
    group, members = lax.axis_size("chan"), lax.axis_size("int")
    flat = interaction.reshape(channels * depth, width)
    share = flat.shape[0] // group
    mine = lax.dynamic_slice(flat, (lax.axis_index("chan") * share, 0), (share, width))
    everyone = lax.all_gather(mine, ("chan", "int"), axis=0, tiled=False)
    everyone = everyone.reshape(group, members, share, width)
    out = jnp.zeros((slots, members * width), t_pp.dtype)
    for member in range(members):
        whole = everyone[:, member].reshape(channels, depth, width)
        for channel in range(channels):
            out = multiply(out, t_pp, meta, member, [(channel, [(0, whole[channel])])])
    return out


def grid_plan(t_pp, interaction, meta_of):
    slots, depth = t_pp.shape
    channels, _, width = interaction.shape
    group, members = lax.axis_size("chan"), lax.axis_size("int")
    axes = ("chan", "int")
    c, z = lax.axis_index("chan"), lax.axis_index("int")
    core, chip = c % 2, c // 2
    half = depth // 2

    def at(chan, member):
        return chan * members + member

    along = []
    for chan in range(group):
        for member in range(members):
            target = member - 1 if chan % 2 == 0 else member + 1
            if 0 <= target < members:
                along.append((at(chan, member), at(chan, target)))
    pair = [(at(a, m), at(a, m ^ 1)) for a in range(group) for m in range(members)]
    plane = [
        (at(a, m), at(a ^ (2 if a % 2 == 0 else 4), m)) for a in range(group) for m in range(members)
    ]
    other = [(a, a ^ 1) for a in range(group)]

    def sib(x):
        return lax.ppermute(x, "chan", other)

    flat = interaction.reshape(channels * depth, width)

    def own_rows(channel, first, count):
        return lax.dynamic_slice(flat, (channel * depth + first, 0), (count, width))

    sent = [own_rows(chip, 0, half), own_rows(chip, half, half)]
    steps = []
    for step in range(members - 1):
        sent = [lax.ppermute(x, axes, along) for x in sent]
        steps.append(sent)
    extra = lax.ppermute(own_rows(chip ^ 3, core * half, half), axes, pair)

    met = [[sib(x) for x in got] for got in steps]

    end = (z == 0) | (z == members - 1)
    low = z < members // 2
    down = core == 0

    def pick(wanted_down, a, b):
        return jnp.where(wanted_down == down, a, b)

    slot_rows = [[pick(z % 2 == 0, steps[0][h], met[0][h]) for h in range(2)]]
    for step in (0, 1):
        slot_rows.append(
            [
                pick(
                    low,
                    jnp.where(end, steps[step + 1][h], steps[step][h]),
                    jnp.where(end, met[step + 1][h], met[step][h]),
                )
                for h in range(2)
            ]
        )
    block_of = [z ^ 1, jnp.where(low, 2, 1), jnp.where(low, 3, 0)]

    meta = meta_of()
    out = jnp.zeros((slots, members * width), t_pp.dtype)
    for channel in range(channels):
        out = multiply(out, t_pp, meta, z, [(channel, [(0, interaction[channel])])])

    near = chip ^ (1 + core)
    far = chip ^ (2 - core)
    mine, theirs = core * half, (1 - core) * half
    extra_sib = sib(extra)
    for slot in range(3):
        column = block_of[slot]
        a, b = slot_rows[slot]
        got = [lax.ppermute(x, axes, plane) for x in (a, b)]
        got_sib = [sib(x) for x in got]
        out = multiply(out, t_pp, meta, column, [(chip, [(0, a), (half, b)])])
        out = multiply(out, t_pp, meta, column, [(near, [(0, got[0]), (half, got[1])])])
        out = multiply(out, t_pp, meta, column, [(far, [(0, got_sib[0]), (half, got_sib[1])])])
        if slot == 0:
            across, across_sib = extra, extra_sib
        else:
            across = lax.ppermute(jnp.where(core == 0, got_sib[0], got_sib[1]), axes, plane)
            across_sib = sib(across)
        out = multiply(out, t_pp, meta, column, [(chip ^ 3, [(mine, across), (theirs, across_sib)])])
    return out


def on_device(t_pp, interaction, send_order, recv_order, ph_channel, recouple_weight):
    meta_of = functools.partial(row_meta, send_order, recv_order, ph_channel, recouple_weight)
    planes = lax.axis_size("chan") // 2
    if planes == 4 and lax.axis_size("int") == 4 and interaction.shape[0] == planes:
        return grid_plan(t_pp, interaction, meta_of)
    return general_plan(t_pp, interaction, meta_of())


def solution(mesh):
    in_specs = (
        P(("chan", "int"), None),
        P(None, None, "int"),
        P(("chan", "int")),
        P(("chan", "int")),
        P("chan"),
        P("chan"),
    )
    out_specs = P(("chan", "int"), None)
    return jax.shard_map(
        on_device, mesh=mesh, in_specs=in_specs, out_specs=out_specs, check_vma=False
    )
```

time: 621 us -> 254 us (0.41)
  waiting for transfers between devices: 329 us -> 90 us
  blocking collectives: 157 us -> 0 us
  Pallas kernels: 36.9 us -> 102 us
  local copies, waits for them, and re-layouts: 59 us -> 13 us
  starting transfers between devices: 5.34 us -> 31.6 us
  between operations: 13.5 us -> 0.18 us
    all_gather x1 -> x0, waiting for transfers between devices: 279 us -> none  [on_device(): everyone = lax.all_gather(ph_rows, 'int', axis=0, tiled=True)]
    all_to_all x2 -> x0, blocking collectives: 157 us -> none  [the longest x1 94.5 us: on_device(): lax.all_to_all(column_shares, 'int', split_axis=0, concat_axis=1, tiled=T...]
    pallas_call x0 -> x16, Pallas kernels: none -> 102 us  [multiply(): pl.pallas_call(functools.partial(multiply_body, layout), grid_spec=grid_s...]
    ppermute x0 -> x30, waiting for transfers between devices: none -> 90 us  [the longest x6 59.7 us: grid_plan(): sent = [lax.ppermute(x, axes, along) for x in sent]]
    all_to_all x1, waiting for transfers between devices: 49.1 us -> 0.01 us  [row_meta(): back = lax.all_to_all(back, 'chan', split_axis=0, concat_axis=0, tiled=True)]
    another operation x4 -> x0, Pallas kernels: 31.5 us -> none
    ppermute x0 -> x30, starting transfers between devices: none -> 27.3 us  [the longest x6 8.46 us: grid_plan(): got = [lax.ppermute(x, axes, plane) for x in (a, b)]]
    gather x2 -> x0, local copies, waits for them, and re-layouts: 23.1 us -> none  [the longest x1 11.5 us: on_device(): ph_rows = jnp.take(arrived, recv_order, axis=0)]
  transfers between devices with their start and end apart: 2 -> 31, of which waited for: 2 -> 10; matrix products, arithmetic and copies ran while one was open for 0% -> 10% of each run, Pallas kernels for 1% -> 38%
where the time goes in v1:
time: 254 us; the launch traced here: 253 us
  Pallas kernels  102 us (40%)
  waiting for transfers between devices  90 us (35%)
  starting transfers between devices  31.6 us (12%)
  other arithmetic  16.2 us (6%)
  local copies, waits for them, and re-layouts  13 us (5%)
    pallas_call x16, Pallas kernels, multiply(): pl.pallas_call(functools.partial(multiply_body, layout), grid_spec=grid_s...  102 us
    ppermute x6, waiting for transfers between devices, grid_plan(): sent = [lax.ppermute(x, axes, along) for x in sent]  59.7 us
    ppermute x6, waiting for transfers between devices, grid_plan(): got = [lax.ppermute(x, axes, plane) for x in (a, b)]  30.2 us
    select_n x2, other arithmetic, pick(): return jnp.where(wanted_down == down, a, b)  8.53 us
    ppermute x6, starting transfers between devices, grid_plan(): got = [lax.ppermute(x, axes, plane) for x in (a, b)]  8.46 us
    ppermute x15, starting transfers between devices, sib(): return lax.ppermute(x, 'chan', other)  8.02 us
    ppermute x6, starting transfers between devices, grid_plan(): sent = [lax.ppermute(x, axes, along) for x in sent]  7.69 us
    squeeze x1, local copies, waits for them, and re-layouts, grid_plan(): out = multiply(out, t_pp, meta, z, [(channel, [(0, interaction[channel])])])  5.65 us
  transfers between devices with their start and end apart: 31, of which 10 were waited for; matrix products, arithmetic and copies ran while one was open for 10% of the time, Pallas kernels for 38%

profile of v1, /device:TPU:0, one launch (start us, length us, event | category | flops | bytes accessed | tf_op | source)
XLA Modules:
  0.0 252.9 jit_solution(14629423050772420946)
XLA Ops:
  0.0 3.1 %constant_dynamic-slice_fusion = (bf16[1024,512]{1,0:T(8,128)(2,1)}, bf16[1024,512]{1,0:T(8,128)(2,1)S(1)}, bf16[1024,512]{1,0:T(8,128)(2,1)S(1)}) fusion(bf16[8192,512]{1,0:T(8,128)(2,1)} %bitcast.26, s32[]{:T(128)S(6)} %select_n.162, s32[]{:T(128)S(6)} %select_n.149, s32[]{:T(128)S(6)} %select_n.145), kind=kLoop, calls=%fused_computation.21 | loop fusion | bytes 6291468 | tf_op jit(solution)/shard_map/dynamic_slice | solution.py:139
  3.1 1.3 collective-permute-start.7
  4.3 1.3 collective-permute-start
  5.6 15.1 %collective-permute-done.7 = bf16[1024,512]{1,0:T(8,128)(2,1)S(1)} collective-permute-done((bf16[1024,512]{1,0:T(8,128)(2,1)S(1)}, bf16[1024,512]{1,0:T(8,128)(2,1)S(1)}, u32[]{:S(2)}, u32[]{:S(2)}) %collective-permute-start.7) | collective-permute-done | bytes 1048608 | tf_op jit(solution)/shard_map/ppermute | solution.py:144
  20.7 1.3 collective-permute-start.8
  22.0 9.9 %collective-permute-done = bf16[1024,512]{1,0:T(8,128)(2,1)S(1)} collective-permute-done((bf16[1024,512]{1,0:T(8,128)(2,1)S(1)}, bf16[1024,512]{1,0:T(8,128)(2,1)S(1)}, u32[]{:S(2)}, u32[]{:S(2)}) %collective-permute-start) | collective-permute-done | bytes 1048608 | tf_op jit(solution)/shard_map/ppermute | solution.py:144
  32.0 1.3 collective-permute-start.1
  33.3 9.9 %collective-permute-done.8 = bf16[1024,512]{1,0:T(8,128)(2,1)S(1)} collective-permute-done((bf16[1024,512]{1,0:T(8,128)(2,1)S(1)}, bf16[1024,512]{1,0:T(8,128)(2,1)S(1)}, u32[]{:S(2)}, u32[]{:S(2)}) %collective-permute-start.8) | collective-permute-done | bytes 1048608 | tf_op jit(solution)/shard_map/ppermute | solution.py:144
  43.2 1.3 collective-permute-start.9
  44.5 2.3 collective-permute-start.19
  46.9 7.7 %collective-permute-done.1 = bf16[1024,512]{1,0:T(8,128)(2,1)} collective-permute-done((bf16[1024,512]{1,0:T(8,128)(2,1)S(1)}, bf16[1024,512]{1,0:T(8,128)(2,1)}, u32[]{:S(2)}, u32[]{:S(2)}) %collective-permute-start.1) | collective-permute-done | bytes 1048608 | tf_op jit(solution)/shard_map/ppermute | solution.py:144
  54.6 1.3 collective-permute-start.2
  55.8 2.3 collective-permute-start.11
  58.2 7.6 %collective-permute-done.9 = bf16[1024,512]{1,0:T(8,128)(2,1)} collective-permute-done((bf16[1024,512]{1,0:T(8,128)(2,1)S(1)}, bf16[1024,512]{1,0:T(8,128)(2,1)}, u32[]{:S(2)}, u32[]{:S(2)}) %collective-permute-start.9) | collective-permute-done | bytes 1048608 | tf_op jit(solution)/shard_map/ppermute | solution.py:144
  65.8 0.7 dynamic_slice.16
  66.5 0.7 dynamic-slice_convert_fusion
  67.2 0.5 collective-permute-start.16
  67.7 9.3 %collective-permute-done.2 = bf16[1024,512]{1,0:T(8,128)(2,1)} collective-permute-done((bf16[1024,512]{1,0:T(8,128)(2,1)}, bf16[1024,512]{1,0:T(8,128)(2,1)}, u32[]{:S(2)}, u32[]{:S(2)}) %collective-permute-start.2) | collective-permute-done | bytes 1048608 | tf_op jit(solution)/shard_map/ppermute | solution.py:144
  77.0 1.2 select_reduce_fusion.3
  78.3 0.6 maximum_bitcast_fusion
  78.9 4.3 %all-to-all-start = ((f32[8,2,128]{2,1,0:T(2,128)}), f32[8,2,128]{2,1,0:T(2,128)S(1)}, u32[]{:S(2)}, u32[]{:S(2)}) async-start(f32[8,2,128]{2,1,0:T(2,128)} %maximum_bitcast_fusion), calls=%async_computation | async-start | bytes 16384 | tf_op jit(solution)/shard_map/all_to_all | solution.py:85
  83.4 1.6 collective-permute-start.24
  85.0 4.1 %broadcast_select_fusion = (bf16[1024,512]{1,0:T(8,128)(2,1)}, bf16[1024,512]{1,0:T(8,128)(2,1)S(1)}, bf16[1024,512]{1,0:T(8,128)(2,1)S(1)}) fusion(bf16[1024,512]{1,0:T(8,128)(2,1)} %copy-done.10, bf16[1024,512]{1,0:T(8,128)(2,1)} %collective-permute-done.19, pred[]{:T(512)S(6)} %eq.92, bf16[1024,512]{1,0:T(8,128)(2,1)} %collective-permute-done.11, ...), kind=kLoop, calls=%fused_computation.14 | loop fusion | flops 3670016 | bytes 9437187 | tf_op jit(solution)/shard_map/jit(_where)/select_n | solution.py:155
  89.1 2.0 collective-permute-start.20
  91.1 4.4 %broadcast_select_fusion.1 = (bf16[1024,512]{1,0:T(8,128)(2,1)}, bf16[1024,512]{1,0:T(8,128)(2,1)S(1)}, bf16[1024,512]{1,0:T(8,128)(2,1)}) fusion(bf16[1024,512]{1,0:T(8,128)(2,1)} %copy-done.9, bf16[1024,512]{1,0:T(8,128)(2,1)} %collective-permute-done.16, pred[]{:T(512)S(6)} %eq.92, bf16[1024,512]{1,0:T(8,128)(2,1)} %collective-permute-done.4, ...), kind=kLoop, calls=%fused_computation.15 | loop fusion | flops 3670016 | bytes 9437187 | tf_op jit(solution)/shard_map/jit(_where)/select_n | solution.py:155
  95.6 0.4 collective-permute-start.17
  95.9 1.0 copy-done.5
  97.5 0.1 pad_add_fusion.8
  97.6 0.1 pad_add_fusion.18
  97.7 1.7 collective-permute-start.12
  99.3 0.4 collective-permute-start.5
  99.7 4.3 %collective-permute-done.20.refs_1_ = bf16[1024,512]{1,0:T(8,128)(2,1)} collective-permute-done((bf16[1024,512]{1,0:T(8,128)(2,1)S(1)}, bf16[1024,512]{1,0:T(8,128)(2,1)}, u32[]{:S(2)}, u32[]{:S(2)}) %collective-permute-start.20) | collective-permute-done | bytes 1048608 | tf_op jit(solution)/shard_map/ppermute | solution.py:183
  104.0 11.2 %collective-permute-done.17.refs_0_ = bf16[1024,512]{1,0:T(8,128)(2,1)} collective-permute-done((bf16[1024,512]{1,0:T(8,128)(2,1)S(1)}, bf16[1024,512]{1,0:T(8,128)(2,1)}, u32[]{:S(2)}, u32[]{:S(2)}) %collective-permute-start.17) | collective-permute-done | bytes 1048608 | tf_op jit(solution)/shard_map/ppermute | solution.py:183
  115.2 5.6 %slice_bitcast_fusion = (bf16[2048,512]{1,0:T(8,128)(2,1)}, bf16[2048,512]{1,0:T(8,128)(2,1)}, bf16[2048,512]{1,0:T(8,128)(2,1)S(1)}, bf16[2048,512]{1,0:T(8,128)(2,1)}) fusion(bf16[4,2048,512]{2,1,0:T(8,128)(2,1)} %param.7), kind=kLoop, calls=%fused_computation.6 | loop fusion | bytes 16777216 | tf_op jit(solution)/shard_map/squeeze | solution.py:174
  121.0 5.5 %collective-permute-done.12.refs_1_ = bf16[1024,512]{1,0:T(8,128)(2,1)} collective-permute-done((bf16[1024,512]{1,0:T(8,128)(2,1)S(1)}, bf16[1024,512]{1,0:T(8,128)(2,1)}, u32[]{:S(2)}, u32[]{:S(2)}) %collective-permute-start.12) | collective-permute-done | bytes 1048608 | tf_op jit(solution)/shard_map/ppermute | solution.py:183
  126.5 2.0 collective-permute-start.28
  128.5 9.2 %collective-permute-done.5.refs_0_ = bf16[1024,512]{1,0:T(8,128)(2,1)} collective-permute-done((bf16[1024,512]{1,0:T(8,128)(2,1)}, bf16[1024,512]{1,0:T(8,128)(2,1)}, u32[]{:S(2)}, u32[]{:S(2)}) %collective-permute-start.5) | collective-permute-done | bytes 1048608 | tf_op jit(solution)/shard_map/ppermute | solution.py:183
  137.7 2.0 collective-permute-start.26
  139.7 1.2 select_reduce_fusion.1
  141.1 0.5 collective-permute-start.6
  141.6 0.3 select_select_fusion.4.meta_ref
  141.9 2.5 %broadcast_in_dim.94.refs_1_ = bf16[1024,2048]{1,0:T(8,128)(2,1)} broadcast(bf16[]{:T(256)} %constant.69.clone.1), dimensions={} | broadcast | bytes 4194306 | tf_op jit(solution)/shard_map/broadcast_in_dim | solution.py:172
  144.4 6.2 %shard_map.64.refs_1_ = bf16[1024,2048]{1,0:T(8,128)(2,1)} custom-call(s32[3]{0:T(128)S(1)} %pad.7.scalars, bf16[1024,2048]{1,0:T(8,128)(2,1)} %t_ref.31, f32[1024,128]{1,0:T(8,128)S(1)} %select_select_fusion.4.meta_ref, bf16[2048,512]{1,0:T(8,128)(2,1)S(1)} %copy-done.2, bf16[1024,2048]{1,0:T(8,128)(2,1)} %broadcast_in_dim.94.refs_1_), custom_call_target="tpu_custom_call", output_to_operand_aliasing={{}: (4, {})} | custom-call | flops 2147483648 | bytes 8388608 | tf_op jit(solution)/shard_map/pallas_call | solution.py:58
  150.6 2.5 broadcast_select_fusion.2
  153.1 6.2 %shard_map.65.refs_1_ = bf16[1024,2048]{1,0:T(8,128)(2,1)} custom-call(s32[3]{0:T(128)S(1)} %get-tuple-element.26.scalars, bf16[1024,2048]{1,0:T(8,128)(2,1)} %t_ref.31, f32[1024,128]{1,0:T(8,128)S(1)} %select_select_fusion.4.meta_ref, bf16[2048,512]{1,0:T(8,128)(2,1)S(1)} %copy-done.1, ...), custom_call_target="tpu_custom_call", output_to_operand_aliasing={{}: (4, {})} | custom-call | flops 2147483648 | bytes 8388608 | tf_op jit(solution)/shard_map/pallas_call | solution.py:58
  159.3 1.3 collective-permute-start.29
  160.7 6.2 %shard_map.66.refs_1_ = bf16[1024,2048]{1,0:T(8,128)(2,1)} custom-call(s32[3]{0:T(128)S(1)} %get-tuple-element.27.scalars, bf16[1024,2048]{1,0:T(8,128)(2,1)} %t_ref.31, f32[1024,128]{1,0:T(8,128)S(1)} %select_select_fusion.4.meta_ref, bf16[2048,512]{1,0:T(8,128)(2,1)S(1)} %copy-done, ...), custom_call_target="tpu_custom_call", output_to_operand_aliasing={{}: (4, {})} | custom-call | flops 2147483648 | bytes 8388608 | tf_op jit(solution)/shard_map/pallas_call | solution.py:58
  166.8 0.4 collective-permute-start.25
  167.3 0.1 broadcast_select_fusion.3
  167.4 1.6 collective-permute-start.14
  169.0 6.3 %shard_map.67.refs_2_ = bf16[1024,2048]{1,0:T(8,128)(2,1)} custom-call(s32[3]{0:T(128)S(1)} %pad_add_fusion.20.scalars, bf16[1024,2048]{1,0:T(8,128)(2,1)} %t_ref.31, f32[1024,128]{1,0:T(8,128)S(1)} %select_select_fusion.4.meta_ref, bf16[2048,512]{1,0:T(8,128)(2,1)S(1)} %get-tuple-element.11.refs_0_, ...), custom_call_target="tpu_custom_call", output_to_operand_aliasing={{}: (4, {})} | custom-call | flops 2147483648 | bytes 8388608 | tf_op jit(solution)/shard_map/pallas_call | solution.py:58
  175.2 6.2 %shard_map.68.refs_2_ = bf16[1024,2048]{1,0:T(8,128)(2,1)} custom-call(s32[4]{0:T(128)S(1)} %pad_add_fusion.scalars, bf16[1024,2048]{1,0:T(8,128)(2,1)} %t_ref.31, f32[1024,128]{1,0:T(8,128)S(1)} %select_select_fusion.4.meta_ref, bf16[1024,512]{1,0:T(8,128)(2,1)S(1)} %copy-done.8, bf16[1024,512]{1,0:T(8,128)(2,1)S(1)} %copy-done.7, ...), custom_call_target="tpu_custom_call", output_to_operand_aliasing={{}: (5, {})} | custom-call | flops 2147483648 | bytes 8388608 | tf_op jit(solution)/shard_map/pallas_call | solution.py:58
  181.4 6.2 %shard_map.69.refs_2_ = bf16[1024,2048]{1,0:T(8,128)(2,1)} custom-call(s32[4]{0:T(128)S(1)} %pad_add_fusion.1.scalars, bf16[1024,2048]{1,0:T(8,128)(2,1)} %t_ref.31, f32[1024,128]{1,0:T(8,128)S(1)} %select_select_fusion.4.meta_ref, bf16[1024,512]{1,0:T(8,128)(2,1)S(1)} %collective-permute-done.26.refs_0_, ...), custom_call_target="tpu_custom_call", output_to_operand_aliasing={{}: (5, {})} | custom-call | flops 2147483648 | bytes 8388608 | tf_op jit(solution)/shard_map/pallas_call | solution.py:58
  187.6 6.2 %shard_map.70.refs_2_ = bf16[1024,2048]{1,0:T(8,128)(2,1)} custom-call(s32[4]{0:T(128)S(1)} %pad_add_fusion.2.scalars, bf16[1024,2048]{1,0:T(8,128)(2,1)} %t_ref.31, f32[1024,128]{1,0:T(8,128)S(1)} %select_select_fusion.4.meta_ref, bf16[1024,512]{1,0:T(8,128)(2,1)S(1)} %collective-permute-done.27.refs_0_, ...), custom_call_target="tpu_custom_call", output_to_operand_aliasing={{}: (5, {})} | custom-call | flops 2147483648 | bytes 8388608 | tf_op jit(solution)/shard_map/pallas_call | solution.py:58
  193.8 6.9 %shard_map.71.refs_2_ = bf16[1024,2048]{1,0:T(8,128)(2,1)} custom-call(s32[4]{0:T(128)S(1)} %add_add_fusion.2.scalars, bf16[1024,2048]{1,0:T(8,128)(2,1)} %t_ref.31, f32[1024,128]{1,0:T(8,128)S(1)} %select_select_fusion.4.meta_ref, bf16[1024,512]{1,0:T(8,128)(2,1)} %collective-permute-done.24.refs_0_, ...), custom_call_target="tpu_custom_call", output_to_operand_aliasing={{}: (5, {})} | custom-call | flops 2147483648 | bytes 8388608 | tf_op jit(solution)/shard_map/pallas_call | solution.py:58
  200.7 6.2 %shard_map.72.refs_2_ = bf16[1024,2048]{1,0:T(8,128)(2,1)} custom-call(s32[4]{0:T(128)S(1)} %pad_add_fusion.3.scalars, bf16[1024,2048]{1,0:T(8,128)(2,1)} %t_ref.31, f32[1024,128]{1,0:T(8,128)S(1)} %select_select_fusion.4.meta_ref, bf16[1024,512]{1,0:T(8,128)(2,1)S(1)} %copy-done.6, bf16[1024,512]{1,0:T(8,128)(2,1)S(1)} %copy-done.4, ...), custom_call_target="tpu_custom_call", output_to_operand_aliasing={{}: (5, {})} | custom-call | flops 2147483648 | bytes 8388608 | tf_op jit(solution)/shard_map/pallas_call | solution.py:58
  206.8 0.5 collective-permute-start.15
  207.3 6.9 %shard_map.73.refs_2_ = bf16[1024,2048]{1,0:T(8,128)(2,1)} custom-call(s32[4]{0:T(128)S(1)} %pad_add_fusion.4.scalars, bf16[1024,2048]{1,0:T(8,128)(2,1)} %t_ref.31, f32[1024,128]{1,0:T(8,128)S(1)} %select_select_fusion.4.meta_ref, bf16[1024,512]{1,0:T(8,128)(2,1)} %collective-permute-done.17.refs_0_, ...), custom_call_target="tpu_custom_call", output_to_operand_aliasing={{}: (5, {})} | custom-call | flops 2147483648 | bytes 8388608 | tf_op jit(solution)/shard_map/pallas_call | solution.py:58
  214.2 6.9 %shard_map.74.refs_2_ = bf16[1024,2048]{1,0:T(8,128)(2,1)} custom-call(s32[4]{0:T(128)S(1)} %pad_add_fusion.5.scalars, bf16[1024,2048]{1,0:T(8,128)(2,1)} %t_ref.31, f32[1024,128]{1,0:T(8,128)S(1)} %select_select_fusion.4.meta_ref, bf16[1024,512]{1,0:T(8,128)(2,1)} %collective-permute-done.18.refs_0_, ...), custom_call_target="tpu_custom_call", output_to_operand_aliasing={{}: (5, {})} | custom-call | flops 2147483648 | bytes 8388608 | tf_op jit(solution)/shard_map/pallas_call | solution.py:58
  221.0 6.2 %shard_map.75.refs_2_ = bf16[1024,2048]{1,0:T(8,128)(2,1)} custom-call(s32[4]{0:T(128)S(1)} %add_add_fusion.1.scalars, bf16[1024,2048]{1,0:T(8,128)(2,1)} %t_ref.31, f32[1024,128]{1,0:T(8,128)S(1)} %select_select_fusion.4.meta_ref, bf16[1024,512]{1,0:T(8,128)(2,1)S(1)} %collective-permute-done.22.refs_0_, ...), custom_call_target="tpu_custom_call", output_to_operand_aliasing={{}: (5, {})} | custom-call | flops 2147483648 | bytes 8388608 | tf_op jit(solution)/shard_map/pallas_call | solution.py:58
  227.2 6.5 %shard_map.76.refs_2_ = bf16[1024,2048]{1,0:T(8,128)(2,1)} custom-call(s32[4]{0:T(128)S(1)} %pad_add_fusion.6.scalars, bf16[1024,2048]{1,0:T(8,128)(2,1)} %t_ref.31, f32[1024,128]{1,0:T(8,128)S(1)} %select_select_fusion.4.meta_ref, bf16[1024,512]{1,0:T(8,128)(2,1)} %get-tuple-element.21.refs_0_, ...), custom_call_target="tpu_custom_call", output_to_operand_aliasing={{}: (5, {})} | custom-call | flops 2147483648 | bytes 8388608 | tf_op jit(solution)/shard_map/pallas_call | solution.py:58
  233.7 6.9 %shard_map.77.refs_2_ = bf16[1024,2048]{1,0:T(8,128)(2,1)} custom-call(s32[4]{0:T(128)S(1)} %pad_add_fusion.7.scalars, bf16[1024,2048]{1,0:T(8,128)(2,1)} %t_ref.31, f32[1024,128]{1,0:T(8,128)S(1)} %select_select_fusion.4.meta_ref, bf16[1024,512]{1,0:T(8,128)(2,1)} %collective-permute-done.5.refs_0_, ...), custom_call_target="tpu_custom_call", output_to_operand_aliasing={{}: (5, {})} | custom-call | flops 2147483648 | bytes 8388608 | tf_op jit(solution)/shard_map/pallas_call | solution.py:58
  240.6 6.2 %shard_map.78.refs_2_ = bf16[1024,2048]{1,0:T(8,128)(2,1)} custom-call(s32[4]{0:T(128)S(1)} %get-tuple-element.24.scalars, bf16[1024,2048]{1,0:T(8,128)(2,1)} %t_ref.31, f32[1024,128]{1,0:T(8,128)S(1)} %select_select_fusion.4.meta_ref, bf16[1024,512]{1,0:T(8,128)(2,1)S(1)} %collective-permute-done.6.refs_0_, ...), custom_call_target="tpu_custom_call", output_to_operand_aliasing={{}: (5, {})} | custom-call | flops 2147483648 | bytes 8388608 | tf_op jit(solution)/shard_map/pallas_call | solution.py:58
  246.7 6.2 %shard_map.79 = bf16[1024,2048]{1,0:T(8,128)(2,1)} custom-call(s32[4]{0:T(128)S(1)} %get-tuple-element.25.scalars, bf16[1024,2048]{1,0:T(8,128)(2,1)} %t_ref.31, f32[1024,128]{1,0:T(8,128)S(1)} %select_select_fusion.4.meta_ref, bf16[1024,512]{1,0:T(8,128)(2,1)S(1)} %collective-permute-done.14.refs_0_, ...), custom_call_target="tpu_custom_call", output_to_operand_aliasing={{}: (5, {})} | custom-call | flops 2147483648 | bytes 8388608 | tf_op jit(solution)/shard_map/pallas_call | solution.py:58
  (71 shorter events, 1.1 us)
Async XLA Ops:
  0.0 77.0 %copy-start.12 = (s32[1024]{0:T(1024)S(1)}, s32[1024]{0:T(1024)}, u32[]{:S(2)}) copy-start(s32[1024]{0:T(1024)} %param.9) | copy-start | bytes 12292
  3.1 17.7 %collective-permute-start.7 = (bf16[1024,512]{1,0:T(8,128)(2,1)S(1)}, bf16[1024,512]{1,0:T(8,128)(2,1)S(1)}, u32[]{:S(2)}, u32[]{:S(2)}) collective-permute-start(bf16[1024,512]{1,0:T(8,128)(2,1)S(1)} %get-tuple-element.14), channel_id=1, source_target_pairs={{1,0},{2,1},{3,2},{4,5},{5,6},{6,7},{9,8},{10,9},{11,10},{12,13},{... | collective-permute-start | bytes 3145736 | tf_op jit(solution)/shard_map/ppermute | solution.py:144
  4.3 27.6 %collective-permute-start = (bf16[1024,512]{1,0:T(8,128)(2,1)S(1)}, bf16[1024,512]{1,0:T(8,128)(2,1)S(1)}, u32[]{:S(2)}, u32[]{:S(2)}) collective-permute-start(bf16[1024,512]{1,0:T(8,128)(2,1)S(1)} %get-tuple-element.15), channel_id=1, source_target_pairs={{1,0},{2,1},{3,2},{4,5},{5,6},{6,7},{9,8},{10,9},{11,10},{12,13},{... | collective-permute-start | bytes 3145736 | tf_op jit(solution)/shard_map/ppermute | solution.py:144
  20.7 64.2 %copy-start.10 = (bf16[1024,512]{1,0:T(8,128)(2,1)}, bf16[1024,512]{1,0:T(8,128)(2,1)S(1)}, u32[]{:S(2)}) copy-start(bf16[1024,512]{1,0:T(8,128)(2,1)S(1)} %collective-permute-done.7) | copy-start | bytes 3145732
  20.7 22.5 %collective-permute-start.8 = (bf16[1024,512]{1,0:T(8,128)(2,1)S(1)}, bf16[1024,512]{1,0:T(8,128)(2,1)S(1)}, u32[]{:S(2)}, u32[]{:S(2)}) collective-permute-start(bf16[1024,512]{1,0:T(8,128)(2,1)S(1)} %collective-permute-done.7), channel_id=1, source_target_pairs={{1,0},{2,1},{3,2},{4,5},{5,6},{6,7},{9,8},{10,9},{11,10},{12,13},{... | collective-permute-start | bytes 3145736 | tf_op jit(solution)/shard_map/ppermute | solution.py:144
  32.0 57.1 %copy-start.9 = (bf16[1024,512]{1,0:T(8,128)(2,1)}, bf16[1024,512]{1,0:T(8,128)(2,1)S(1)}, u32[]{:S(2)}) copy-start(bf16[1024,512]{1,0:T(8,128)(2,1)S(1)} %collective-permute-done) | copy-start | bytes 3145732
  32.0 22.6 %collective-permute-start.1 = (bf16[1024,512]{1,0:T(8,128)(2,1)S(1)}, bf16[1024,512]{1,0:T(8,128)(2,1)}, u32[]{:S(2)}, u32[]{:S(2)}) collective-permute-start(bf16[1024,512]{1,0:T(8,128)(2,1)S(1)} %collective-permute-done), channel_id=1, source_target_pairs={{1,0},{2,1},{3,2},{4,5},{5,6},{6,7},{9,8},{10,9},{11,10},{12,13},{... | collective-permute-start | bytes 3145736 | tf_op jit(solution)/shard_map/ppermute | solution.py:144
  43.2 41.8 %copy-start.11 = (bf16[1024,512]{1,0:T(8,128)(2,1)}, bf16[1024,512]{1,0:T(8,128)(2,1)S(1)}, u32[]{:S(2)}) copy-start(bf16[1024,512]{1,0:T(8,128)(2,1)S(1)} %collective-permute-done.8) | copy-start | bytes 3145732
  43.2 22.6 %collective-permute-start.9 = (bf16[1024,512]{1,0:T(8,128)(2,1)S(1)}, bf16[1024,512]{1,0:T(8,128)(2,1)}, u32[]{:S(2)}, u32[]{:S(2)}) collective-permute-start(bf16[1024,512]{1,0:T(8,128)(2,1)S(1)} %collective-permute-done.8), channel_id=1, source_target_pairs={{1,0},{2,1},{3,2},{4,5},{5,6},{6,7},{9,8},{10,9},{11,10},{12,13},{... | collective-permute-start | bytes 3145736 | tf_op jit(solution)/shard_map/ppermute | solution.py:144
  44.5 23.2 %collective-permute-start.19 = (bf16[1024,512]{1,0:T(8,128)(2,1)S(1)}, bf16[1024,512]{1,0:T(8,128)(2,1)}, u32[]{:S(2)}, u32[]{:S(2)}) collective-permute-start(bf16[1024,512]{1,0:T(8,128)(2,1)S(1)} %collective-permute-done.7), channel_id=1, source_target_pairs={{0,4},{4,0},{8,12},{12,8},{16,20},{20,16},{24,28},{28,24},{1,5},{5... | collective-permute-start | bytes 3145736 | tf_op jit(solution)/shard_map/ppermute | solution.py:134
  54.6 22.5 %collective-permute-start.2 = (bf16[1024,512]{1,0:T(8,128)(2,1)}, bf16[1024,512]{1,0:T(8,128)(2,1)}, u32[]{:S(2)}, u32[]{:S(2)}) collective-permute-start(bf16[1024,512]{1,0:T(8,128)(2,1)} %collective-permute-done.1), channel_id=1, source_target_pairs={{1,0},{2,1},{3,2},{4,5},{5,6},{6,7},{9,8},{10,9},{11,10},{12,13},{... | collective-permute-start | bytes 3145736 | tf_op jit(solution)/shard_map/ppermute | solution.py:144
  55.8 27.5 %collective-permute-start.11 = (bf16[1024,512]{1,0:T(8,128)(2,1)S(1)}, bf16[1024,512]{1,0:T(8,128)(2,1)}, u32[]{:S(2)}, u32[]{:S(2)}) collective-permute-start(bf16[1024,512]{1,0:T(8,128)(2,1)S(1)} %collective-permute-done.8), channel_id=1, source_target_pairs={{0,4},{4,0},{8,12},{12,8},{16,20},{20,16},{24,28},{28,24},{1,5},{5... | collective-permute-start | bytes 3145736 | tf_op jit(solution)/shard_map/ppermute | solution.py:134
  65.8 19.2 %collective-permute-start.10 = (bf16[1024,512]{1,0:T(8,128)(2,1)}, bf16[1024,512]{1,0:T(8,128)(2,1)}, u32[]{:S(2)}, u32[]{:S(2)}) collective-permute-start(bf16[1024,512]{1,0:T(8,128)(2,1)} %collective-permute-done.9), channel_id=1, source_target_pairs={{0,4},{4,0},{8,12},{12,8},{16,20},{20,16},{24,28},{28,24},{1,5},{5... | collective-permute-start | bytes 3145736 | tf_op jit(solution)/shard_map/ppermute | solution.py:134
  67.2 23.9 %collective-permute-start.16 = (bf16[1024,512]{1,0:T(8,128)(2,1)S(1)}, bf16[1024,512]{1,0:T(8,128)(2,1)}, u32[]{:S(2)}, u32[]{:S(2)}) collective-permute-start(bf16[1024,512]{1,0:T(8,128)(2,1)S(1)} %collective-permute-done), channel_id=1, source_target_pairs={{0,4},{4,0},{8,12},{12,8},{16,20},{20,16},{24,28},{28,24},{1,5},{5... | collective-permute-start | bytes 3145736 | tf_op jit(solution)/shard_map/ppermute | solution.py:134
  67.7 23.4 %collective-permute-start.4 = (bf16[1024,512]{1,0:T(8,128)(2,1)}, bf16[1024,512]{1,0:T(8,128)(2,1)}, u32[]{:S(2)}, u32[]{:S(2)}) collective-permute-start(bf16[1024,512]{1,0:T(8,128)(2,1)} %collective-permute-done.1), channel_id=1, source_target_pairs={{0,4},{4,0},{8,12},{12,8},{16,20},{20,16},{24,28},{28,24},{1,5},{5... | collective-permute-start | bytes 3145736 | tf_op jit(solution)/shard_map/ppermute | solution.py:134
  77.0 14.1 %collective-permute-start.3 = (bf16[1024,512]{1,0:T(8,128)(2,1)}, bf16[1024,512]{1,0:T(8,128)(2,1)}, u32[]{:S(2)}, u32[]{:S(2)}) collective-permute-start(bf16[1024,512]{1,0:T(8,128)(2,1)} %collective-permute-done.2), channel_id=1, source_target_pairs={{0,4},{4,0},{8,12},{12,8},{16,20},{20,16},{24,28},{28,24},{1,5},{5... | collective-permute-start | bytes 3145736 | tf_op jit(solution)/shard_map/ppermute | solution.py:134
  78.9 42.1 %all-to-all-start = ((f32[8,2,128]{2,1,0:T(2,128)}), f32[8,2,128]{2,1,0:T(2,128)S(1)}, u32[]{:S(2)}, u32[]{:S(2)}) async-start(f32[8,2,128]{2,1,0:T(2,128)} %maximum_bitcast_fusion), calls=%async_computation | async-start | bytes 16384 | tf_op jit(solution)/shard_map/all_to_all | solution.py:85
  83.4 69.7 %collective-permute-start.24 = (bf16[1024,512]{1,0:T(8,128)(2,1)}, bf16[1024,512]{1,0:T(8,128)(2,1)}, u32[]{:S(2)}, u32[]{:S(2)}) collective-permute-start(bf16[1024,512]{1,0:T(8,128)(2,1)} %get-tuple-element.13), channel_id=1, source_target_pairs={{0,1},{1,0},{2,3},{3,2},{4,5},{5,4},{6,7},{7,6},{8,9},{9,8},{10,11... | collective-permute-start | bytes 3145736 | tf_op jit(solution)/shard_map/ppermute | solution.py:146
  89.1 6.5 %copy-start.3 = (bf16[1024,512]{1,0:T(8,128)(2,1)}, bf16[1024,512]{1,0:T(8,128)(2,1)S(1)}, u32[]{:S(2)}) copy-start(bf16[1024,512]{1,0:T(8,128)(2,1)S(1)} %get-tuple-element.17.refs_1_) | copy-start | bytes 3145732
  89.1 14.9 %collective-permute-start.20 = (bf16[1024,512]{1,0:T(8,128)(2,1)S(1)}, bf16[1024,512]{1,0:T(8,128)(2,1)}, u32[]{:S(2)}, u32[]{:S(2)}) collective-permute-start(bf16[1024,512]{1,0:T(8,128)(2,1)S(1)} %get-tuple-element.17.refs_1_), channel_id=1, source_target_pairs={{0,8},{1,9},{2,10},{3,11},{4,20},{5,21},{6,22},{7,23},{8,0},{9,1},... | collective-permute-start | bytes 3145736 | tf_op jit(solution)/shard_map/ppermute | solution.py:183
  95.6 19.7 %collective-permute-start.17 = (bf16[1024,512]{1,0:T(8,128)(2,1)S(1)}, bf16[1024,512]{1,0:T(8,128)(2,1)}, u32[]{:S(2)}, u32[]{:S(2)}) collective-permute-start(bf16[1024,512]{1,0:T(8,128)(2,1)S(1)} %get-tuple-element.20.refs_0_), channel_id=1, source_target_pairs={{0,8},{1,9},{2,10},{3,11},{4,20},{5,21},{6,22},{7,23},{8,0},{9,1},... | collective-permute-start | bytes 3145736 | tf_op jit(solution)/shard_map/ppermute | solution.py:183
  95.9 1.0 copy-start.5
  97.7 28.8 %collective-permute-start.12 = (bf16[1024,512]{1,0:T(8,128)(2,1)S(1)}, bf16[1024,512]{1,0:T(8,128)(2,1)}, u32[]{:S(2)}, u32[]{:S(2)}) collective-permute-start(bf16[1024,512]{1,0:T(8,128)(2,1)S(1)} %get-tuple-element.18.refs_1_), channel_id=1, source_target_pairs={{0,8},{1,9},{2,10},{3,11},{4,20},{5,21},{6,22},{7,23},{8,0},{9,1},... | collective-permute-start | bytes 3145736 | tf_op jit(solution)/shard_map/ppermute | solution.py:183
  99.3 40.4 %copy-start.13 = (s32[1024]{0:T(1024)S(1)}, s32[1024]{0:T(1024)}, u32[]{:S(2)}) copy-start(s32[1024]{0:T(1024)} %param.8) | copy-start | bytes 12292
  99.3 38.4 %collective-permute-start.5 = (bf16[1024,512]{1,0:T(8,128)(2,1)}, bf16[1024,512]{1,0:T(8,128)(2,1)}, u32[]{:S(2)}, u32[]{:S(2)}) collective-permute-start(bf16[1024,512]{1,0:T(8,128)(2,1)} %get-tuple-element.21.refs_0_), channel_id=1, source_target_pairs={{0,8},{1,9},{2,10},{3,11},{4,20},{5,21},{6,22},{7,23},{8,0},{9,1},... | collective-permute-start | bytes 3145736 | tf_op jit(solution)/shard_map/ppermute | solution.py:183
  104.0 37.0 %collective-permute-start.21 = (bf16[1024,512]{1,0:T(8,128)(2,1)}, bf16[1024,512]{1,0:T(8,128)(2,1)}, u32[]{:S(2)}, u32[]{:S(2)}) collective-permute-start(bf16[1024,512]{1,0:T(8,128)(2,1)} %collective-permute-done.20.refs_1_), channel_id=1, source_target_pairs={{0,4},{4,0},{8,12},{12,8},{16,20},{20,16},{24,28},{28,24},{1,5},{5... | collective-permute-start | bytes 3145736 | tf_op jit(solution)/shard_map/ppermute | solution.py:134
  115.2 25.8 %collective-permute-start.18 = (bf16[1024,512]{1,0:T(8,128)(2,1)}, bf16[1024,512]{1,0:T(8,128)(2,1)}, u32[]{:S(2)}, u32[]{:S(2)}) collective-permute-start(bf16[1024,512]{1,0:T(8,128)(2,1)} %collective-permute-done.17.refs_0_), channel_id=1, source_target_pairs={{0,4},{4,0},{8,12},{12,8},{16,20},{20,16},{24,28},{28,24},{1,5},{5... | collective-permute-start | bytes 3145736 | tf_op jit(solution)/shard_map/ppermute | solution.py:134
  121.0 23.5 %copy-start.2 = (bf16[2048,512]{1,0:T(8,128)(2,1)S(1)}, bf16[2048,512]{1,0:T(8,128)(2,1)}, u32[]{:S(2)}) copy-start(bf16[2048,512]{1,0:T(8,128)(2,1)} %get-tuple-element.9.refs_0_) | copy-start | bytes 6291460
  126.5 32.9 %collective-permute-start.28 = (bf16[1024,512]{1,0:T(8,128)(2,1)}, bf16[1024,512]{1,0:T(8,128)(2,1)S(1)}, u32[]{:S(2)}, u32[]{:S(2)}) collective-permute-start(bf16[1024,512]{1,0:T(8,128)(2,1)} %get-tuple-element.16.refs_1_), channel_id=1, source_target_pairs={{0,8},{1,9},{2,10},{3,11},{4,20},{5,21},{6,22},{7,23},{8,0},{9,1},... | collective-permute-start | bytes 3145736 | tf_op jit(solution)/shard_map/ppermute | solution.py:183
  137.7 22.9 %collective-permute-start.26 = (bf16[1024,512]{1,0:T(8,128)(2,1)}, bf16[1024,512]{1,0:T(8,128)(2,1)S(1)}, u32[]{:S(2)}, u32[]{:S(2)}) collective-permute-start(bf16[1024,512]{1,0:T(8,128)(2,1)} %get-tuple-element.19.refs_0_), channel_id=1, source_target_pairs={{0,8},{1,9},{2,10},{3,11},{4,20},{5,21},{6,22},{7,23},{8,0},{9,1},... | collective-permute-start | bytes 3145736 | tf_op jit(solution)/shard_map/ppermute | solution.py:183
  141.0 25.9 %collective-permute-start.13 = (bf16[1024,512]{1,0:T(8,128)(2,1)}, bf16[1024,512]{1,0:T(8,128)(2,1)S(1)}, u32[]{:S(2)}, u32[]{:S(2)}) collective-permute-start(bf16[1024,512]{1,0:T(8,128)(2,1)} %collective-permute-done.12.refs_1_), channel_id=1, source_target_pairs={{0,4},{4,0},{8,12},{12,8},{16,20},{20,16},{24,28},{28,24},{1,5},{5... | collective-permute-start | bytes 3145736 | tf_op jit(solution)/shard_map/ppermute | solution.py:134
  141.1 26.2 %collective-permute-start.6 = (bf16[1024,512]{1,0:T(8,128)(2,1)}, bf16[1024,512]{1,0:T(8,128)(2,1)S(1)}, u32[]{:S(2)}, u32[]{:S(2)}) collective-permute-start(bf16[1024,512]{1,0:T(8,128)(2,1)} %collective-permute-done.5.refs_0_), channel_id=1, source_target_pairs={{0,4},{4,0},{8,12},{12,8},{16,20},{20,16},{24,28},{28,24},{1,5},{5... | collective-permute-start | bytes 3145736 | tf_op jit(solution)/shard_map/ppermute | solution.py:134
  150.6 2.5 copy-start.1
  153.1 28.3 %collective-permute-start.22 = (bf16[1024,512]{1,0:T(8,128)(2,1)}, bf16[1024,512]{1,0:T(8,128)(2,1)S(1)}, u32[]{:S(2)}, u32[]{:S(2)}) collective-permute-start(bf16[1024,512]{1,0:T(8,128)(2,1)} %broadcast_select_fusion.2), channel_id=1, source_target_pairs={{0,8},{1,9},{2,10},{3,11},{4,20},{5,21},{6,22},{7,23},{8,0},{9,1},... | collective-permute-start | bytes 3145736 | tf_op jit(solution)/shard_map/ppermute | solution.py:191
  153.1 7.6 %copy-start = (bf16[2048,512]{1,0:T(8,128)(2,1)S(1)}, bf16[2048,512]{1,0:T(8,128)(2,1)}, u32[]{:S(2)}) copy-start(bf16[2048,512]{1,0:T(8,128)(2,1)} %get-tuple-element.10.refs_0_) | copy-start | bytes 6291460
  159.3 28.2 %collective-permute-start.29 = (bf16[1024,512]{1,0:T(8,128)(2,1)S(1)}, bf16[1024,512]{1,0:T(8,128)(2,1)S(1)}, u32[]{:S(2)}, u32[]{:S(2)}) collective-permute-start(bf16[1024,512]{1,0:T(8,128)(2,1)S(1)} %collective-permute-done.28.refs_1_), channel_id=1, source_target_pairs={{0,4},{4,0},{8,12},{12,8},{16,20},{20,16},{24,28},{28,24},{1,5},{5... | collective-permute-start | bytes 3145736 | tf_op jit(solution)/shard_map/ppermute | solution.py:134
  160.6 27.0 %collective-permute-start.27 = (bf16[1024,512]{1,0:T(8,128)(2,1)S(1)}, bf16[1024,512]{1,0:T(8,128)(2,1)S(1)}, u32[]{:S(2)}, u32[]{:S(2)}) collective-permute-start(bf16[1024,512]{1,0:T(8,128)(2,1)S(1)} %collective-permute-done.26.refs_0_), channel_id=1, source_target_pairs={{0,4},{4,0},{8,12},{12,8},{16,20},{20,16},{24,28},{28,24},{1,5},{5... | collective-permute-start | bytes 3145736 | tf_op jit(solution)/shard_map/ppermute | solution.py:134
  166.8 26.9 %collective-permute-start.25 = (bf16[1024,512]{1,0:T(8,128)(2,1)}, bf16[1024,512]{1,0:T(8,128)(2,1)}, u32[]{:S(2)}, u32[]{:S(2)}) collective-permute-start(bf16[1024,512]{1,0:T(8,128)(2,1)} %collective-permute-done.24.refs_0_), channel_id=1, source_target_pairs={{0,4},{4,0},{8,12},{12,8},{16,20},{20,16},{24,28},{28,24},{1,5},{5... | collective-permute-start | bytes 3145736 | tf_op jit(solution)/shard_map/ppermute | solution.py:134
  167.4 39.4 %collective-permute-start.14 = (bf16[1024,512]{1,0:T(8,128)(2,1)S(1)}, bf16[1024,512]{1,0:T(8,128)(2,1)S(1)}, u32[]{:S(2)}, u32[]{:S(2)}) collective-permute-start(bf16[1024,512]{1,0:T(8,128)(2,1)S(1)} %broadcast_select_fusion.3), channel_id=1, source_target_pairs={{0,8},{1,9},{2,10},{3,11},{4,20},{5,21},{6,22},{7,23},{8,0},{9,1},... | collective-permute-start | bytes 3145736 | tf_op jit(solution)/shard_map/ppermute | solution.py:191
  169.0 6.3 %copy-start.7 = (bf16[1024,512]{1,0:T(8,128)(2,1)S(1)}, bf16[1024,512]{1,0:T(8,128)(2,1)}, u32[]{:S(2)}) copy-start(bf16[1024,512]{1,0:T(8,128)(2,1)} %get-tuple-element.16.refs_1_) | copy-start | bytes 3145732
  169.0 6.3 %copy-start.8 = (bf16[1024,512]{1,0:T(8,128)(2,1)S(1)}, bf16[1024,512]{1,0:T(8,128)(2,1)}, u32[]{:S(2)}) copy-start(bf16[1024,512]{1,0:T(8,128)(2,1)} %get-tuple-element.19.refs_0_) | copy-start | bytes 3145732
  181.4 39.6 %collective-permute-start.23 = (bf16[1024,512]{1,0:T(8,128)(2,1)S(1)}, bf16[1024,512]{1,0:T(8,128)(2,1)S(1)}, u32[]{:S(2)}, u32[]{:S(2)}) collective-permute-start(bf16[1024,512]{1,0:T(8,128)(2,1)S(1)} %collective-permute-done.22.refs_0_), channel_id=1, source_target_pairs={{0,4},{4,0},{8,12},{12,8},{16,20},{20,16},{24,28},{28,24},{1,5},{5... | collective-permute-start | bytes 3145736 | tf_op jit(solution)/shard_map/ppermute | solution.py:134
  193.7 6.9 %copy-start.4 = (bf16[1024,512]{1,0:T(8,128)(2,1)S(1)}, bf16[1024,512]{1,0:T(8,128)(2,1)}, u32[]{:S(2)}) copy-start(bf16[1024,512]{1,0:T(8,128)(2,1)} %copy-done.3) | copy-start | bytes 3145732
  193.7 6.9 %copy-start.6 = (bf16[1024,512]{1,0:T(8,128)(2,1)S(1)}, bf16[1024,512]{1,0:T(8,128)(2,1)}, u32[]{:S(2)}) copy-start(bf16[1024,512]{1,0:T(8,128)(2,1)} %copy-done.5) | copy-start | bytes 3145732
  206.8 39.9 %collective-permute-start.15 = (bf16[1024,512]{1,0:T(8,128)(2,1)S(1)}, bf16[1024,512]{1,0:T(8,128)(2,1)S(1)}, u32[]{:S(2)}, u32[]{:S(2)}) collective-permute-start(bf16[1024,512]{1,0:T(8,128)(2,1)S(1)} %collective-permute-done.14.refs_0_), channel_id=1, source_target_pairs={{0,4},{4,0},{8,12},{12,8},{16,20},{20,16},{24,28},{28,24},{1,5},{5... | collective-permute-start | bytes 3145736 | tf_op jit(solution)/shard_map/ppermute | solution.py:134

commit v2 on v0

v2 whole, which is shorter than its diff:
```python
import functools

import jax
import jax.numpy as jnp
from jax import lax
from jax.experimental import pallas as pl
from jax.experimental.pallas import tpu as pltpu
from jax.sharding import PartitionSpec as P

VMEM_BYTES = 64 * 1024 * 1024 - 256 * 1024
IN_SMEM = pl.BlockSpec(memory_space=pltpu.SMEM)
IN_HBM = pl.BlockSpec(memory_space=pl.ANY)
PARAMS = pltpu.CompilerParams(vmem_limit_bytes=VMEM_BYTES)
NO_COST = pl.CostEstimate(flops=1, bytes_accessed=1, transcendentals=0)


def after(arrays, earlier):
    count = len(arrays)

    def body(*refs):
        del refs

    return pl.pallas_call(
        body,
        in_specs=[IN_HBM] * (count + len(earlier)),
        out_specs=[IN_HBM] * count,
        out_shape=[jax.ShapeDtypeStruct(x.shape, x.dtype) for x in arrays],
        input_output_aliases={n: n for n in range(count)},
        cost_estimate=NO_COST,
        compiler_params=PARAMS,
    )(*arrays, *earlier)


def choose(index, choices, earlier, pieces=2):
    count = len(choices)
    height, width = choices[0].shape
    part = height // pieces

    def body(index_ref, *refs):
        out_ref, staged, got, put = refs[-4:]

        def fetch(n, p):
            rows = pl.ds(p * part, part)
            return pltpu.make_async_copy(refs[n].at[rows, :], staged.at[rows, :], got.at[p])

        def store(p):
            rows = pl.ds(p * part, part)
            return pltpu.make_async_copy(staged.at[rows, :], out_ref.at[rows, :], put.at[p])

        for n in range(count):

            @pl.when(index_ref[0] == n)
            def _():
                for p in range(pieces):
                    fetch(n, p).start()

        for p in range(pieces):
            fetch(0, p).wait()
            store(p).start()
        for p in range(pieces):
            store(p).wait()

    return pl.pallas_call(
        body,
        in_specs=[IN_SMEM] + [IN_HBM] * (count + len(earlier)),
        out_specs=IN_HBM,
        out_shape=jax.ShapeDtypeStruct((height, width), choices[0].dtype),
        scratch_shapes=[
            pltpu.VMEM((height, width), choices[0].dtype),
            pltpu.SemaphoreType.DMA((pieces,)),
            pltpu.SemaphoreType.DMA((pieces,)),
        ],
        cost_estimate=NO_COST,
        compiler_params=PARAMS,
    )(index, *choices, *earlier)


def cut(x, index, sizes, earlier):
    def body(index_ref, x_ref, *refs):
        out_ref, staged, sem = refs[-3:]
        rows = pl.ds(pl.multiple_of(index_ref[1], 16), sizes[0])
        columns = pl.ds(pl.multiple_of(index_ref[2], 128), sizes[1])
        fetch = pltpu.make_async_copy(x_ref.at[index_ref[0], rows, columns], staged, sem)
        fetch.start()
        fetch.wait()
        store = pltpu.make_async_copy(staged, out_ref, sem)
        store.start()
        store.wait()

    return pl.pallas_call(
        body,
        in_specs=[IN_SMEM] + [IN_HBM] * (1 + len(earlier)),
        out_specs=IN_HBM,
        out_shape=jax.ShapeDtypeStruct(sizes, x.dtype),
        scratch_shapes=[pltpu.VMEM(sizes, x.dtype), pltpu.SemaphoreType.DMA],
        cost_estimate=NO_COST,
        compiler_params=PARAMS,
    )(jnp.stack([jnp.asarray(n, jnp.int32) for n in index]), x, *earlier)


class Group:
    def __init__(self, blocks, before=None, column=None):
        self.blocks, self.before, self.column = blocks, before, column


def products_body(plan, scalars, *refs):
    layouts, finals, befores, sides, tile, stacked, in_count = plan
    hbm_rows = refs[: 2 * sides]
    place = 2 * sides
    array_count = sum(len(counts) for layout in layouts for counts in layout)
    if stacked:
        arrays = [refs[place].at[n] for n in range(array_count)]
        place += 1
    else:
        arrays = refs[place : place + array_count]
        place += array_count
    before_hbm = []
    for before in befores:
        before_hbm.append(refs[place : place + sides] if before else None)
        place += sides if before else 0
    outs = refs[in_count : in_count + sides * len(layouts)]
    scratch = refs[in_count + sides * len(layouts) :]
    t_refs, meta_refs = scratch[:sides], scratch[sides : 2 * sides]
    held = scratch[2 * sides : 2 * sides + array_count]
    staged, before_ref, t_sems, meta_sems, v_sems, before_sems, out_sems = scratch[2 * sides + array_count :]
    slots = t_refs[0].shape[0]
    width = staged.shape[2]
    tiles = slots // tile
    steps = [(side, i) for side in range(sides) for i in range(tiles)]

    def t_copy(step):
        side, i = steps[step]
        rows = pl.ds(i * tile, tile)
        return pltpu.make_async_copy(hbm_rows[side].at[rows, :], t_refs[side].at[rows, :], t_sems.at[step])

    def meta_copy(side):
        return pltpu.make_async_copy(hbm_rows[sides + side], meta_refs[side], meta_sems.at[side])

    def v_copy(n):
        return pltpu.make_async_copy(arrays[n], held[n], v_sems.at[n])

    def before_copy(g, side):
        rows = pl.ds(side * slots, slots)
        return pltpu.make_async_copy(before_hbm[g][side], before_ref.at[g, rows, :], before_sems.at[g * sides + side])

    def out_copy(g, step):
        side, i = steps[step]
        rows = pl.ds(i * tile, tile)
        target = outs[g * sides + side].at[rows, :]
        if side == 0 and finals[g]:
            columns = pl.ds(pl.multiple_of(scalars[g], 128), width)
            target = outs[g * sides].at[rows, columns]
        return pltpu.make_async_copy(
            staged.at[g, pl.ds(step * tile, tile), :], target, out_sems.at[g * len(steps) + step]
        )

    v_copy(0).start()
    meta_copy(0).start()
    for step in range(tiles):
        t_copy(step).start()
    for n in range(1, array_count):
        v_copy(n).start()
    for step in range(tiles, len(steps)):
        t_copy(step).start()
    if sides == 2:
        meta_copy(1).start()
    for g in range(len(layouts)):
        for side in range(sides if befores[g] else 0):
            before_copy(g, side).start()
    for step, (side, i) in enumerate(steps):
        if i == 0:
            meta_copy(side).wait()
            for later in range(tiles):
                t_copy(step + later).wait()
            if step == 0:
                for n in range(array_count):
                    v_copy(n).wait()
            for g in range(len(layouts)):
                if befores[g]:
                    before_copy(g, side).wait()
        rows = pl.ds(i * tile, tile)
        here = pl.ds(step * tile, tile)
        at, used = len(layouts), 0
        for g, layout in enumerate(layouts):
            total = None
            for counts in layout:
                channel = scalars[at].astype(jnp.float32)
                at += 1
                scale = jnp.where(meta_refs[side][rows, 0:1] == channel, meta_refs[side][rows, 1:2], 0.0)
                product = None
                for count in counts:
                    part = jnp.dot(
                        t_refs[side][rows, pl.ds(pl.multiple_of(scalars[at], 256), count)],
                        held[used][...],
                        preferred_element_type=jnp.float32,
                    )
                    product = part if product is None else product + part
                    at += 1
                    used += 1
                total = scale * product if total is None else total + scale * product
            if befores[g]:
                total = total + before_ref[g, here, :].astype(jnp.float32)
            staged[g, here, :] = total.astype(staged.dtype)
        if i == tiles - 1:
            for g in range(len(layouts)):
                for done in range(step - tiles + 1, step + 1):
                    out_copy(g, done).start()
    for g in range(len(layouts)):
        for step in range(len(steps)):
            out_copy(g, step).wait()


def products(t_rows, metas, groups, earlier, out=None, result=None):
    sides = len(t_rows)
    slots, depth = t_rows[0].shape
    dtype = t_rows[0].dtype
    tile = min(512, slots)
    stacked = not isinstance(groups[0].blocks[0][1], list)
    if stacked:
        arrays = [groups[0].blocks[0][1]]
        width = arrays[0].shape[2]
        held = [pltpu.VMEM(arrays[0].shape[1:], dtype)] * len(groups[0].blocks)
        layouts = (((depth,),) * len(groups[0].blocks),)
        firsts = [[(channel, [0]) for channel, _ in groups[0].blocks]]
    else:
        arrays = [x for group in groups for _, parts in group.blocks for _, x in parts]
        width = arrays[0].shape[1]
        held = [pltpu.VMEM(x.shape, dtype) for x in arrays]
        layouts = tuple(
            tuple(tuple(x.shape[0] for _, x in parts) for _, parts in group.blocks) for group in groups
        )
        firsts = [[(channel, [n for n, _ in parts]) for channel, parts in group.blocks] for group in groups]
    scalars = [0 if group.column is None else group.column for group in groups]
    for group in firsts:
        for channel, starts in group:
            scalars.extend([channel, *starts])
    scalars = jnp.stack([jnp.asarray(value, jnp.int32) for value in scalars])
    operands = [*t_rows, *metas, *arrays]
    for group in groups:
        operands.extend(group.before or ())
    aliases, totals = {}, []
    for n, group in enumerate(groups):
        totals.extend([jax.ShapeDtypeStruct((slots, width), dtype)] * sides)
        if group.column is not None:
            totals[n * sides] = jax.ShapeDtypeStruct(result, dtype)
            if out is not None:
                aliases[1 + len(operands)] = n * sides
                operands.append(out)
    operands.extend(earlier)
    steps = sides * (slots // tile)
    finals = tuple(group.column is not None for group in groups)
    befores = tuple(group.before is not None for group in groups)
    plan = (layouts, finals, befores, sides, tile, stacked, len(operands))
    height = sides * slots
    sums = pl.pallas_call(
        functools.partial(products_body, plan),
        in_specs=[IN_SMEM] + [IN_HBM] * len(operands),
        out_specs=[IN_HBM] * len(totals),
        out_shape=totals,
        input_output_aliases=aliases,
        scratch_shapes=[
            *[pltpu.VMEM((slots, depth), dtype)] * sides,
            *[pltpu.VMEM(metas[0].shape, metas[0].dtype)] * sides,
            *held,
            pltpu.VMEM((len(groups), height, width), dtype),
            pltpu.VMEM((len(groups), height if any(befores) else 16, width), dtype),
            pltpu.SemaphoreType.DMA((steps,)),
            pltpu.SemaphoreType.DMA((sides,)),
            pltpu.SemaphoreType.DMA((len(held),)),
            pltpu.SemaphoreType.DMA((sides * len(groups),)),
            pltpu.SemaphoreType.DMA((steps * len(groups),)),
        ],
        cost_estimate=NO_COST,
        compiler_params=PARAMS,
    )(scalars, *operands)
    return [sums[n * sides : (n + 1) * sides] for n in range(len(groups))]


def place(out, columns, arrays, earlier):
    count, pieces = len(arrays), 2
    slots, width = arrays[0].shape
    part = slots // pieces

    def body(columns_ref, *refs):
        out_ref, staged, got, put = refs[-4:]

        def fetch(n, p):
            rows = pl.ds(p * part, part)
            return pltpu.make_async_copy(refs[n].at[rows, :], staged.at[n, rows, :], got.at[n * pieces + p])

        def store(n, p):
            rows = pl.ds(p * part, part)
            columns = pl.ds(pl.multiple_of(columns_ref[n], 128), width)
            return pltpu.make_async_copy(staged.at[n, rows, :], out_ref.at[rows, columns], put.at[n * pieces + p])

        every = [(n, p) for n in range(count) for p in range(pieces)]
        for n, p in every:
            fetch(n, p).start()
        for n, p in every:
            fetch(n, p).wait()
            store(n, p).start()
        for n, p in every:
            store(n, p).wait()

    return pl.pallas_call(
        body,
        in_specs=[IN_SMEM] + [IN_HBM] * (count + 1 + len(earlier)),
        out_specs=IN_HBM,
        out_shape=jax.ShapeDtypeStruct(out.shape, out.dtype),
        input_output_aliases={1 + count: 0},
        scratch_shapes=[
            pltpu.VMEM((count, slots, width), out.dtype),
            pltpu.SemaphoreType.DMA((count * pieces,)),
            pltpu.SemaphoreType.DMA((count * pieces,)),
        ],
        cost_estimate=NO_COST,
        compiler_params=PARAMS,
    )(jnp.stack(columns).astype(jnp.int32), *arrays, out, *earlier)


def inverse_take(order, values):
    hit = order[None, :] == jnp.arange(order.shape[0], dtype=order.dtype)[:, None]
    return [jnp.sum(jnp.where(hit, value[None, :], 0.0), axis=1) for value in values]


def meta_to_owners(recv_order, ph_channel, recouple_weight, earlier=None):
    slots = recv_order.shape[0]
    group = lax.axis_size("chan")
    member = lax.axis_index("int") * slots
    ids = lax.dynamic_slice(ph_channel, (member,), (slots,)).astype(jnp.float32)
    scale = lax.dynamic_slice(recouple_weight, (member,), (slots,))
    back = jnp.stack(inverse_take(recv_order, [ids, scale]), axis=0)
    back = back.reshape(2, group, slots // group).transpose(1, 0, 2)
    if earlier is not None:
        (back,) = after([back], [earlier])
    return lax.all_to_all(back, "chan", split_axis=0, concat_axis=0, tiled=True)


def meta_of_rows(send_order, returned):
    back = returned.transpose(1, 0, 2).reshape(2, -1)
    ids, scale = inverse_take(send_order, [back[0], back[1]])
    lane = jnp.arange(128)[None, :]
    return jnp.where(lane == 0, ids[:, None], jnp.where(lane == 1, scale[:, None], 0.0))


def general_plan(t_pp, interaction, meta):
    slots, depth = t_pp.shape
    channels, _, width = interaction.shape
    group, members = lax.axis_size("chan"), lax.axis_size("int")
    flat = interaction.reshape(channels * depth, width)
    share = flat.shape[0] // group
    mine = lax.dynamic_slice(flat, (lax.axis_index("chan") * share, 0), (share, width))
    everyone = lax.all_gather(mine, ("chan", "int"), axis=0, tiled=False)
    everyone = everyone.reshape(group, members, share, width)
    out = None
    for member in range(members):
        whole = everyone[:, member].reshape(channels, depth, width)
        column, shape = jnp.int32(member * width), (slots, members * width)
        group_of = Group([(channel, whole) for channel in range(channels)], column=column)
        ((out,),) = products([t_pp], [meta], [group_of], [], out=out, result=shape)
    return out


def grid_plan(t_pp, interaction, meta_sent, meta_got):
    slots, depth = t_pp.shape
    channels, _, width = interaction.shape
    group, members = lax.axis_size("chan"), lax.axis_size("int")
    axes = ("chan", "int")
    c, z = lax.axis_index("chan"), lax.axis_index("int")
    core, chip = c % 2, c // 2
    half, part = depth // 2, width // 2
    shape = (slots, members * width)

    def at(chan, member):
        return chan * members + member

    def along(pairs):
        return [(at(a, m), at(a, n)) for a in range(group) for m, n in pairs]

    outer = along([(0, 1), (1, 0), (2, 3), (3, 2)])
    middle = along([(1, 2), (2, 1)])
    outwards = along([(1, 0), (2, 3)])
    sideways = [(a, a ^ 2) for a in range(group)]
    upwards = [(a, a ^ 4) for a in range(group)]
    other = [(a, a ^ 1) for a in range(group)]

    def step(x, pairs):
        return lax.ppermute(x, axes, pairs)

    def by_x(x):
        return lax.ppermute(x, "chan", sideways)

    def by_y(x):
        return lax.ppermute(x, "chan", upwards)

    def sib(x):
        return lax.ppermute(x, "chan", other)

    end = ((z == 0) | (z == members - 1)).astype(jnp.int32).reshape(1)
    low = z < members // 2
    column_of = [(z ^ 1) * width, jnp.where(low, 2, 1) * width, jnp.where(low, 3, 0) * width]
    mine, theirs = core * part, (1 - core) * part

    def quarter(channel, a, b):
        return (channel, [(0, a), (half, b)])

    def own_rows(channel, first, earlier):
        return cut(interaction, (channel, first, core * part), (half, part), earlier)

    own_a = lax.dynamic_slice(interaction, (chip, 0, core * part), (1, half, part)).reshape(half, part)
    p1a, p2a = step(own_a, outer), step(own_a, middle)
    own_b = own_rows(chip, half, [own_a])
    p1b, p2b = step(own_b, outer), step(own_b, middle)
    other_t = sib(t_pp)
    returned = meta_sent(own_b)

    p1a, p2a = after([p1a, p2a], [returned])
    x1a, y1a, p3a, p4a = by_x(p1a), by_y(p1a), step(p2a, outwards), step(p1a, middle)
    (meta,) = after([meta_got(returned)], [p1a])
    other_meta = sib(meta)
    extra_a = own_rows(chip ^ 3, 0, [meta])
    extra_b = own_rows(chip ^ 3, half, [extra_a])

    p1b, p2b = after([p1b, p2b], [extra_b])
    x1b, y1b, p3b, p4b = by_x(p1b), by_y(p1b), step(p2b, outwards), step(p1b, middle)
    own = Group([(channel, interaction) for channel in range(channels)], column=z * width)
    ((out,),) = products([t_pp], [meta], [own], [p1b], result=shape)

    x1a, y1a, p3a, p4a = after([x1a, y1a, p3a, p4a], [out])
    s2a = choose(end, [p2a, p3a], [x1a])
    x2a, y2a, p5a = by_x(s2a), by_y(s2a), step(p4a, outwards)

    x1b, y1b, p3b, p4b = after([x1b, y1b, p3b, p4b], [s2a])
    s2b = choose(end, [p2b, p3b], [x1b])
    x2b, y2b, p5b = by_x(s2b), by_y(s2b), step(p4b, outwards)
    x2a, y2a = after([x2a, y2a], [s2b])
    d2x = by_x(y2a)
    t_rows = [t_pp, other_t]
    metas = [meta, other_meta]
    blocks = [quarter(chip, p1a, p1b), quarter(chip ^ 1, x1a, x1b), quarter(chip ^ 2, y1a, y1b)]
    (sum1,) = products(t_rows, metas, [Group(blocks)], [x2a])

    p5a, x2b, y2b = after([p5a, x2b, y2b], [sum1[0]])
    d2y = by_y(x2b)
    s3a = choose(end, [p4a, p5a], [x2b])
    x3a, y3a = by_x(s3a), by_y(s3a)
    ea = step(extra_a, outer)

    (p5b,) = after([p5b], [s3a])
    s3b = choose(end, [p4b, p5b], [p5b])
    x3b, y3b = by_x(s3b), by_y(s3b)
    eb = step(extra_b, outer)
    d2x, d2y = after([d2x, d2y], [s3b])
    blocks = [
        quarter(chip, s2a, s2b),
        quarter(chip ^ 1, x2a, x2b),
        quarter(chip ^ 2, y2a, y2b),
        quarter(chip ^ 3, d2x, d2y),
    ]
    (out, rest2), sum3 = products(
        t_rows, metas, [Group(blocks, column=column_of[1] + mine), Group([quarter(chip, s3a, s3b)])],
        [d2x], out=out, result=shape,
    )

    x3a, y3a = after([x3a, y3a], [out])
    d3x = by_x(y3a)
    ea, x3b, y3b, eb = after([ea, x3b, y3b, eb], [x3a])
    d3y = by_y(x3b)
    back2 = sib(rest2)
    blocks = [quarter(chip ^ 1, x3a, x3b), quarter(chip ^ 2, y3a, y3b)]
    sum3, (out, rest1) = products(
        t_rows,
        metas,
        [Group(blocks, before=sum3), Group([quarter(chip ^ 3, ea, eb)], before=sum1, column=column_of[0] + mine)],
        [x3b],
        out=out,
        result=shape,
    )
    back1 = sib(rest1)

    d3x, d3y = after([d3x, d3y], [out])
    ((out, rest3),) = products(
        t_rows, metas, [Group([quarter(chip ^ 3, d3x, d3y)], before=sum3, column=column_of[2] + mine)],
        [d3x], out=out, result=shape,
    )
    back3 = sib(rest3)
    columns = [start + theirs for start in column_of]
    return place(out, columns, [back1, back2, back3], [])


def on_device(t_pp, interaction, send_order, recv_order, ph_channel, recouple_weight):
    sent = functools.partial(meta_to_owners, recv_order, ph_channel, recouple_weight)
    got = functools.partial(meta_of_rows, send_order)
    planes = lax.axis_size("chan") // 2
    if planes == 4 and lax.axis_size("int") == 4 and interaction.shape[0] == planes:
        return grid_plan(t_pp, interaction, sent, got)
    return general_plan(t_pp, interaction, got(sent()))


def solution(mesh):
    in_specs = (
        P(("chan", "int"), None),
        P(None, None, "int"),
        P(("chan", "int")),
        P(("chan", "int")),
        P("chan"),
        P("chan"),
    )
    out_specs = P(("chan", "int"), None)
    return jax.shard_map(
        on_device, mesh=mesh, in_specs=in_specs, out_specs=out_specs, check_vma=False
    )
```

time: 621 us -> 171 us (0.28)
  waiting for transfers between devices: 329 us -> 24.4 us
  blocking collectives: 157 us -> 0 us
  local copies, waits for them, and re-layouts: 59 us -> 5.82 us
  Pallas kernels: 36.9 us -> 82.3 us
  starting transfers between devices: 5.34 us -> 47.1 us
  between operations: 13.5 us -> 0.53 us
  other arithmetic: 20.2 us -> 7.94 us
    all_gather x1 -> x0, waiting for transfers between devices: 279 us -> none  [on_device(): everyone = lax.all_gather(ph_rows, 'int', axis=0, tiled=True)]
    all_to_all x2 -> x0, blocking collectives: 157 us -> none  [the longest x1 94.5 us: on_device(): lax.all_to_all(column_shares, 'int', split_axis=0, concat_axis=1, tiled=T...]
    pallas_call x0 -> x26, Pallas kernels: none -> 82.3 us  [the longest x5 64.7 us: products(): pl.pallas_call(functools.partial(products_body, plan), in_specs=[IN_SMEM]...]
    all_to_all x1, waiting for transfers between devices: 49.1 us -> 4.69 us  [meta_to_owners(): return lax.all_to_all(back, 'chan', split_axis=0, concat_axis=0, tiled=True)]
    ppermute x0 -> x33, starting transfers between devices: none -> 43.4 us  [the longest x12 21.8 us: step(): return lax.ppermute(x, axes, pairs)]
    another operation x4 -> x0, Pallas kernels: 31.5 us -> none
    gather x2 -> x0, local copies, waits for them, and re-layouts: 23.1 us -> none  [the longest x1 11.5 us: on_device(): ph_rows = jnp.take(arrived, recv_order, axis=0)]
    scatter x2 -> x0, local copies, waits for them, and re-layouts: 20.2 us -> none  [the longest x1 10.1 us: on_device(): return jnp.zeros_like(returned).at[send_order].set(returned)]
  transfers between devices with their start and end apart: 2 -> 34, of which waited for: 2 -> 7; matrix products, arithmetic and copies ran while one was open for 0% -> 8% of each run, Pallas kernels for 1% -> 47%
where the time goes in v2:
time: 171 us; the launch traced here: 168 us
  Pallas kernels  82.3 us (48%)
  starting transfers between devices  47.1 us (28%)
  waiting for transfers between devices  24.4 us (14%)
  other arithmetic  7.94 us (5%)
  local copies, waits for them, and re-layouts  5.82 us (3%)
    pallas_call x5, Pallas kernels, products(): pl.pallas_call(functools.partial(products_body, plan), in_specs=[IN_SMEM]...  64.7 us
    ppermute x12, starting transfers between devices, step(): return lax.ppermute(x, axes, pairs)  21.8 us
    ppermute x8, waiting for transfers between devices, by_x(): return lax.ppermute(x, 'chan', sideways)  12 us
    ppermute x8, starting transfers between devices, by_x(): return lax.ppermute(x, 'chan', sideways)  11.2 us
    ppermute x8, starting transfers between devices, by_y(): return lax.ppermute(x, 'chan', upwards)  9.34 us
    pallas_call x3, Pallas kernels, cut(): pl.pallas_call(body, in_specs=[IN_SMEM] + [IN_HBM] * (1 + len(earlier)),...  7.55 us
    pallas_call x4, Pallas kernels, choose(): pl.pallas_call(body, in_specs=[IN_SMEM] + [IN_HBM] * (count + len(earlier...  7.19 us
    ppermute x12, waiting for transfers between devices, step(): return lax.ppermute(x, axes, pairs)  6.09 us
  transfers between devices with their start and end apart: 34, of which 7 were waited for; matrix products, arithmetic and copies ran while one was open for 8% of the time, Pallas kernels for 47%

profile of v2, /device:TPU:0, one launch (start us, length us, event | category | flops | bytes accessed | tf_op | source)
XLA Modules:
  0.0 168.2 jit_solution(15069770563033160658)
XLA Ops:
  0.5 1.9 %dynamic-slice_bitcast_fusion.refs_0_ = bf16[1024,256]{1,0:T(8,128)(2,1)} fusion(bf16[4,2048,512]{2,1,0:T(8,128)(2,1)} %refs_2_.1, s32[]{:T(128)S(6)} %select_n.56, s32[]{:T(128)S(6)} %select_n.57), kind=kLoop, calls=%fused_computation.7 | loop fusion | bytes 1048584 | tf_op jit(solution)/shard_map/reshape | solution.py:410
  2.3 2.6 %collective-permute-start.1 = (bf16[1024,256]{1,0:T(8,128)(2,1)}, bf16[1024,256]{1,0:T(8,128)(2,1)}, u32[]{:S(2)}, u32[]{:S(2)}) collective-permute-start(bf16[1024,256]{1,0:T(8,128)(2,1)} %dynamic-slice_bitcast_fusion.refs_0_), channel_id=1, source_target_pairs={{0,1},{1,0},{2,3},{3,2},{4,5},{5,4},{6,7},{7,6},{8,9},{9,8},{10,11... | collective-permute-start | bytes 1572872 | tf_op jit(solution)/shard_map/ppermute | solution.py:388
  4.9 0.6 fusion.index_ref
  5.5 1.6 collective-permute-start.2
  7.1 2.5 %shard_map.64.refs_1_ = bf16[1024,256]{1,0:T(8,128)(2,1)} custom-call(s32[3]{0:T(128)} %fusion.index_ref, bf16[4,2048,512]{2,1,0:T(8,128)(2,1)} %refs_2_.1, bf16[1024,256]{1,0:T(8,128)(2,1)} %dynamic-slice_bitcast_fusion.refs_0_), custom_call_target="tpu_custom_call" | custom-call | flops 1 | bytes 1 | tf_op jit(solution)/shard_map/pallas_call | solution.py:90
  9.7 3.6 %collective-permute-start.8 = (bf16[1024,256]{1,0:T(8,128)(2,1)}, bf16[1024,256]{1,0:T(8,128)(2,1)}, u32[]{:S(2)}, u32[]{:S(2)}) collective-permute-start(bf16[1024,256]{1,0:T(8,128)(2,1)} %shard_map.64.refs_1_), channel_id=1, source_target_pairs={{0,1},{1,0},{2,3},{3,2},{4,5},{5,4},{6,7},{7,6},{8,9},{9,8},{10,11... | collective-permute-start | bytes 1572872 | tf_op jit(solution)/shard_map/ppermute | solution.py:388
  13.3 0.7 dynamic_slice.10
  14.0 0.7 dynamic-slice_convert_fusion
  14.7 1.2 select_reduce_fusion.3
  15.9 0.6 maximum_bitcast_fusion.refs_0_
  16.5 1.5 collective-permute-start.9
  18.0 3.7 %all-to-all-start = ((f32[8,2,128]{2,1,0:T(2,128)}), f32[8,2,128]{2,1,0:T(2,128)S(1)}, u32[]{:S(2)}, u32[]{:S(2)}) async-start(f32[8,2,128]{2,1,0:T(2,128)} %shard_map.65), calls=%async_computation | async-start | bytes 16384 | tf_op jit(solution)/shard_map/all_to_all | solution.py:336
  21.7 4.7 %all-to-all-done.refs_2_ = f32[8,2,128]{2,1,0:T(2,128)S(1)} async-done(((f32[8,2,128]{2,1,0:T(2,128)}), f32[8,2,128]{2,1,0:T(2,128)S(1)}, u32[]{:S(2)}, u32[]{:S(2)}) %all-to-all-start) | async-done | bytes 8224 | tf_op jit(solution)/shard_map/all_to_all | solution.py:336
  26.4 0.6 copy-done
  27.5 0.6 collective-permute-start.5
  28.1 1.2 select_reduce_fusion.1
  29.4 1.1 select_select_fusion.refs_0_
  30.5 0.6 add_add_fusion.index_ref
  31.1 1.5 collective-permute-start.7
  32.6 1.3 collective-permute-start.6
  33.9 0.6 fusion.1.index_ref
  34.5 2.5 %shard_map.68.refs_0_ = bf16[1024,256]{1,0:T(8,128)(2,1)} custom-call(s32[3]{0:T(128)} %add_add_fusion.index_ref, bf16[4,2048,512]{2,1,0:T(8,128)(2,1)} %refs_2_.1, f32[1024,128]{1,0:T(8,128)} %shard_map.67.refs_0_.refs_1_.refs_2_), custom_call_target="tpu_custom_call" | custom-call | flops 1 | bytes 1 | tf_op jit(solution)/shard_map/pallas_call | solution.py:90
  37.0 2.5 %shard_map.69.refs_2_ = bf16[1024,256]{1,0:T(8,128)(2,1)} custom-call(s32[3]{0:T(128)} %fusion.1.index_ref, bf16[4,2048,512]{2,1,0:T(8,128)(2,1)} %refs_2_.1, bf16[1024,256]{1,0:T(8,128)(2,1)} %shard_map.68.refs_0_), custom_call_target="tpu_custom_call" | custom-call | flops 1 | bytes 1 | tf_op jit(solution)/shard_map/pallas_call | solution.py:90
  39.5 1.4 collective-permute-done.4.refs_0_
  40.9 0.8 collective-permute-start.11
  41.8 0.8 collective-permute-start.12
  42.5 0.6 stack.101.scalars
  43.2 5.4 %collective-permute-done.6.refs_2_ = bf16[1024,256]{1,0:T(8,128)(2,1)} collective-permute-done((bf16[1024,256]{1,0:T(8,128)(2,1)}, bf16[1024,256]{1,0:T(8,128)(2,1)}, u32[]{:S(2)}, u32[]{:S(2)}) %collective-permute-start.6) | collective-permute-done | bytes 524320 | tf_op jit(solution)/shard_map/ppermute | solution.py:388
  48.6 1.3 collective-permute-start.13
  49.9 15.3 %shard_map.71.refs_4_.refs_14_ = bf16[1024,2048]{1,0:T(8,128)(2,1)} custom-call(s32[9]{0:T(128)} %stack.101.scalars, bf16[1024,2048]{1,0:T(8,128)(2,1)} %refs_0_.9, f32[1024,128]{1,0:T(8,128)} %shard_map.67.refs_0_.refs_1_.refs_2_, bf16[4,2048,512]{2,1,0:T(8,128)(2,1)} %refs_2_.1, bf16[1024,256]{1,0:T(8,128)(2,1)} %get-tuple-element.46.refs_3_.refs_5_), custom_call_target="tpu_custom_call" | custom-call | flops 1 | bytes 1 | tf_op jit(solution)/shard_map/pallas_call | solution.py:255
  65.2 1.5 collective-permute-start.14
  66.7 1.8 %shard_map.73.refs_4_ = bf16[1024,256]{1,0:T(8,128)(2,1)} custom-call(s32[1]{0:T(128)} %bitcast.16.index_ref, bf16[1024,256]{1,0:T(8,128)(2,1)} %get-tuple-element.45.refs_0_, bf16[1024,256]{1,0:T(8,128)(2,1)} %get-tuple-element.49.refs_1_, bf16[1024,256]{1,0:T(8,128)(2,1)} %get-tuple-element.50.refs_2_.refs_6_), custom_call_target="tpu_custom_call" | custom-call | flops 1 | bytes 1 | tf_op jit(solution)/shard_map/pallas_call | solution.py:63
  68.5 1.5 collective-permute-start.17
  70.1 1.1 collective-permute-start.18
  71.2 1.8 %shard_map.75.refs_2_.refs_5_ = bf16[1024,256]{1,0:T(8,128)(2,1)} custom-call(s32[1]{0:T(128)} %bitcast.16.index_ref, bf16[1024,256]{1,0:T(8,128)(2,1)} %get-tuple-element.48.refs_0_, bf16[1024,256]{1,0:T(8,128)(2,1)} %get-tuple-element.51.refs_1_, bf16[1024,256]{1,0:T(8,128)(2,1)} %get-tuple-element.52.refs_2_.refs_7_), custom_call_target="tpu_custom_call" | custom-call | flops 1 | bytes 1 | tf_op jit(solution)/shard_map/pallas_call | solution.py:63
  73.0 0.9 collective-permute-start.15
  73.9 9.9 %collective-permute-done.17.refs_0_ = bf16[1024,256]{1,0:T(8,128)(2,1)} collective-permute-done((bf16[1024,256]{1,0:T(8,128)(2,1)}, bf16[1024,256]{1,0:T(8,128)(2,1)}, u32[]{:S(2)}, u32[]{:S(2)}) %collective-permute-start.17) | collective-permute-done | bytes 524320 | tf_op jit(solution)/shard_map/ppermute | solution.py:391
  83.8 1.3 collective-permute-start.16
  85.1 1.3 collective-permute-start.10
  86.4 0.7 stack.104.scalars
  87.1 1.5 collective-permute-start.23
  88.6 1.3 collective-permute-start.21
  89.8 12.3 %shard_map.77 = (bf16[1024,256]{1,0:T(8,128)(2,1)}, bf16[1024,256]{1,0:T(8,128)(2,1)}) custom-call(s32[10]{0:T(128)} %stack.104.scalars, bf16[1024,2048]{1,0:T(8,128)(2,1)} %refs_0_.9, bf16[1024,2048]{1,0:T(8,128)(2,1)} %collective-permute-done.refs_1_, f32[1024,128]{1,0:T(8,128)} %shard_map.67.refs_0_.refs_1_.refs_2_, ...), custom_call_target="tpu_custom_call" | custom-call | flops 1 | bytes 1 | tf_op jit(solution)/shard_map/pallas_call | solution.py:255
  102.2 1.6 collective-permute-start.22
  103.7 1.8 %shard_map.79.refs_1_.refs_12_ = bf16[1024,256]{1,0:T(8,128)(2,1)} custom-call(s32[1]{0:T(128)} %bitcast.16.index_ref, bf16[1024,256]{1,0:T(8,128)(2,1)} %get-tuple-element.47.refs_0_, bf16[1024,256]{1,0:T(8,128)(2,1)} %get-tuple-element.57.refs_1_, bf16[1024,256]{1,0:T(8,128)(2,1)} %get-tuple-element.58.refs_2_.refs_7_), custom_call_target="tpu_custom_call" | custom-call | flops 1 | bytes 1 | tf_op jit(solution)/shard_map/pallas_call | solution.py:63
  105.5 0.8 collective-permute-start.19
  106.3 4.1 %collective-permute-start.27 = (bf16[1024,256]{1,0:T(8,128)(2,1)}, bf16[1024,256]{1,0:T(8,128)(2,1)}, u32[]{:S(2)}, u32[]{:S(2)}) collective-permute-start(bf16[1024,256]{1,0:T(8,128)(2,1)} %shard_map.69.refs_2_), channel_id=1, source_target_pairs={{0,1},{1,0},{2,3},{3,2},{4,5},{5,4},{6,7},{7,6},{8,9},{9,8},{10,11... | collective-permute-start | bytes 1572872 | tf_op jit(solution)/shard_map/ppermute | solution.py:388
  110.5 0.6 collective-permute-done.23.refs_0_
  111.1 1.9 %collective-permute-start.20 = (bf16[1024,256]{1,0:T(8,128)(2,1)}, bf16[1024,256]{1,0:T(8,128)(2,1)}, u32[]{:S(2)}, u32[]{:S(2)}) collective-permute-start(bf16[1024,256]{1,0:T(8,128)(2,1)} %shard_map.79.refs_1_.refs_12_), channel_id=1, source_target_pairs={{0,16},{4,20},{8,24},{12,28},{16,0},{20,4},{24,8},{28,12},{1,17},{... | collective-permute-start | bytes 1572872 | tf_op jit(solution)/shard_map/ppermute | solution.py:394
  113.0 1.8 %shard_map.81.refs_2_.refs_13_ = bf16[1024,256]{1,0:T(8,128)(2,1)} custom-call(s32[1]{0:T(128)} %bitcast.16.index_ref, bf16[1024,256]{1,0:T(8,128)(2,1)} %get-tuple-element.61.refs_0_, bf16[1024,256]{1,0:T(8,128)(2,1)} %shard_map.80.refs_1_.refs_2_, bf16[1024,256]{1,0:T(8,128)(2,1)} %shard_map.80.refs_1_.refs_2_), custom_call_target="tpu_custom_call" | custom-call | flops 1 | bytes 1 | tf_op jit(solution)/shard_map/pallas_call | solution.py:63
  114.9 3.8 %collective-permute-start.25 = (bf16[1024,256]{1,0:T(8,128)(2,1)}, bf16[1024,256]{1,0:T(8,128)(2,1)}, u32[]{:S(2)}, u32[]{:S(2)}) collective-permute-start(bf16[1024,256]{1,0:T(8,128)(2,1)} %shard_map.81.refs_2_.refs_13_), channel_id=1, source_target_pairs={{0,8},{4,12},{8,0},{12,4},{16,24},{20,28},{24,16},{28,20},{1,9},{5... | collective-permute-start | bytes 1572872 | tf_op jit(solution)/shard_map/ppermute | solution.py:391
  118.8 0.7 collective-permute-done.19.refs_0_
  119.5 1.0 collective-permute-start.26
  120.5 0.7 stack.106.scalars
  121.1 17.2 %shard_map.83 = (bf16[1024,2048]{1,0:T(8,128)(2,1)}, bf16[1024,256]{1,0:T(8,128)(2,1)}, bf16[1024,256]{1,0:T(8,128)(2,1)}, bf16[1024,256]{1,0:T(8,128)(2,1)}) custom-call(s32[17]{0:T(128)} %stack.106.scalars, bf16[1024,2048]{1,0:T(8,128)(2,1)} %refs_0_.9, bf16[1024,2048]{1,0:T(8,128)(2,1)} %collective-permute-done.refs_1_, ...), custom_call_target="tpu_custom_call", output_to_operand_aliasing={{0}: (15, {})} | custom-call | flops 1 | bytes 1 | tf_op jit(solution)/shard_map/pallas_call | solution.py:255
  138.5 1.1 collective-permute-start.31
  139.5 1.5 collective-permute-start.30
  141.0 0.7 stack.93.scalars
  141.7 0.6 pad_add_fusion.3.scalars
  142.3 12.4 %shard_map.86 = (bf16[1024,256]{1,0:T(8,128)(2,1)}, bf16[1024,256]{1,0:T(8,128)(2,1)}, bf16[1024,2048]{1,0:T(8,128)(2,1)}, bf16[1024,256]{1,0:T(8,128)(2,1)}) custom-call(s32[11]{0:T(128)} %stack.93.scalars, bf16[1024,2048]{1,0:T(8,128)(2,1)} %refs_0_.9, bf16[1024,2048]{1,0:T(8,128)(2,1)} %collective-permute-done.refs_1_, ...), custom_call_target="tpu_custom_call", output_to_operand_aliasing={{2}: (15, {})} | custom-call | flops 1 | bytes 1 | tf_op jit(solution)/shard_map/pallas_call | solution.py:255
  155.3 7.5 %shard_map.88 = (bf16[1024,2048]{1,0:T(8,128)(2,1)}, bf16[1024,256]{1,0:T(8,128)(2,1)}) custom-call(s32[4]{0:T(128)} %pad_add_fusion.3.scalars, bf16[1024,2048]{1,0:T(8,128)(2,1)} %refs_0_.9, bf16[1024,2048]{1,0:T(8,128)(2,1)} %collective-permute-done.refs_1_, f32[1024,128]{1,0:T(8,128)} %shard_map.67.refs_0_.refs_1_.refs_2_, ...), custom_call_target="tpu_custom_call", output_to_operand_aliasing={{0}: (9, {})} | custom-call | flops 1 | bytes 1 | tf_op jit(solution)/shard_map/pallas_call | solution.py:255
  163.0 0.6 pad_add_fusion.2.columns_ref
  163.6 1.6 collective-permute-done.32.refs_2_
  165.1 2.8 %shard_map.89 = bf16[1024,2048]{1,0:T(8,128)(2,1)} custom-call(s32[3]{0:T(128)} %pad_add_fusion.2.columns_ref, bf16[1024,256]{1,0:T(8,128)(2,1)} %collective-permute-done.28.refs_0_, bf16[1024,256]{1,0:T(8,128)(2,1)} %collective-permute-done.29.refs_1_, bf16[1024,256]{1,0:T(8,128)(2,1)} %collective-permute-done.32.refs_2_, ...), custom_call_target="tpu_custom_call", output_to_operand_aliasing={{}: (4, {})} | custom-call | flops 1 | bytes 1 | tf_op jit(solution)/shard_map/pallas_call | solution.py:305
  (55 shorter events, 1.9 us)
Async XLA Ops:
  0.0 88.6 %collective-permute-start = (bf16[1024,2048]{1,0:T(8,128)(2,1)}, bf16[1024,2048]{1,0:T(8,128)(2,1)}, u32[]{:S(2)}, u32[]{:S(2)}) collective-permute-start(bf16[1024,2048]{1,0:T(8,128)(2,1)} %refs_0_.9), channel_id=1, source_target_pairs={{0,4},{4,0},{8,12},{12,8},{16,20},{20,16},{24,28},{28,24},{1,5},{5... | collective-permute-start | bytes 12582920 | tf_op jit(solution)/shard_map/ppermute | solution.py:397
  2.3 24.1 %collective-permute-start.1 = (bf16[1024,256]{1,0:T(8,128)(2,1)}, bf16[1024,256]{1,0:T(8,128)(2,1)}, u32[]{:S(2)}, u32[]{:S(2)}) collective-permute-start(bf16[1024,256]{1,0:T(8,128)(2,1)} %dynamic-slice_bitcast_fusion.refs_0_), channel_id=1, source_target_pairs={{0,1},{1,0},{2,3},{3,2},{4,5},{5,4},{6,7},{7,6},{8,9},{9,8},{10,11... | collective-permute-start | bytes 1572872 | tf_op jit(solution)/shard_map/ppermute | solution.py:388
  5.5 9.2 %copy-start.1 = (s32[1024]{0:T(1024)S(1)}, s32[1024]{0:T(1024)}, u32[]{:S(2)}) copy-start(s32[1024]{0:T(1024)} %param.9) | copy-start | bytes 12292
  5.5 22.6 %copy-start.2 = (s32[1024]{0:T(1024)S(1)}, s32[1024]{0:T(1024)}, u32[]{:S(2)}) copy-start(s32[1024]{0:T(1024)} %param.8) | copy-start | bytes 12292
  5.5 20.9 %collective-permute-start.2 = (bf16[1024,256]{1,0:T(8,128)(2,1)}, bf16[1024,256]{1,0:T(8,128)(2,1)}, u32[]{:S(2)}, u32[]{:S(2)}) collective-permute-start(bf16[1024,256]{1,0:T(8,128)(2,1)} %dynamic-slice_bitcast_fusion.refs_0_), channel_id=1, source_target_pairs={{1,2},{2,1},{5,6},{6,5},{9,10},{10,9},{13,14},{14,13},{17,18},{18,... | collective-permute-start | bytes 1572872 | tf_op jit(solution)/shard_map/ppermute | solution.py:388
  9.7 21.5 %collective-permute-start.8 = (bf16[1024,256]{1,0:T(8,128)(2,1)}, bf16[1024,256]{1,0:T(8,128)(2,1)}, u32[]{:S(2)}, u32[]{:S(2)}) collective-permute-start(bf16[1024,256]{1,0:T(8,128)(2,1)} %shard_map.64.refs_1_), channel_id=1, source_target_pairs={{0,1},{1,0},{2,3},{3,2},{4,5},{5,4},{6,7},{7,6},{8,9},{9,8},{10,11... | collective-permute-start | bytes 1572872 | tf_op jit(solution)/shard_map/ppermute | solution.py:388
  16.5 16.1 %collective-permute-start.9 = (bf16[1024,256]{1,0:T(8,128)(2,1)}, bf16[1024,256]{1,0:T(8,128)(2,1)}, u32[]{:S(2)}, u32[]{:S(2)}) collective-permute-start(bf16[1024,256]{1,0:T(8,128)(2,1)} %shard_map.64.refs_1_), channel_id=1, source_target_pairs={{1,2},{2,1},{5,6},{6,5},{9,10},{10,9},{13,14},{14,13},{17,18},{18,... | collective-permute-start | bytes 1572872 | tf_op jit(solution)/shard_map/ppermute | solution.py:388
  18.0 8.4 %all-to-all-start = ((f32[8,2,128]{2,1,0:T(2,128)}), f32[8,2,128]{2,1,0:T(2,128)S(1)}, u32[]{:S(2)}, u32[]{:S(2)}) async-start(f32[8,2,128]{2,1,0:T(2,128)} %shard_map.65), calls=%async_computation | async-start | bytes 16384 | tf_op jit(solution)/shard_map/all_to_all | solution.py:336
  26.4 0.6 copy-start
  27.0 13.9 %collective-permute-start.4 = (bf16[1024,256]{1,0:T(8,128)(2,1)}, bf16[1024,256]{1,0:T(8,128)(2,1)}, u32[]{:S(2)}, u32[]{:S(2)}) collective-permute-start(bf16[1024,256]{1,0:T(8,128)(2,1)} %get-tuple-element.44.refs_1_.refs_4_), channel_id=1, source_target_pairs={{0,8},{4,12},{8,0},{12,4},{16,24},{20,28},{24,16},{28,20},{1,9},{5... | collective-permute-start | bytes 1572872 | tf_op jit(solution)/shard_map/ppermute | solution.py:391
  27.5 14.2 %collective-permute-start.5 = (bf16[1024,256]{1,0:T(8,128)(2,1)}, bf16[1024,256]{1,0:T(8,128)(2,1)}, u32[]{:S(2)}, u32[]{:S(2)}) collective-permute-start(bf16[1024,256]{1,0:T(8,128)(2,1)} %get-tuple-element.44.refs_1_.refs_4_), channel_id=1, source_target_pairs={{0,16},{4,20},{8,24},{12,28},{16,0},{20,4},{24,8},{28,12},{1,17},{... | collective-permute-start | bytes 1572872 | tf_op jit(solution)/shard_map/ppermute | solution.py:394
  31.1 34.1 %collective-permute-start.7 = (bf16[1024,256]{1,0:T(8,128)(2,1)}, bf16[1024,256]{1,0:T(8,128)(2,1)}, u32[]{:S(2)}, u32[]{:S(2)}) collective-permute-start(bf16[1024,256]{1,0:T(8,128)(2,1)} %get-tuple-element.44.refs_1_.refs_4_), channel_id=1, source_target_pairs={{1,2},{2,1},{5,6},{6,5},{9,10},{10,9},{13,14},{14,13},{17,18},{18,... | collective-permute-start | bytes 1572872 | tf_op jit(solution)/shard_map/ppermute | solution.py:388
  32.6 16.0 %collective-permute-start.6 = (bf16[1024,256]{1,0:T(8,128)(2,1)}, bf16[1024,256]{1,0:T(8,128)(2,1)}, u32[]{:S(2)}, u32[]{:S(2)}) collective-permute-start(bf16[1024,256]{1,0:T(8,128)(2,1)} %get-tuple-element.45.refs_0_), channel_id=1, source_target_pairs={{1,0},{2,3},{5,4},{6,7},{9,8},{10,11},{13,12},{14,15},{17,16},{18,... | collective-permute-start | bytes 1572872 | tf_op jit(solution)/shard_map/ppermute | solution.py:388
  40.9 27.6 %collective-permute-start.11 = (bf16[1024,256]{1,0:T(8,128)(2,1)}, bf16[1024,256]{1,0:T(8,128)(2,1)}, u32[]{:S(2)}, u32[]{:S(2)}) collective-permute-start(bf16[1024,256]{1,0:T(8,128)(2,1)} %get-tuple-element.46.refs_3_.refs_5_), channel_id=1, source_target_pairs={{0,8},{4,12},{8,0},{12,4},{16,24},{20,28},{24,16},{28,20},{1,9},{5... | collective-permute-start | bytes 1572872 | tf_op jit(solution)/shard_map/ppermute | solution.py:391
  41.8 28.3 %collective-permute-start.12 = (bf16[1024,256]{1,0:T(8,128)(2,1)}, bf16[1024,256]{1,0:T(8,128)(2,1)}, u32[]{:S(2)}, u32[]{:S(2)}) collective-permute-start(bf16[1024,256]{1,0:T(8,128)(2,1)} %get-tuple-element.46.refs_3_.refs_5_), channel_id=1, source_target_pairs={{0,16},{4,20},{8,24},{12,28},{16,0},{20,4},{24,8},{28,12},{1,17},{... | collective-permute-start | bytes 1572872 | tf_op jit(solution)/shard_map/ppermute | solution.py:394
  48.6 22.6 %collective-permute-start.13 = (bf16[1024,256]{1,0:T(8,128)(2,1)}, bf16[1024,256]{1,0:T(8,128)(2,1)}, u32[]{:S(2)}, u32[]{:S(2)}) collective-permute-start(bf16[1024,256]{1,0:T(8,128)(2,1)} %get-tuple-element.48.refs_0_), channel_id=1, source_target_pairs={{1,0},{2,3},{5,4},{6,7},{9,8},{10,11},{13,12},{14,15},{17,16},{18,... | collective-permute-start | bytes 1572872 | tf_op jit(solution)/shard_map/ppermute | solution.py:388
  65.2 5.9 %collective-permute-start.14 = (bf16[1024,256]{1,0:T(8,128)(2,1)}, bf16[1024,256]{1,0:T(8,128)(2,1)}, u32[]{:S(2)}, u32[]{:S(2)}) collective-permute-start(bf16[1024,256]{1,0:T(8,128)(2,1)} %get-tuple-element.46.refs_3_.refs_5_), channel_id=1, source_target_pairs={{1,2},{2,1},{5,6},{6,5},{9,10},{10,9},{13,14},{14,13},{17,18},{18,... | collective-permute-start | bytes 1572872 | tf_op jit(solution)/shard_map/ppermute | solution.py:388
  68.5 15.2 %collective-permute-start.17 = (bf16[1024,256]{1,0:T(8,128)(2,1)}, bf16[1024,256]{1,0:T(8,128)(2,1)}, u32[]{:S(2)}, u32[]{:S(2)}) collective-permute-start(bf16[1024,256]{1,0:T(8,128)(2,1)} %shard_map.73.refs_4_), channel_id=1, source_target_pairs={{0,8},{4,12},{8,0},{12,4},{16,24},{20,28},{24,16},{28,20},{1,9},{5... | collective-permute-start | bytes 1572872 | tf_op jit(solution)/shard_map/ppermute | solution.py:391
  70.1 15.0 %collective-permute-start.18 = (bf16[1024,256]{1,0:T(8,128)(2,1)}, bf16[1024,256]{1,0:T(8,128)(2,1)}, u32[]{:S(2)}, u32[]{:S(2)}) collective-permute-start(bf16[1024,256]{1,0:T(8,128)(2,1)} %shard_map.73.refs_4_), channel_id=1, source_target_pairs={{0,16},{4,20},{8,24},{12,28},{16,0},{20,4},{24,8},{28,12},{1,17},{... | collective-permute-start | bytes 1572872 | tf_op jit(solution)/shard_map/ppermute | solution.py:394
  71.1 15.9 %collective-permute-start.3 = (f32[1024,128]{1,0:T(8,128)}, f32[1024,128]{1,0:T(8,128)}, u32[]{:S(2)}, u32[]{:S(2)}) collective-permute-start(f32[1024,128]{1,0:T(8,128)} %shard_map.67.refs_0_.refs_1_.refs_2_), channel_id=1, source_target_pairs={{0,4},{4,0},{8,12},{12,8},{16,20},{20,16},{24,28},{28,24},{1,5},{5... | collective-permute-start | bytes 1572872 | tf_op jit(solution)/shard_map/ppermute | solution.py:397
  73.0 29.1 %collective-permute-start.15 = (bf16[1024,256]{1,0:T(8,128)(2,1)}, bf16[1024,256]{1,0:T(8,128)(2,1)}, u32[]{:S(2)}, u32[]{:S(2)}) collective-permute-start(bf16[1024,256]{1,0:T(8,128)(2,1)} %shard_map.75.refs_2_.refs_5_), channel_id=1, source_target_pairs={{0,8},{4,12},{8,0},{12,4},{16,24},{20,28},{24,16},{28,20},{1,9},{5... | collective-permute-start | bytes 1572872 | tf_op jit(solution)/shard_map/ppermute | solution.py:391
  83.8 18.4 %collective-permute-start.16 = (bf16[1024,256]{1,0:T(8,128)(2,1)}, bf16[1024,256]{1,0:T(8,128)(2,1)}, u32[]{:S(2)}, u32[]{:S(2)}) collective-permute-start(bf16[1024,256]{1,0:T(8,128)(2,1)} %shard_map.75.refs_2_.refs_5_), channel_id=1, source_target_pairs={{0,16},{4,20},{8,24},{12,28},{16,0},{20,4},{24,8},{28,12},{1,17},{... | collective-permute-start | bytes 1572872 | tf_op jit(solution)/shard_map/ppermute | solution.py:394
  85.1 17.1 %collective-permute-start.10 = (bf16[1024,256]{1,0:T(8,128)(2,1)}, bf16[1024,256]{1,0:T(8,128)(2,1)}, u32[]{:S(2)}, u32[]{:S(2)}) collective-permute-start(bf16[1024,256]{1,0:T(8,128)(2,1)} %get-tuple-element.47.refs_0_), channel_id=1, source_target_pairs={{1,0},{2,3},{5,4},{6,7},{9,8},{10,11},{13,12},{14,15},{17,16},{18,... | collective-permute-start | bytes 1572872 | tf_op jit(solution)/shard_map/ppermute | solution.py:388
  87.1 24.0 %collective-permute-start.23 = (bf16[1024,256]{1,0:T(8,128)(2,1)}, bf16[1024,256]{1,0:T(8,128)(2,1)}, u32[]{:S(2)}, u32[]{:S(2)}) collective-permute-start(bf16[1024,256]{1,0:T(8,128)(2,1)} %get-tuple-element.61.refs_0_), channel_id=1, source_target_pairs={{1,0},{2,3},{5,4},{6,7},{9,8},{10,11},{13,12},{14,15},{17,16},{18,... | collective-permute-start | bytes 1572872 | tf_op jit(solution)/shard_map/ppermute | solution.py:388
  88.6 26.3 %collective-permute-start.21 = (bf16[1024,256]{1,0:T(8,128)(2,1)}, bf16[1024,256]{1,0:T(8,128)(2,1)}, u32[]{:S(2)}, u32[]{:S(2)}) collective-permute-start(bf16[1024,256]{1,0:T(8,128)(2,1)} %get-tuple-element.59.refs_8_), channel_id=1, source_target_pairs={{0,8},{4,12},{8,0},{12,4},{16,24},{20,28},{24,16},{28,20},{1,9},{5... | collective-permute-start | bytes 1572872 | tf_op jit(solution)/shard_map/ppermute | solution.py:391
  102.2 12.8 %collective-permute-start.22 = (bf16[1024,256]{1,0:T(8,128)(2,1)}, bf16[1024,256]{1,0:T(8,128)(2,1)}, u32[]{:S(2)}, u32[]{:S(2)}) collective-permute-start(bf16[1024,256]{1,0:T(8,128)(2,1)} %get-tuple-element.58.refs_2_.refs_7_), channel_id=1, source_target_pairs={{0,16},{4,20},{8,24},{12,28},{16,0},{20,4},{24,8},{28,12},{1,17},{... | collective-permute-start | bytes 1572872 | tf_op jit(solution)/shard_map/ppermute | solution.py:394
  105.5 13.9 %collective-permute-start.19 = (bf16[1024,256]{1,0:T(8,128)(2,1)}, bf16[1024,256]{1,0:T(8,128)(2,1)}, u32[]{:S(2)}, u32[]{:S(2)}) collective-permute-start(bf16[1024,256]{1,0:T(8,128)(2,1)} %shard_map.79.refs_1_.refs_12_), channel_id=1, source_target_pairs={{0,8},{4,12},{8,0},{12,4},{16,24},{20,28},{24,16},{28,20},{1,9},{5... | collective-permute-start | bytes 1572872 | tf_op jit(solution)/shard_map/ppermute | solution.py:391
  106.3 32.1 %collective-permute-start.27 = (bf16[1024,256]{1,0:T(8,128)(2,1)}, bf16[1024,256]{1,0:T(8,128)(2,1)}, u32[]{:S(2)}, u32[]{:S(2)}) collective-permute-start(bf16[1024,256]{1,0:T(8,128)(2,1)} %shard_map.69.refs_2_), channel_id=1, source_target_pairs={{0,1},{1,0},{2,3},{3,2},{4,5},{5,4},{6,7},{7,6},{8,9},{9,8},{10,11... | collective-permute-start | bytes 1572872 | tf_op jit(solution)/shard_map/ppermute | solution.py:388
  111.1 27.3 %collective-permute-start.20 = (bf16[1024,256]{1,0:T(8,128)(2,1)}, bf16[1024,256]{1,0:T(8,128)(2,1)}, u32[]{:S(2)}, u32[]{:S(2)}) collective-permute-start(bf16[1024,256]{1,0:T(8,128)(2,1)} %shard_map.79.refs_1_.refs_12_), channel_id=1, source_target_pairs={{0,16},{4,20},{8,24},{12,28},{16,0},{20,4},{24,8},{28,12},{1,17},{... | collective-permute-start | bytes 1572872 | tf_op jit(solution)/shard_map/ppermute | solution.py:394
  114.8 23.6 %collective-permute-start.24 = (bf16[1024,256]{1,0:T(8,128)(2,1)}, bf16[1024,256]{1,0:T(8,128)(2,1)}, u32[]{:S(2)}, u32[]{:S(2)}) collective-permute-start(bf16[1024,256]{1,0:T(8,128)(2,1)} %shard_map.68.refs_0_), channel_id=1, source_target_pairs={{0,1},{1,0},{2,3},{3,2},{4,5},{5,4},{6,7},{7,6},{8,9},{9,8},{10,11... | collective-permute-start | bytes 1572872 | tf_op jit(solution)/shard_map/ppermute | solution.py:388
  114.9 23.5 %collective-permute-start.25 = (bf16[1024,256]{1,0:T(8,128)(2,1)}, bf16[1024,256]{1,0:T(8,128)(2,1)}, u32[]{:S(2)}, u32[]{:S(2)}) collective-permute-start(bf16[1024,256]{1,0:T(8,128)(2,1)} %shard_map.81.refs_2_.refs_13_), channel_id=1, source_target_pairs={{0,8},{4,12},{8,0},{12,4},{16,24},{20,28},{24,16},{28,20},{1,9},{5... | collective-permute-start | bytes 1572872 | tf_op jit(solution)/shard_map/ppermute | solution.py:391
  119.5 19.0 %collective-permute-start.26 = (bf16[1024,256]{1,0:T(8,128)(2,1)}, bf16[1024,256]{1,0:T(8,128)(2,1)}, u32[]{:S(2)}, u32[]{:S(2)}) collective-permute-start(bf16[1024,256]{1,0:T(8,128)(2,1)} %shard_map.81.refs_2_.refs_13_), channel_id=1, source_target_pairs={{0,16},{4,20},{8,24},{12,28},{16,0},{20,4},{24,8},{28,12},{1,17},{... | collective-permute-start | bytes 1572872 | tf_op jit(solution)/shard_map/ppermute | solution.py:394
  138.5 16.9 %collective-permute-start.31 = (bf16[1024,256]{1,0:T(8,128)(2,1)}, bf16[1024,256]{1,0:T(8,128)(2,1)}, u32[]{:S(2)}, u32[]{:S(2)}) collective-permute-start(bf16[1024,256]{1,0:T(8,128)(2,1)} %get-tuple-element.66.refs_5_.refs_15_), channel_id=1, source_target_pairs={{0,16},{4,20},{8,24},{12,28},{16,0},{20,4},{24,8},{28,12},{1,17},{... | collective-permute-start | bytes 1572872 | tf_op jit(solution)/shard_map/ppermute | solution.py:394
  139.5 15.8 %collective-permute-start.30 = (bf16[1024,256]{1,0:T(8,128)(2,1)}, bf16[1024,256]{1,0:T(8,128)(2,1)}, u32[]{:S(2)}, u32[]{:S(2)}) collective-permute-start(bf16[1024,256]{1,0:T(8,128)(2,1)} %get-tuple-element.67.refs_6_), channel_id=1, source_target_pairs={{0,8},{4,12},{8,0},{12,4},{16,24},{20,28},{24,16},{28,20},{1,9},{5... | collective-permute-start | bytes 1572872 | tf_op jit(solution)/shard_map/ppermute | solution.py:391
  154.7 8.8 %collective-permute-start.28 = (bf16[1024,256]{1,0:T(8,128)(2,1)}, bf16[1024,256]{1,0:T(8,128)(2,1)}, u32[]{:S(2)}, u32[]{:S(2)}) collective-permute-start(bf16[1024,256]{1,0:T(8,128)(2,1)} %get-tuple-element.74), channel_id=1, source_target_pairs={{0,4},{4,0},{8,12},{12,8},{16,20},{20,16},{24,28},{28,24},{1,5},{5... | collective-permute-start | bytes 1572872 | tf_op jit(solution)/shard_map/ppermute | solution.py:397
  154.8 8.8 %collective-permute-start.29 = (bf16[1024,256]{1,0:T(8,128)(2,1)}, bf16[1024,256]{1,0:T(8,128)(2,1)}, u32[]{:S(2)}, u32[]{:S(2)}) collective-permute-start(bf16[1024,256]{1,0:T(8,128)(2,1)} %get-tuple-element.75), channel_id=1, source_target_pairs={{0,4},{4,0},{8,12},{12,8},{16,20},{20,16},{24,28},{28,24},{1,5},{5... | collective-permute-start | bytes 1572872 | tf_op jit(solution)/shard_map/ppermute | solution.py:397
  162.8 2.3 %collective-permute-start.32 = (bf16[1024,256]{1,0:T(8,128)(2,1)}, bf16[1024,256]{1,0:T(8,128)(2,1)}, u32[]{:S(2)}, u32[]{:S(2)}) collective-permute-start(bf16[1024,256]{1,0:T(8,128)(2,1)} %get-tuple-element.81), channel_id=1, source_target_pairs={{0,4},{4,0},{8,12},{12,8},{16,20},{20,16},{24,28},{28,24},{1,5},{5... | collective-permute-start | bytes 1572872 | tf_op jit(solution)/shard_map/ppermute | solution.py:397

commit v3 on v2

v3 whole, which is shorter than its diff:
```python
import functools

import jax
import jax.numpy as jnp
from jax import lax
from jax.experimental import pallas as pl
from jax.experimental.pallas import tpu as pltpu
from jax.sharding import PartitionSpec as P

VMEM_BYTES = 64 * 1024 * 1024 - 256 * 1024
IN_SMEM = pl.BlockSpec(memory_space=pltpu.SMEM)
IN_HBM = pl.BlockSpec(memory_space=pl.ANY)
PARAMS = pltpu.CompilerParams(vmem_limit_bytes=VMEM_BYTES)
NO_COST = pl.CostEstimate(flops=1, bytes_accessed=1, transcendentals=0)


def after(arrays, earlier):
    count = len(arrays)

    def body(*refs):
        del refs

    return pl.pallas_call(
        body,
        in_specs=[IN_HBM] * (count + len(earlier)),
        out_specs=[IN_HBM] * count,
        out_shape=[jax.ShapeDtypeStruct(x.shape, x.dtype) for x in arrays],
        input_output_aliases={n: n for n in range(count)},
        cost_estimate=NO_COST,
        compiler_params=PARAMS,
    )(*arrays, *earlier)


class Group:
    def __init__(self, blocks, before=None, column=None):
        self.blocks, self.before, self.column = blocks, before, column


def products_body(plan, scalars, *refs):
    layouts, places, finals, befores, sides, tile, stacked, in_count = plan
    hbm_rows = refs[: 2 * sides]
    place = 2 * sides
    array_count = sum(len(counts) for layout in layouts for counts in layout)
    if stacked:
        arrays = [refs[place].at[n] for n in range(array_count)]
        place += 1
    else:
        arrays = refs[place : place + array_count]
        place += array_count
    before_hbm = []
    for before in befores:
        before_hbm.append(refs[place : place + sides] if before else None)
        place += sides if before else 0
    outs = refs[in_count : in_count + sides * len(layouts)]
    scratch = refs[in_count + sides * len(layouts) :]
    t_refs, meta_refs = scratch[:sides], scratch[sides : 2 * sides]
    held = scratch[2 * sides : 2 * sides + array_count]
    staged, before_ref, t_sems, meta_sems, v_sems, before_sems, out_sems = scratch[2 * sides + array_count :]
    slots = t_refs[0].shape[0]
    width = staged.shape[2]
    tiles = slots // tile
    steps = [(side, i) for side in range(sides) for i in range(tiles)]

    def t_copy(step):
        side, i = steps[step]
        rows = pl.ds(i * tile, tile)
        return pltpu.make_async_copy(hbm_rows[side].at[rows, :], t_refs[side].at[rows, :], t_sems.at[step])

    def meta_copy(side):
        return pltpu.make_async_copy(hbm_rows[sides + side], meta_refs[side], meta_sems.at[side])

    def v_copy(n):
        return pltpu.make_async_copy(arrays[n], held[n], v_sems.at[n])

    def before_copy(g, side):
        rows = pl.ds(side * slots, slots)
        return pltpu.make_async_copy(before_hbm[g][side], before_ref.at[g, rows, :], before_sems.at[g * sides + side])

    def out_copy(g, step):
        side, i = steps[step]
        rows = pl.ds(i * tile, tile)
        if side == 0 and finals[g] is not None:
            first = next(n for n in range(len(finals)) if finals[n] is not None)
            columns = pl.ds(pl.multiple_of(scalars[finals[g]], 128), width)
            target = outs[first * sides].at[rows, columns]
        else:
            target = outs[g * sides + side].at[rows, :]
        return pltpu.make_async_copy(
            staged.at[g, pl.ds(step * tile, tile), :], target, out_sems.at[g * len(steps) + step]
        )

    v_copy(0).start()
    meta_copy(0).start()
    for step in range(tiles):
        t_copy(step).start()
    for n in range(1, array_count):
        v_copy(n).start()
    for step in range(tiles, len(steps)):
        t_copy(step).start()
    if sides == 2:
        meta_copy(1).start()
    for g in range(len(layouts)):
        for side in range(sides if befores[g] else 0):
            before_copy(g, side).start()
    for step, (side, i) in enumerate(steps):
        if i == 0:
            meta_copy(side).wait()
            for later in range(tiles):
                t_copy(step + later).wait()
            if step == 0:
                for n in range(array_count):
                    v_copy(n).wait()
            for g in range(len(layouts)):
                if befores[g]:
                    before_copy(g, side).wait()
        rows = pl.ds(i * tile, tile)
        here = pl.ds(step * tile, tile)
        used = 0
        for g, layout in enumerate(layouts):
            total = None
            for counts, (at, starts) in zip(layout, places[g]):
                channel = (jnp.int32(at) if stacked else scalars[at]).astype(jnp.float32)
                scale = jnp.where(meta_refs[side][rows, 0:1] == channel, meta_refs[side][rows, 1:2], 0.0)
                product = None
                for count, first in zip(counts, starts):
                    part = jnp.dot(
                        t_refs[side][rows, first : first + count],
                        held[used][...],
                        preferred_element_type=jnp.float32,
                    )
                    product = part if product is None else product + part
                    used += 1
                total = scale * product if total is None else total + scale * product
            if befores[g]:
                total = total + before_ref[g, here, :].astype(jnp.float32)
            staged[g, here, :] = total.astype(staged.dtype)
        if i == tiles - 1:
            for g in range(len(layouts)):
                for done in range(step - tiles + 1, step + 1):
                    out_copy(g, done).start()
    for g in range(len(layouts)):
        for step in range(len(steps)):
            out_copy(g, step).wait()


def products(table, t_rows, metas, groups, earlier, out=None, result=None):
    sides = len(t_rows)
    slots, depth = t_rows[0].shape
    dtype = t_rows[0].dtype
    tile = min(512, slots)
    stacked = not isinstance(groups[0].blocks[0][1], list)
    if stacked:
        arrays = [groups[0].blocks[0][1]]
        width = arrays[0].shape[2]
        held = [pltpu.VMEM(arrays[0].shape[1:], dtype)] * len(groups[0].blocks)
        layouts = (((depth,),) * len(groups[0].blocks),)
        places = (tuple((channel, (0,)) for channel, _ in groups[0].blocks),)
    else:
        arrays = [x for group in groups for _, parts in group.blocks for _, x in parts]
        width = arrays[0].shape[1]
        held = [pltpu.VMEM(x.shape, dtype) for x in arrays]
        layouts = tuple(
            tuple(tuple(x.shape[0] for _, x in parts) for _, parts in group.blocks) for group in groups
        )
        places = tuple(
            tuple((channel, tuple(n for n, _ in parts)) for channel, parts in group.blocks) for group in groups
        )
    operands = [*t_rows, *metas, *arrays]
    for group in groups:
        operands.extend(group.before or ())
    aliases, totals = {}, []
    for n, group in enumerate(groups):
        totals.extend([jax.ShapeDtypeStruct((slots, width), dtype)] * sides)
        if group.column is not None and result is not None:
            totals[n * sides] = jax.ShapeDtypeStruct(result, dtype)
            result = None
            if out is not None:
                aliases[1 + len(operands)] = n * sides
                operands.append(out)
        elif group.column is not None:
            totals[n * sides] = jax.ShapeDtypeStruct((16, width), dtype)
    operands.extend(earlier)
    steps = sides * (slots // tile)
    finals = tuple(group.column for group in groups)
    befores = tuple(group.before is not None for group in groups)
    plan = (layouts, places, finals, befores, sides, tile, stacked, len(operands))
    height = sides * slots
    sums = pl.pallas_call(
        functools.partial(products_body, plan),
        in_specs=[IN_SMEM] + [IN_HBM] * len(operands),
        out_specs=[IN_HBM] * len(totals),
        out_shape=totals,
        input_output_aliases=aliases,
        scratch_shapes=[
            *[pltpu.VMEM((slots, depth), dtype)] * sides,
            *[pltpu.VMEM(metas[0].shape, metas[0].dtype)] * sides,
            *held,
            pltpu.VMEM((len(groups), height, width), dtype),
            pltpu.VMEM((len(groups), height if any(befores) else 16, width), dtype),
            pltpu.SemaphoreType.DMA((steps,)),
            pltpu.SemaphoreType.DMA((sides,)),
            pltpu.SemaphoreType.DMA((len(held),)),
            pltpu.SemaphoreType.DMA((sides * len(groups),)),
            pltpu.SemaphoreType.DMA((steps * len(groups),)),
        ],
        cost_estimate=NO_COST,
        compiler_params=PARAMS,
    )(table, *operands)
    return [sums[n * sides : (n + 1) * sides] for n in range(len(groups))]


def place(table, out, columns, arrays, earlier):
    count, pieces = len(arrays), 2
    slots, width = arrays[0].shape
    part = slots // pieces

    def body(table_ref, *refs):
        out_ref, staged, got, put = refs[-4:]

        def fetch(n, p):
            rows = pl.ds(p * part, part)
            return pltpu.make_async_copy(refs[n].at[rows, :], staged.at[n, rows, :], got.at[n * pieces + p])

        def store(n, p):
            rows = pl.ds(p * part, part)
            there = pl.ds(pl.multiple_of(table_ref[columns[n]], 128), width)
            return pltpu.make_async_copy(staged.at[n, rows, :], out_ref.at[rows, there], put.at[n * pieces + p])

        every = [(n, p) for n in range(count) for p in range(pieces)]
        for n, p in every:
            fetch(n, p).start()
        for n, p in every:
            fetch(n, p).wait()
            store(n, p).start()
        for n, p in every:
            store(n, p).wait()

    return pl.pallas_call(
        body,
        in_specs=[IN_SMEM] + [IN_HBM] * (count + 1 + len(earlier)),
        out_specs=IN_HBM,
        out_shape=jax.ShapeDtypeStruct(out.shape, out.dtype),
        input_output_aliases={1 + count: 0},
        scratch_shapes=[
            pltpu.VMEM((count, slots, width), out.dtype),
            pltpu.SemaphoreType.DMA((count * pieces,)),
            pltpu.SemaphoreType.DMA((count * pieces,)),
        ],
        cost_estimate=NO_COST,
        compiler_params=PARAMS,
    )(table, *arrays, out, *earlier)


def inverse_take(order, values):
    hit = order[None, :] == jnp.arange(order.shape[0], dtype=order.dtype)[:, None]
    return [jnp.sum(jnp.where(hit, value[None, :], 0.0), axis=1) for value in values]


def meta_to_send(recv_order, ph_channel, recouple_weight, earlier=None):
    slots = recv_order.shape[0]
    group = lax.axis_size("chan")
    member = lax.axis_index("int") * slots
    ids = lax.dynamic_slice(ph_channel, (member,), (slots,)).astype(jnp.float32)
    scale = lax.dynamic_slice(recouple_weight, (member,), (slots,))
    back = jnp.stack(inverse_take(recv_order, [ids, scale]), axis=0)
    back = back.reshape(2, group, slots // group).transpose(1, 0, 2)
    return back if earlier is None else after([back], [earlier])[0]


def meta_over(back):
    return lax.all_to_all(back, "chan", split_axis=0, concat_axis=0, tiled=True)


def meta_of_rows(send_order, returned):
    back = returned.transpose(1, 0, 2).reshape(2, -1)
    ids, scale = inverse_take(send_order, [back[0], back[1]])
    lane = jnp.arange(128)[None, :]
    return jnp.where(lane == 0, ids[:, None], jnp.where(lane == 1, scale[:, None], 0.0))


def general_plan(t_pp, interaction, meta):
    slots, depth = t_pp.shape
    channels, _, width = interaction.shape
    group, members = lax.axis_size("chan"), lax.axis_size("int")
    flat = interaction.reshape(channels * depth, width)
    share = flat.shape[0] // group
    mine = lax.dynamic_slice(flat, (lax.axis_index("chan") * share, 0), (share, width))
    everyone = lax.all_gather(mine, ("chan", "int"), axis=0, tiled=False)
    everyone = everyone.reshape(group, members, share, width)
    out = None
    for member in range(members):
        whole = everyone[:, member].reshape(channels, depth, width)
        group_of = Group([(channel, whole) for channel in range(channels)], column=0)
        table = jnp.full((1,), member * width, jnp.int32)
        ((out,),) = products(table, [t_pp], [meta], [group_of], [], out=out, result=(slots, members * width))
    return out


def grid_plan(t_pp, interaction, meta_sent, meta_over, meta_got):
    slots, depth = t_pp.shape
    channels, _, width = interaction.shape
    group, members = lax.axis_size("chan"), lax.axis_size("int")
    axes = ("chan", "int")
    c, z = lax.axis_index("chan"), lax.axis_index("int")
    core, chip = c % 2, c // 2
    half, part = depth // 2, width // 2
    shape = (slots, members * width)

    def at(chan, member):
        return chan * members + member

    def along(pairs):
        return [(at(a, m), at(a, n)) for a in range(group) for m, n in pairs]

    outer = along([(0, 1), (1, 0), (2, 3), (3, 2)])
    middle = along([(1, 2), (2, 1)])
    outwards = along([(1, 0), (2, 3)])
    near_pairs = [(a, a ^ (4 if a % 2 else 2)) for a in range(group)]
    far_pairs = [(a, a ^ (2 if a % 2 else 4)) for a in range(group)]
    other = [(a, a ^ 1) for a in range(group)]

    def step(x, pairs):
        return lax.ppermute(x, axes, pairs)

    def by_near(x):
        return lax.ppermute(x, "chan", near_pairs)

    def by_far(x):
        return lax.ppermute(x, "chan", far_pairs)

    def sib(x):
        return lax.ppermute(x, "chan", other)

    end = (z == 0) | (z == members - 1)
    low = z < members // 2
    mine, theirs = core * part, (1 - core) * part
    starts = [(z ^ 1) * width, jnp.where(low, 2, 1) * width, jnp.where(low, 3, 0) * width]
    table = [chip, chip ^ (1 + core), chip ^ (2 - core), chip ^ 3] + [z * width] + [n + mine for n in starts] + [n + theirs for n in starts]
    table = jnp.stack(table).astype(jnp.int32)
    own_column, columns, other_columns = 4, (5, 6, 7), (8, 9, 10)

    def quarter(n, x):
        return (n, [(0, x)])

    def own_rows(channel):
        rows = lax.dynamic_slice(interaction, (channel, 0, core * part), (1, depth, part))
        return rows.reshape(depth, part)

    (own,) = after([own_rows(chip)], [])
    p1, p2 = step(own, outer), step(own, middle)
    other_t = sib(t_pp)
    fence = sib(own[:16])
    meta = meta_got(meta_over(meta_sent(fence)))
    (later,) = after([table], [meta])
    extra = own_rows(later[3])
    meta, extra = after([meta, extra], [own])

    p1, p2, other_t = after([p1, p2, other_t], [meta])
    near1, p3, far1, p4 = by_near(p1), step(p2, outwards), by_far(p1), step(p1, middle)
    other_meta = sib(meta)
    local = Group([(channel, interaction) for channel in range(channels)], column=own_column)
    ((out,),) = products(table, [t_pp], [meta], [local], [p1], result=shape)

    near1, far1, p3, other_meta = after([near1, far1, p3, other_meta], [out])
    s2 = jnp.where(end, p3, p2)
    far2, near2 = by_far(s2), by_near(s2)
    (p4,) = after([p4], [s2])
    p5 = step(p4, outwards)
    t_rows = [t_pp, other_t]
    metas = [meta, other_meta]
    (sum1,) = products(table, t_rows, metas, [Group([quarter(0, p1), quarter(1, near1), quarter(2, far1)])], [p4])

    far2, near2, p5 = after([far2, near2, p5], [sum1[0]])
    across2 = by_near(far2)
    s3 = jnp.where(end, p5, p4)
    (extra,) = after([extra], [s3])
    far3, e, near3 = by_far(s3), step(extra, outer), by_near(s3)
    sum2, sum3 = products(
        table, t_rows, metas,
        [Group([quarter(0, s2), quarter(1, near2), quarter(2, far2)]), Group([quarter(0, s3)])],
        [extra],
    )
    across2, e = after([across2, e], [sum2[0]])
    (out, rest1), (_, rest2) = products(
        table, t_rows, metas,
        [
            Group([quarter(3, e)], before=sum1, column=columns[0]),
            Group([quarter(3, across2)], before=sum2, column=columns[1]),
        ],
        [across2], out=out, result=shape,
    )
    back1, back2 = sib(rest1), sib(rest2)

    far3, near3 = after([far3, near3], [out])
    across3 = by_near(far3)
    (sum3,) = products(
        table, t_rows, metas, [Group([quarter(1, near3), quarter(2, far3)], before=sum3)], [near3]
    )
    back3 = sib(sum3[1])

    out = place(table, out, other_columns[:2], [back1, back2], [sum3[0]])

    (across3,) = after([across3], [out])
    groups = [
        Group([quarter(3, across3)], before=[sum3[0]], column=columns[2]),
        Group([quarter(3, sib(across3))], before=[back3], column=other_columns[2]),
    ]
    ((out,), _) = products(table, [t_pp], [meta], groups, [], out=out, result=shape)
    return out


def on_device(t_pp, interaction, send_order, recv_order, ph_channel, recouple_weight):
    sent = functools.partial(meta_to_send, recv_order, ph_channel, recouple_weight)
    got = functools.partial(meta_of_rows, send_order)
    planes = lax.axis_size("chan") // 2
    if planes == 4 and lax.axis_size("int") == 4 and interaction.shape[0] == planes:
        return grid_plan(t_pp, interaction, sent, meta_over, got)
    return general_plan(t_pp, interaction, got(meta_over(sent())))


def solution(mesh):
    in_specs = (
        P(("chan", "int"), None),
        P(None, None, "int"),
        P(("chan", "int")),
        P(("chan", "int")),
        P("chan"),
        P("chan"),
    )
    out_specs = P(("chan", "int"), None)
    return jax.shard_map(
        on_device, mesh=mesh, in_specs=in_specs, out_specs=out_specs, check_vma=False
    )
```

time: 171 us -> 161 us (0.942); the launches traced: 168 us -> 160 us
  starting transfers between devices: 47.1 us -> 25.8 us
  waiting for transfers between devices: 24.4 us -> 40.9 us
  Pallas kernels: 82.3 us -> 73.2 us
  local copies, waits for them, and re-layouts: 5.82 us -> 8.36 us
    ppermute x12 -> x6, waiting for transfers between devices: 6.09 us -> 25.7 us  [step(): return lax.ppermute(x, axes, pairs)]
    pallas_call x7 -> x0, Pallas kernels: 14.7 us -> none  [the longest x3 7.55 us: cut(): pl.pallas_call(body, in_specs=[IN_SMEM] + [IN_HBM] * (1 + len(earlier)),...]
    ppermute x16 -> x8, starting transfers between devices: 20.5 us -> 8.62 us  [the longest x5 6.03 us: by_near(): return lax.ppermute(x, 'chan', near_pairs)]
    ppermute x12 -> x6, starting transfers between devices: 21.8 us -> 11.7 us  [step(): return lax.ppermute(x, axes, pairs)]
    pallas_call x5 -> x6, Pallas kernels: 64.7 us -> 70.5 us  [products(): pl.pallas_call(functools.partial(products_body, plan), in_specs=[IN_SMEM]...]
    select_n x0 -> x2, other arithmetic: none -> 4.64 us  [the longest x1 2.35 us: grid_plan(): s3 = jnp.where(end, p5, p4)]
    ppermute x16 -> x8, waiting for transfers between devices: 12 us -> 7.96 us  [the longest x5 7.95 us: by_near(): return lax.ppermute(x, 'chan', near_pairs)]
    another operation x5 -> x0, other arithmetic: 3.03 us -> none  [the longest x3 1.81 us: cut(): jnp.stack([jnp.asarray(n, jnp.int32) for n in index])]
  transfers between devices with their start and end apart: 34 -> 22, of which waited for: 7 -> 10; matrix products, arithmetic and copies ran while one was open for 8% -> 9% of each run, Pallas kernels for 47% -> 41%
where the time goes in v3:
time: 161 us; the launch traced here: 160 us
  Pallas kernels  73.2 us (45%)
  waiting for transfers between devices  40.9 us (25%)
  starting transfers between devices  25.8 us (16%)
  other arithmetic  9.59 us (6%)
  local copies, waits for them, and re-layouts  8.36 us (5%)
  between operations  2.06 us (1%)
    pallas_call x6, Pallas kernels, products(): pl.pallas_call(functools.partial(products_body, plan), in_specs=[IN_SMEM]...  70.5 us
    ppermute x6, waiting for transfers between devices, step(): return lax.ppermute(x, axes, pairs)  25.7 us
    ppermute x6, starting transfers between devices, step(): return lax.ppermute(x, axes, pairs)  11.7 us
    ppermute x5, waiting for transfers between devices, by_near(): return lax.ppermute(x, 'chan', near_pairs)  7.95 us
    ppermute x5, starting transfers between devices, by_near(): return lax.ppermute(x, 'chan', near_pairs)  6.03 us
    reshape x2, local copies, waits for them, and re-layouts, own_rows(): return rows.reshape(depth, part)  4.57 us
    all_to_all x1, waiting for transfers between devices, meta_over(): return lax.all_to_all(back, 'chan', split_axis=0, concat_axis=0, tiled=True)  4.05 us
    all_to_all x1, starting transfers between devices, meta_over(): return lax.all_to_all(back, 'chan', split_axis=0, concat_axis=0, tiled=True)  3.72 us
  transfers between devices with their start and end apart: 22, of which 10 were waited for; matrix products, arithmetic and copies ran while one was open for 9% of the time, Pallas kernels for 41%

profile of v3, /device:TPU:0, one launch (start us, length us, event | category | flops | bytes accessed | tf_op | source)
XLA Modules:
  0.0 159.9 jit_solution(3230246213863942901)
XLA Ops:
  0.0 0.5 collective-permute-start.3
  0.5 2.3 %dynamic-slice_bitcast_fusion.1.refs_0_ = bf16[2048,256]{1,0:T(8,128)(2,1)} fusion(bf16[4,2048,512]{2,1,0:T(8,128)(2,1)} %refs_2_.1, s32[]{:T(128)S(6)} %select_n.72, s32[]{:T(128)S(6)} %select_n.73), kind=kLoop, calls=%fused_computation.7 | loop fusion | bytes 2097160 | tf_op jit(solution)/shard_map/reshape | solution.py:347
  2.7 2.6 %collective-permute-start.1 = (bf16[2048,256]{1,0:T(8,128)(2,1)}, bf16[2048,256]{1,0:T(8,128)(2,1)}, u32[]{:S(2)}, u32[]{:S(2)}) collective-permute-start(bf16[2048,256]{1,0:T(8,128)(2,1)} %shard_map.64.refs_2_), channel_id=1, source_target_pairs={{0,1},{1,0},{2,3},{3,2},{4,5},{5,4},{6,7},{7,6},{8,9},{9,8},{10,11... | collective-permute-start | bytes 3145736 | tf_op jit(solution)/shard_map/ppermute | solution.py:323
  5.3 1.6 %collective-permute-start.2 = (bf16[2048,256]{1,0:T(8,128)(2,1)}, bf16[2048,256]{1,0:T(8,128)(2,1)}, u32[]{:S(2)}, u32[]{:S(2)}) collective-permute-start(bf16[2048,256]{1,0:T(8,128)(2,1)} %shard_map.64.refs_2_), channel_id=1, source_target_pairs={{1,2},{2,1},{5,6},{6,5},{9,10},{10,9},{13,14},{14,13},{17,18},{18,... | collective-permute-start | bytes 3145736 | tf_op jit(solution)/shard_map/ppermute | solution.py:323
  7.0 0.7 slice.18
  7.7 0.2 collective-permute-start
  7.9 0.7 dynamic_slice.13
  8.5 0.7 dynamic-slice_convert_fusion
  9.2 1.2 select_reduce_fusion.3
  10.5 0.6 maximum_bitcast_fusion.refs_0_
  11.1 0.0 collective-permute-done.refs_1_
  11.1 0.6 copy-done.1
  11.7 3.7 %all-to-all-start = ((f32[8,2,128]{2,1,0:T(2,128)}), f32[8,2,128]{2,1,0:T(2,128)S(1)}, u32[]{:S(2)}, u32[]{:S(2)}) async-start(f32[8,2,128]{2,1,0:T(2,128)} %shard_map.65), calls=%async_computation | async-start | bytes 16384 | tf_op jit(solution)/shard_map/all_to_all | solution.py:271
  15.4 0.1 stack.56.scalars.table_ref
  15.5 0.5 copy.34.refs_0_
  16.1 4.1 %all-to-all-done = f32[8,2,128]{2,1,0:T(2,128)S(1)} async-done(((f32[8,2,128]{2,1,0:T(2,128)}), f32[8,2,128]{2,1,0:T(2,128)S(1)}, u32[]{:S(2)}, u32[]{:S(2)}) %all-to-all-start) | async-done | bytes 8224 | tf_op jit(solution)/shard_map/all_to_all | solution.py:271
  20.1 1.2 select_reduce_fusion.1
  21.4 1.2 select_select_fusion.refs_1_.refs_0_
  22.5 1.2 slice.17
  25.4 2.3 %dynamic-slice_bitcast_fusion.refs_1_ = bf16[2048,256]{1,0:T(8,128)(2,1)} fusion(bf16[4,2048,512]{2,1,0:T(8,128)(2,1)} %refs_2_.1, s32[]{:T(128)S(6)} %select_n.78, s32[]{:T(128)S(6)} %select_n.73), kind=kLoop, calls=%fused_computation.6 | loop fusion | bytes 2097160 | tf_op jit(solution)/shard_map/reshape | solution.py:347
  27.7 1.7 %collective-permute-done.1.refs_0_ = bf16[2048,256]{1,0:T(8,128)(2,1)} collective-permute-done((bf16[2048,256]{1,0:T(8,128)(2,1)}, bf16[2048,256]{1,0:T(8,128)(2,1)}, u32[]{:S(2)}, u32[]{:S(2)}) %collective-permute-start.1) | collective-permute-done | bytes 1048608 | tf_op jit(solution)/shard_map/ppermute | solution.py:323
  29.4 0.0 collective-permute-done.2.refs_1_
  29.4 0.0 collective-permute-done.3.refs_2_
  29.5 1.7 %collective-permute-start.4 = (bf16[2048,256]{1,0:T(8,128)(2,1)}, bf16[2048,256]{1,0:T(8,128)(2,1)}, u32[]{:S(2)}, u32[]{:S(2)}) collective-permute-start(bf16[2048,256]{1,0:T(8,128)(2,1)} %get-tuple-element.34.refs_3_.refs_4_), channel_id=1, source_target_pairs={{0,8},{4,20},{8,0},{12,28},{16,24},{20,4},{24,16},{28,12},{1,9},{5... | collective-permute-start | bytes 3145736 | tf_op jit(solution)/shard_map/ppermute | solution.py:326
  31.2 1.5 collective-permute-start.5
  32.7 1.3 collective-permute-start.6
  34.0 0.1 collective-permute-start.7
  34.1 1.7 %collective-permute-start.10 = (bf16[2048,256]{1,0:T(8,128)(2,1)}, bf16[2048,256]{1,0:T(8,128)(2,1)}, u32[]{:S(2)}, u32[]{:S(2)}) collective-permute-start(bf16[2048,256]{1,0:T(8,128)(2,1)} %get-tuple-element.34.refs_3_.refs_4_), channel_id=1, source_target_pairs={{1,2},{2,1},{5,6},{6,5},{9,10},{10,9},{13,14},{14,13},{17,18},{18,... | collective-permute-start | bytes 3145736 | tf_op jit(solution)/shard_map/ppermute | solution.py:323
  35.8 15.3 %shard_map.69.refs_4_.refs_10_ = bf16[1024,2048]{1,0:T(8,128)(2,1)} custom-call(s32[11]{0:T(128)} %copy-done, bf16[1024,2048]{1,0:T(8,128)(2,1)} %refs_0_.11, f32[1024,128]{1,0:T(8,128)} %get-tuple-element.33.refs_3_.refs_1_.refs_2_, bf16[4,2048,512]{2,1,0:T(8,128)(2,1)} %refs_2_.1, bf16[2048,256]{1,0:T(8,128)(2,1)} %get-tuple-element.34.refs_3_.refs_4_), custom_call_target="tpu_custom_call" | custom-call | flops 1 | bytes 1 | tf_op jit(solution)/shard_map/pallas_call | solution.py:188
  51.2 0.0 collective-permute-done.7.refs_3_
  51.2 4.6 %collective-permute-done.4.refs_0_ = bf16[2048,256]{1,0:T(8,128)(2,1)} collective-permute-done((bf16[2048,256]{1,0:T(8,128)(2,1)}, bf16[2048,256]{1,0:T(8,128)(2,1)}, u32[]{:S(2)}, u32[]{:S(2)}) %collective-permute-start.4) | collective-permute-done | bytes 1048608 | tf_op jit(solution)/shard_map/ppermute | solution.py:326
  55.8 0.0 collective-permute-done.5.refs_1_
  55.8 5.5 %collective-permute-done.6.refs_2_ = bf16[2048,256]{1,0:T(8,128)(2,1)} collective-permute-done((bf16[2048,256]{1,0:T(8,128)(2,1)}, bf16[2048,256]{1,0:T(8,128)(2,1)}, u32[]{:S(2)}, u32[]{:S(2)}) %collective-permute-start.6) | collective-permute-done | bytes 1048608 | tf_op jit(solution)/shard_map/ppermute | solution.py:323
  61.2 2.3 %broadcast_select_fusion.1.refs_1_.refs_4_ = bf16[2048,256]{1,0:T(8,128)(2,1)} fusion(bf16[2048,256]{1,0:T(8,128)(2,1)} %get-tuple-element.36, bf16[2048,256]{1,0:T(8,128)(2,1)} %get-tuple-element.35, pred[]{:T(512)S(6)} %or.3), kind=kLoop, calls=%fused_computation.9 | loop fusion | flops 524288 | bytes 3145729 | tf_op jit(solution)/shard_map/jit(_where)/select_n | solution.py:365
  63.5 0.0 collective-permute-done.10.refs_0_
  63.5 1.5 collective-permute-start.11
  65.0 0.6 collective-permute-start.8
  65.6 0.5 collective-permute-start.9
  66.1 12.3 %shard_map.72 = (bf16[1024,256]{1,0:T(8,128)(2,1)}, bf16[1024,256]{1,0:T(8,128)(2,1)}) custom-call(s32[11]{0:T(128)} %copy-done, bf16[1024,2048]{1,0:T(8,128)(2,1)} %refs_0_.11, bf16[1024,2048]{1,0:T(8,128)(2,1)} %get-tuple-element.37.refs_1_, f32[1024,128]{1,0:T(8,128)} %get-tuple-element.33.refs_3_.refs_1_.refs_2_, f32[1024,128]{1,0:T(8,128)} %get-tuple-element.38.refs_3_, ...), custom_call_target="tpu_custom_call" | custom-call | flops 1 | bytes 1 | tf_op jit(solution)/shard_map/pallas_call | solution.py:188
  78.4 13.5 %collective-permute-done.11.refs_2_ = bf16[2048,256]{1,0:T(8,128)(2,1)} collective-permute-done((bf16[2048,256]{1,0:T(8,128)(2,1)}, bf16[2048,256]{1,0:T(8,128)(2,1)}, u32[]{:S(2)}, u32[]{:S(2)}) %collective-permute-start.11) | collective-permute-done | bytes 1048608 | tf_op jit(solution)/shard_map/ppermute | solution.py:323
  91.9 0.0 collective-permute-done.8.refs_0_
  91.9 0.0 collective-permute-done.9.refs_1_
  91.9 2.3 %broadcast_select_fusion.refs_1_.refs_7_ = bf16[2048,256]{1,0:T(8,128)(2,1)} fusion(bf16[2048,256]{1,0:T(8,128)(2,1)} %get-tuple-element.42, bf16[2048,256]{1,0:T(8,128)(2,1)} %shard_map.71.refs_7_, pred[]{:T(512)S(6)} %or.3), kind=kLoop, calls=%fused_computation.8 | loop fusion | flops 524288 | bytes 3145729 | tf_op jit(solution)/shard_map/jit(_where)/select_n | solution.py:375
  94.3 3.0 %collective-permute-start.15 = (bf16[2048,256]{1,0:T(8,128)(2,1)}, bf16[2048,256]{1,0:T(8,128)(2,1)}, u32[]{:S(2)}, u32[]{:S(2)}) collective-permute-start(bf16[2048,256]{1,0:T(8,128)(2,1)} %shard_map.74.refs_8_), channel_id=1, source_target_pairs={{0,1},{1,0},{2,3},{3,2},{4,5},{5,4},{6,7},{7,6},{8,9},{9,8},{10,11... | collective-permute-start | bytes 3145736 | tf_op jit(solution)/shard_map/ppermute | solution.py:323
  97.2 1.5 collective-permute-start.14
  98.7 0.5 collective-permute-start.12
  99.2 0.5 collective-permute-start.13
  99.8 15.2 %shard_map.75 = (bf16[1024,256]{1,0:T(8,128)(2,1)}, bf16[1024,256]{1,0:T(8,128)(2,1)}, bf16[1024,256]{1,0:T(8,128)(2,1)}, bf16[1024,256]{1,0:T(8,128)(2,1)}) custom-call(s32[11]{0:T(128)} %copy-done, bf16[1024,2048]{1,0:T(8,128)(2,1)} %refs_0_.11, bf16[1024,2048]{1,0:T(8,128)(2,1)} %get-tuple-element.37.refs_1_, ...), custom_call_target="tpu_custom_call" | custom-call | flops 1 | bytes 1 | tf_op jit(solution)/shard_map/pallas_call | solution.py:188
  115.0 5.0 %collective-permute-done.15.refs_1_ = bf16[2048,256]{1,0:T(8,128)(2,1)} collective-permute-done((bf16[2048,256]{1,0:T(8,128)(2,1)}, bf16[2048,256]{1,0:T(8,128)(2,1)}, u32[]{:S(2)}, u32[]{:S(2)}) %collective-permute-start.15) | collective-permute-done | bytes 1048608 | tf_op jit(solution)/shard_map/ppermute | solution.py:323
  120.0 2.4 %collective-permute-done.14.refs_0_ = bf16[2048,256]{1,0:T(8,128)(2,1)} collective-permute-done((bf16[2048,256]{1,0:T(8,128)(2,1)}, bf16[2048,256]{1,0:T(8,128)(2,1)}, u32[]{:S(2)}, u32[]{:S(2)}) %collective-permute-start.14) | collective-permute-done | bytes 1048608 | tf_op jit(solution)/shard_map/ppermute | solution.py:326
  122.4 10.5 %shard_map.77 = (bf16[1024,2048]{1,0:T(8,128)(2,1)}, bf16[1024,256]{1,0:T(8,128)(2,1)}, bf16[16,256]{1,0:T(8,128)(2,1)}, bf16[1024,256]{1,0:T(8,128)(2,1)}) custom-call(s32[11]{0:T(128)} %copy-done, bf16[1024,2048]{1,0:T(8,128)(2,1)} %refs_0_.11, bf16[1024,2048]{1,0:T(8,128)(2,1)} %get-tuple-element.37.refs_1_, ...), custom_call_target="tpu_custom_call", output_to_operand_aliasing={{0}: (11, {})} | custom-call | flops 1 | bytes 1 | tf_op jit(solution)/shard_map/pallas_call | solution.py:188
  132.9 0.7 collective-permute-done.13.refs_1_
  133.6 1.7 %collective-permute-start.16 = (bf16[2048,256]{1,0:T(8,128)(2,1)}, bf16[2048,256]{1,0:T(8,128)(2,1)}, u32[]{:S(2)}, u32[]{:S(2)}) collective-permute-start(bf16[2048,256]{1,0:T(8,128)(2,1)} %get-tuple-element.52.refs_5_), channel_id=1, source_target_pairs={{0,8},{4,20},{8,0},{12,28},{16,24},{20,4},{24,16},{28,12},{1,9},{5... | collective-permute-start | bytes 3145736 | tf_op jit(solution)/shard_map/ppermute | solution.py:326
  135.4 0.0 collective-permute-start.17
  135.4 0.5 collective-permute-start.18
  135.9 9.9 %shard_map.79 = (bf16[1024,256]{1,0:T(8,128)(2,1)}, bf16[1024,256]{1,0:T(8,128)(2,1)}) custom-call(s32[11]{0:T(128)} %copy-done, bf16[1024,2048]{1,0:T(8,128)(2,1)} %refs_0_.11, bf16[1024,2048]{1,0:T(8,128)(2,1)} %get-tuple-element.37.refs_1_, f32[1024,128]{1,0:T(8,128)} %get-tuple-element.33.refs_3_.refs_1_.refs_2_, f32[1024,128]{1,0:T(8,128)} %get-tuple-element.38.refs_3_, ...), custom_call_target="tpu_custom_call" | custom-call | flops 1 | bytes 1 | tf_op jit(solution)/shard_map/pallas_call | solution.py:188
  145.8 0.0 collective-permute-done.17.refs_0_
  145.9 2.6 %shard_map.80.refs_1_.refs_6_ = bf16[1024,2048]{1,0:T(8,128)(2,1)} custom-call(s32[11]{0:T(128)} %copy-done, bf16[1024,256]{1,0:T(8,128)(2,1)} %collective-permute-done.17.refs_0_, bf16[1024,256]{1,0:T(8,128)(2,1)} %collective-permute-done.18.refs_1_, bf16[1024,2048]{1,0:T(8,128)(2,1)} %get-tuple-element.51.refs_2_, ...), custom_call_target="tpu_custom_call", output_to_operand_aliasing={{}: (3, {})} | custom-call | flops 1 | bytes 1 | tf_op jit(solution)/shard_map/pallas_call | solution.py:238
  148.5 0.2 collective-permute-done.16.refs_0_
  148.8 0.0 collective-permute-start.19
  148.8 0.5 collective-permute-start.20
  149.3 3.2 %collective-permute-done.20.refs_5_ = bf16[1024,256]{1,0:T(8,128)(2,1)} collective-permute-done((bf16[1024,256]{1,0:T(8,128)(2,1)}, bf16[1024,256]{1,0:T(8,128)(2,1)}, u32[]{:S(2)}, u32[]{:S(2)}) %collective-permute-start.20) | collective-permute-done | bytes 524320 | tf_op jit(solution)/shard_map/ppermute | solution.py:332
  152.5 0.0 collective-permute-done.19.refs_3_
  152.5 7.3 %shard_map.82 = (bf16[1024,2048]{1,0:T(8,128)(2,1)}, bf16[16,256]{1,0:T(8,128)(2,1)}) custom-call(s32[11]{0:T(128)} %copy-done, bf16[1024,2048]{1,0:T(8,128)(2,1)} %refs_0_.11, f32[1024,128]{1,0:T(8,128)} %get-tuple-element.33.refs_3_.refs_1_.refs_2_, bf16[2048,256]{1,0:T(8,128)(2,1)} %shard_map.81.refs_2_, ...), custom_call_target="tpu_custom_call", output_to_operand_aliasing={{0}: (7, {})} | custom-call | flops 1 | bytes 1 | tf_op jit(solution)/shard_map/pallas_call | solution.py:188
  (23 shorter events, 0.0 us)
Async XLA Ops:
  0.0 9.2 %copy-start.2 = (s32[1024]{0:T(1024)S(1)}, s32[1024]{0:T(1024)}, u32[]{:S(2)}) copy-start(s32[1024]{0:T(1024)} %param.9) | copy-start | bytes 12292
  0.0 20.1 %copy-start.3 = (s32[1024]{0:T(1024)S(1)}, s32[1024]{0:T(1024)}, u32[]{:S(2)}) copy-start(s32[1024]{0:T(1024)} %param.8) | copy-start | bytes 12292
  0.0 29.4 %collective-permute-start.3 = (bf16[1024,2048]{1,0:T(8,128)(2,1)}, bf16[1024,2048]{1,0:T(8,128)(2,1)}, u32[]{:S(2)}, u32[]{:S(2)}) collective-permute-start(bf16[1024,2048]{1,0:T(8,128)(2,1)} %refs_0_.11), channel_id=1, source_target_pairs={{0,4},{4,0},{8,12},{12,8},{16,20},{20,16},{24,28},{28,24},{1,5},{5... | collective-permute-start | bytes 12582920 | tf_op jit(solution)/shard_map/ppermute | solution.py:332
  2.7 26.7 %collective-permute-start.1 = (bf16[2048,256]{1,0:T(8,128)(2,1)}, bf16[2048,256]{1,0:T(8,128)(2,1)}, u32[]{:S(2)}, u32[]{:S(2)}) collective-permute-start(bf16[2048,256]{1,0:T(8,128)(2,1)} %shard_map.64.refs_2_), channel_id=1, source_target_pairs={{0,1},{1,0},{2,3},{3,2},{4,5},{5,4},{6,7},{7,6},{8,9},{9,8},{10,11... | collective-permute-start | bytes 3145736 | tf_op jit(solution)/shard_map/ppermute | solution.py:323
  5.3 24.1 %collective-permute-start.2 = (bf16[2048,256]{1,0:T(8,128)(2,1)}, bf16[2048,256]{1,0:T(8,128)(2,1)}, u32[]{:S(2)}, u32[]{:S(2)}) collective-permute-start(bf16[2048,256]{1,0:T(8,128)(2,1)} %shard_map.64.refs_2_), channel_id=1, source_target_pairs={{1,2},{2,1},{5,6},{6,5},{9,10},{10,9},{13,14},{14,13},{17,18},{18,... | collective-permute-start | bytes 3145736 | tf_op jit(solution)/shard_map/ppermute | solution.py:323
  7.7 3.4 %collective-permute-start = (bf16[16,256]{1,0:T(8,128)(2,1)S(1)}, bf16[16,256]{1,0:T(8,128)(2,1)S(1)}, u32[]{:S(2)}, u32[]{:S(2)}) collective-permute-start(bf16[16,256]{1,0:T(8,128)(2,1)S(1)} %slice.18), channel_id=1, source_target_pairs={{0,4},{4,0},{8,12},{12,8},{16,20},{20,16},{24,28},{28,24},{1,5},{5... | collective-permute-start | bytes 24584 | tf_op jit(solution)/shard_map/ppermute | solution.py:332
  11.1 0.6 copy-start.1
  11.7 8.4 %all-to-all-start = ((f32[8,2,128]{2,1,0:T(2,128)}), f32[8,2,128]{2,1,0:T(2,128)S(1)}, u32[]{:S(2)}, u32[]{:S(2)}) async-start(f32[8,2,128]{2,1,0:T(2,128)} %shard_map.65), calls=%async_computation | async-start | bytes 16384 | tf_op jit(solution)/shard_map/all_to_all | solution.py:271
  15.5 13.9 %copy-start = (s32[11]{0:T(128)}, s32[11]{0:T(128)S(1)}, u32[]{:S(2)}) copy-start(s32[11]{0:T(128)S(1)} %stack.56.scalars.table_ref) | copy-start | bytes 136
  29.5 26.3 %collective-permute-start.4 = (bf16[2048,256]{1,0:T(8,128)(2,1)}, bf16[2048,256]{1,0:T(8,128)(2,1)}, u32[]{:S(2)}, u32[]{:S(2)}) collective-permute-start(bf16[2048,256]{1,0:T(8,128)(2,1)} %get-tuple-element.34.refs_3_.refs_4_), channel_id=1, source_target_pairs={{0,8},{4,20},{8,0},{12,28},{16,24},{20,4},{24,16},{28,12},{1,9},{5... | collective-permute-start | bytes 3145736 | tf_op jit(solution)/shard_map/ppermute | solution.py:326
  31.2 24.6 %collective-permute-start.5 = (bf16[2048,256]{1,0:T(8,128)(2,1)}, bf16[2048,256]{1,0:T(8,128)(2,1)}, u32[]{:S(2)}, u32[]{:S(2)}) collective-permute-start(bf16[2048,256]{1,0:T(8,128)(2,1)} %get-tuple-element.34.refs_3_.refs_4_), channel_id=1, source_target_pairs={{0,16},{4,12},{8,24},{12,4},{16,0},{20,28},{24,8},{28,20},{1,17},{... | collective-permute-start | bytes 3145736 | tf_op jit(solution)/shard_map/ppermute | solution.py:329
  32.7 28.5 %collective-permute-start.6 = (bf16[2048,256]{1,0:T(8,128)(2,1)}, bf16[2048,256]{1,0:T(8,128)(2,1)}, u32[]{:S(2)}, u32[]{:S(2)}) collective-permute-start(bf16[2048,256]{1,0:T(8,128)(2,1)} %get-tuple-element.35), channel_id=1, source_target_pairs={{1,0},{2,3},{5,4},{6,7},{9,8},{10,11},{13,12},{14,15},{17,16},{18,... | collective-permute-start | bytes 3145736 | tf_op jit(solution)/shard_map/ppermute | solution.py:323
  34.0 17.2 %collective-permute-start.7 = (f32[1024,128]{1,0:T(8,128)}, f32[1024,128]{1,0:T(8,128)}, u32[]{:S(2)}, u32[]{:S(2)}) collective-permute-start(f32[1024,128]{1,0:T(8,128)} %get-tuple-element.33.refs_3_.refs_1_.refs_2_), channel_id=1, source_target_pairs={{0,4},{4,0},{8,12},{12,8},{16,20},{20,16},{24,28},{28,24},{1,5},{5... | collective-permute-start | bytes 1572872 | tf_op jit(solution)/shard_map/ppermute | solution.py:332
  34.1 29.5 %collective-permute-start.10 = (bf16[2048,256]{1,0:T(8,128)(2,1)}, bf16[2048,256]{1,0:T(8,128)(2,1)}, u32[]{:S(2)}, u32[]{:S(2)}) collective-permute-start(bf16[2048,256]{1,0:T(8,128)(2,1)} %get-tuple-element.34.refs_3_.refs_4_), channel_id=1, source_target_pairs={{1,2},{2,1},{5,6},{6,5},{9,10},{10,9},{13,14},{14,13},{17,18},{18,... | collective-permute-start | bytes 3145736 | tf_op jit(solution)/shard_map/ppermute | solution.py:323
  63.5 28.4 %collective-permute-start.11 = (bf16[2048,256]{1,0:T(8,128)(2,1)}, bf16[2048,256]{1,0:T(8,128)(2,1)}, u32[]{:S(2)}, u32[]{:S(2)}) collective-permute-start(bf16[2048,256]{1,0:T(8,128)(2,1)} %shard_map.71.refs_7_), channel_id=1, source_target_pairs={{1,0},{2,3},{5,4},{6,7},{9,8},{10,11},{13,12},{14,15},{17,16},{18,... | collective-permute-start | bytes 3145736 | tf_op jit(solution)/shard_map/ppermute | solution.py:323
  65.0 26.9 %collective-permute-start.8 = (bf16[2048,256]{1,0:T(8,128)(2,1)}, bf16[2048,256]{1,0:T(8,128)(2,1)}, u32[]{:S(2)}, u32[]{:S(2)}) collective-permute-start(bf16[2048,256]{1,0:T(8,128)(2,1)} %broadcast_select_fusion.1.refs_1_.refs_4_), channel_id=1, source_target_pairs={{0,16},{4,12},{8,24},{12,4},{16,0},{20,28},{24,8},{28,20},{1,17},{... | collective-permute-start | bytes 3145736 | tf_op jit(solution)/shard_map/ppermute | solution.py:329
  65.6 26.3 %collective-permute-start.9 = (bf16[2048,256]{1,0:T(8,128)(2,1)}, bf16[2048,256]{1,0:T(8,128)(2,1)}, u32[]{:S(2)}, u32[]{:S(2)}) collective-permute-start(bf16[2048,256]{1,0:T(8,128)(2,1)} %broadcast_select_fusion.1.refs_1_.refs_4_), channel_id=1, source_target_pairs={{0,8},{4,20},{8,0},{12,28},{16,24},{20,4},{24,16},{28,12},{1,9},{5... | collective-permute-start | bytes 3145736 | tf_op jit(solution)/shard_map/ppermute | solution.py:326
  94.3 25.8 %collective-permute-start.15 = (bf16[2048,256]{1,0:T(8,128)(2,1)}, bf16[2048,256]{1,0:T(8,128)(2,1)}, u32[]{:S(2)}, u32[]{:S(2)}) collective-permute-start(bf16[2048,256]{1,0:T(8,128)(2,1)} %shard_map.74.refs_8_), channel_id=1, source_target_pairs={{0,1},{1,0},{2,3},{3,2},{4,5},{5,4},{6,7},{7,6},{8,9},{9,8},{10,11... | collective-permute-start | bytes 3145736 | tf_op jit(solution)/shard_map/ppermute | solution.py:323
  97.2 25.2 %collective-permute-start.14 = (bf16[2048,256]{1,0:T(8,128)(2,1)}, bf16[2048,256]{1,0:T(8,128)(2,1)}, u32[]{:S(2)}, u32[]{:S(2)}) collective-permute-start(bf16[2048,256]{1,0:T(8,128)(2,1)} %get-tuple-element.43.refs_6_), channel_id=1, source_target_pairs={{0,8},{4,20},{8,0},{12,28},{16,24},{20,4},{24,16},{28,12},{1,9},{5... | collective-permute-start | bytes 3145736 | tf_op jit(solution)/shard_map/ppermute | solution.py:326
  98.7 34.1 %collective-permute-start.12 = (bf16[2048,256]{1,0:T(8,128)(2,1)}, bf16[2048,256]{1,0:T(8,128)(2,1)}, u32[]{:S(2)}, u32[]{:S(2)}) collective-permute-start(bf16[2048,256]{1,0:T(8,128)(2,1)} %broadcast_select_fusion.refs_1_.refs_7_), channel_id=1, source_target_pairs={{0,16},{4,12},{8,24},{12,4},{16,0},{20,28},{24,8},{28,20},{1,17},{... | collective-permute-start | bytes 3145736 | tf_op jit(solution)/shard_map/ppermute | solution.py:329
  99.2 34.4 %collective-permute-start.13 = (bf16[2048,256]{1,0:T(8,128)(2,1)}, bf16[2048,256]{1,0:T(8,128)(2,1)}, u32[]{:S(2)}, u32[]{:S(2)}) collective-permute-start(bf16[2048,256]{1,0:T(8,128)(2,1)} %broadcast_select_fusion.refs_1_.refs_7_), channel_id=1, source_target_pairs={{0,8},{4,20},{8,0},{12,28},{16,24},{20,4},{24,16},{28,12},{1,9},{5... | collective-permute-start | bytes 3145736 | tf_op jit(solution)/shard_map/ppermute | solution.py:326
  133.6 15.1 %collective-permute-start.16 = (bf16[2048,256]{1,0:T(8,128)(2,1)}, bf16[2048,256]{1,0:T(8,128)(2,1)}, u32[]{:S(2)}, u32[]{:S(2)}) collective-permute-start(bf16[2048,256]{1,0:T(8,128)(2,1)} %get-tuple-element.52.refs_5_), channel_id=1, source_target_pairs={{0,8},{4,20},{8,0},{12,28},{16,24},{20,4},{24,16},{28,12},{1,9},{5... | collective-permute-start | bytes 3145736 | tf_op jit(solution)/shard_map/ppermute | solution.py:326
  135.4 10.5 %collective-permute-start.17 = (bf16[1024,256]{1,0:T(8,128)(2,1)}, bf16[1024,256]{1,0:T(8,128)(2,1)}, u32[]{:S(2)}, u32[]{:S(2)}) collective-permute-start(bf16[1024,256]{1,0:T(8,128)(2,1)} %get-tuple-element.53), channel_id=1, source_target_pairs={{0,4},{4,0},{8,12},{12,8},{16,20},{20,16},{24,28},{28,24},{1,5},{5... | collective-permute-start | bytes 1572872 | tf_op jit(solution)/shard_map/ppermute | solution.py:332
  135.4 10.5 %collective-permute-start.18 = (bf16[1024,256]{1,0:T(8,128)(2,1)}, bf16[1024,256]{1,0:T(8,128)(2,1)}, u32[]{:S(2)}, u32[]{:S(2)}) collective-permute-start(bf16[1024,256]{1,0:T(8,128)(2,1)} %get-tuple-element.54), channel_id=1, source_target_pairs={{0,4},{4,0},{8,12},{12,8},{16,20},{20,16},{24,28},{28,24},{1,5},{5... | collective-permute-start | bytes 1572872 | tf_op jit(solution)/shard_map/ppermute | solution.py:332
  148.8 3.8 %collective-permute-start.19 = (bf16[2048,256]{1,0:T(8,128)(2,1)}, bf16[2048,256]{1,0:T(8,128)(2,1)}, u32[]{:S(2)}, u32[]{:S(2)}) collective-permute-start(bf16[2048,256]{1,0:T(8,128)(2,1)} %shard_map.81.refs_2_), channel_id=1, source_target_pairs={{0,4},{4,0},{8,12},{12,8},{16,20},{20,16},{24,28},{28,24},{1,5},{5... | collective-permute-start | bytes 3145736 | tf_op jit(solution)/shard_map/ppermute | solution.py:332
  148.8 3.7 %collective-permute-start.20 = (bf16[1024,256]{1,0:T(8,128)(2,1)}, bf16[1024,256]{1,0:T(8,128)(2,1)}, u32[]{:S(2)}, u32[]{:S(2)}) collective-permute-start(bf16[1024,256]{1,0:T(8,128)(2,1)} %get-tuple-element.59), channel_id=1, source_target_pairs={{0,4},{4,0},{8,12},{12,8},{16,20},{20,16},{24,28},{28,24},{1,5},{5... | collective-permute-start | bytes 1572872 | tf_op jit(solution)/shard_map/ppermute | solution.py:332

commit v4 on v3

--- a/solution.py
+++ b/solution.py
@@ -356,31 +356,35 @@
     meta, extra = after([meta, extra], [own])
 
     p1, p2, other_t = after([p1, p2, other_t], [meta])
-    near1, p3, far1, p4 = by_near(p1), step(p2, outwards), by_far(p1), step(p1, middle)
+    p3, near1, far1, p4 = step(p2, outwards), by_near(p1), by_far(p1), step(p1, middle)
     other_meta = sib(meta)
     local = Group([(channel, interaction) for channel in range(channels)], column=own_column)
     ((out,),) = products(table, [t_pp], [meta], [local], [p1], result=shape)
 
-    near1, far1, p3, other_meta = after([near1, far1, p3, other_meta], [out])
+    (near1,) = after([near1], [out])
+    (p3,) = after([p3], [near1])
+    far1, other_meta = after([far1, other_meta], [p3])
+    (p4,) = after([p4], [far1])
+    p5 = step(p4, outwards)
     s2 = jnp.where(end, p3, p2)
     far2, near2 = by_far(s2), by_near(s2)
-    (p4,) = after([p4], [s2])
-    p5 = step(p4, outwards)
     t_rows = [t_pp, other_t]
     metas = [meta, other_meta]
-    (sum1,) = products(table, t_rows, metas, [Group([quarter(0, p1), quarter(1, near1), quarter(2, far1)])], [p4])
-
-    far2, near2, p5 = after([far2, near2, p5], [sum1[0]])
+    (sum1,) = products(table, t_rows, metas, [Group([quarter(0, p1), quarter(1, near1), quarter(2, far1)])], [s2])
+
+    (p5,) = after([p5], [sum1[0]])
+    (extra,) = after([extra], [p5])
+    e = step(extra, outer)
+    far2, near2 = after([far2, near2], [extra])
     across2 = by_near(far2)
     s3 = jnp.where(end, p5, p4)
-    (extra,) = after([extra], [s3])
-    far3, e, near3 = by_far(s3), step(extra, outer), by_near(s3)
+    far3, near3 = by_far(s3), by_near(s3)
     sum2, sum3 = products(
         table, t_rows, metas,
         [Group([quarter(0, s2), quarter(1, near2), quarter(2, far2)]), Group([quarter(0, s3)])],
-        [extra],
+        [s3],
     )
-    across2, e = after([across2, e], [sum2[0]])
+    e, across2 = after([e, across2], [sum2[0]])
     (out, rest1), (_, rest2) = products(
         table, t_rows, metas,
         [
@@ -397,7 +401,6 @@
         table, t_rows, metas, [Group([quarter(1, near3), quarter(2, far3)], before=sum3)], [near3]
     )
     back3 = sib(sum3[1])
-
     out = place(table, out, other_columns[:2], [back1, back2], [sum3[0]])
 
     (across3,) = after([across3], [out])

time: 161 us -> 156 us (0.969)
  starting transfers between devices: 25.8 us -> 22.2 us
  waiting for transfers between devices: 40.9 us -> 38.7 us
    ppermute x6, waiting for transfers between devices: 25.7 us -> 18.3 us  [step(): return lax.ppermute(x, axes, pairs)]
    ppermute x5, waiting for transfers between devices: 7.95 us -> 12 us  [by_near(): return lax.ppermute(x, 'chan', near_pairs)]
    ppermute x6, starting transfers between devices: 11.7 us -> 8.68 us  [step(): return lax.ppermute(x, axes, pairs)]
  transfers between devices with their start and end apart: 22 -> 22, of which waited for: 10 -> 10; matrix products, arithmetic and copies ran while one was open for 9% -> 11% of each run, Pallas kernels for 41% -> 43%
where the time goes in v4:
time: 156 us; the launch traced here: 154 us
  Pallas kernels  73.2 us (47%)
  waiting for transfers between devices  38.7 us (25%)
  starting transfers between devices  22.2 us (14%)
  other arithmetic  9.59 us (6%)
  local copies, waits for them, and re-layouts  8.37 us (5%)
  between operations  2.07 us (1%)
    pallas_call x6, Pallas kernels, products(): pl.pallas_call(functools.partial(products_body, plan), in_specs=[IN_SMEM]...  70.5 us
    ppermute x6, waiting for transfers between devices, step(): return lax.ppermute(x, axes, pairs)  18.3 us
    ppermute x5, waiting for transfers between devices, by_near(): return lax.ppermute(x, 'chan', near_pairs)  12 us
    ppermute x6, starting transfers between devices, step(): return lax.ppermute(x, axes, pairs)  8.68 us
    ppermute x5, starting transfers between devices, by_near(): return lax.ppermute(x, 'chan', near_pairs)  5.69 us
    reshape x2, local copies, waits for them, and re-layouts, own_rows(): return rows.reshape(depth, part)  4.58 us
    all_to_all x1, waiting for transfers between devices, meta_over(): return lax.all_to_all(back, 'chan', split_axis=0, concat_axis=0, tiled=True)  4.05 us
    all_to_all x1, starting transfers between devices, meta_over(): return lax.all_to_all(back, 'chan', split_axis=0, concat_axis=0, tiled=True)  3.72 us
  transfers between devices with their start and end apart: 22, of which 10 were waited for; matrix products, arithmetic and copies ran while one was open for 11% of the time, Pallas kernels for 43%

profile of v4, /device:TPU:0, one launch (start us, length us, event | category | flops | bytes accessed | tf_op | source)
XLA Modules:
  0.0 154.1 jit_solution(8353582251052388728)
XLA Ops:
  0.0 0.5 collective-permute-start.3
  0.5 2.3 %dynamic-slice_bitcast_fusion.1.refs_0_ = bf16[2048,256]{1,0:T(8,128)(2,1)} fusion(bf16[4,2048,512]{2,1,0:T(8,128)(2,1)} %refs_2_.1, s32[]{:T(128)S(6)} %select_n.72, s32[]{:T(128)S(6)} %select_n.73), kind=kLoop, calls=%fused_computation.7 | loop fusion | bytes 2097160 | tf_op jit(solution)/shard_map/reshape | solution.py:347
  2.7 2.6 %collective-permute-start.1 = (bf16[2048,256]{1,0:T(8,128)(2,1)}, bf16[2048,256]{1,0:T(8,128)(2,1)}, u32[]{:S(2)}, u32[]{:S(2)}) collective-permute-start(bf16[2048,256]{1,0:T(8,128)(2,1)} %shard_map.64.refs_2_), channel_id=1, source_target_pairs={{0,1},{1,0},{2,3},{3,2},{4,5},{5,4},{6,7},{7,6},{8,9},{9,8},{10,11... | collective-permute-start | bytes 3145736 | tf_op jit(solution)/shard_map/ppermute | solution.py:323
  5.3 1.6 %collective-permute-start.2 = (bf16[2048,256]{1,0:T(8,128)(2,1)}, bf16[2048,256]{1,0:T(8,128)(2,1)}, u32[]{:S(2)}, u32[]{:S(2)}) collective-permute-start(bf16[2048,256]{1,0:T(8,128)(2,1)} %shard_map.64.refs_2_), channel_id=1, source_target_pairs={{1,2},{2,1},{5,6},{6,5},{9,10},{10,9},{13,14},{14,13},{17,18},{18,... | collective-permute-start | bytes 3145736 | tf_op jit(solution)/shard_map/ppermute | solution.py:323
  7.0 0.7 slice.18
  7.7 0.2 collective-permute-start
  7.9 0.7 dynamic_slice.13
  8.5 0.7 dynamic-slice_convert_fusion
  9.2 1.2 select_reduce_fusion.3
  10.5 0.6 maximum_bitcast_fusion.refs_0_
  11.1 0.0 collective-permute-done.refs_1_
  11.1 0.6 copy-done.1
  11.7 3.7 %all-to-all-start = ((f32[8,2,128]{2,1,0:T(2,128)}), f32[8,2,128]{2,1,0:T(2,128)S(1)}, u32[]{:S(2)}, u32[]{:S(2)}) async-start(f32[8,2,128]{2,1,0:T(2,128)} %shard_map.65), calls=%async_computation | async-start | bytes 16384 | tf_op jit(solution)/shard_map/all_to_all | solution.py:271
  15.4 0.1 stack.56.scalars.table_ref
  15.5 0.5 copy.34.refs_0_
  16.1 4.1 %all-to-all-done = f32[8,2,128]{2,1,0:T(2,128)S(1)} async-done(((f32[8,2,128]{2,1,0:T(2,128)}), f32[8,2,128]{2,1,0:T(2,128)S(1)}, u32[]{:S(2)}, u32[]{:S(2)}) %all-to-all-start) | async-done | bytes 8224 | tf_op jit(solution)/shard_map/all_to_all | solution.py:271
  20.1 1.2 select_reduce_fusion.1
  21.4 1.2 select_select_fusion.refs_1_.refs_0_
  22.5 1.2 slice.17
  25.4 2.3 %dynamic-slice_bitcast_fusion.refs_1_ = bf16[2048,256]{1,0:T(8,128)(2,1)} fusion(bf16[4,2048,512]{2,1,0:T(8,128)(2,1)} %refs_2_.1, s32[]{:T(128)S(6)} %select_n.78, s32[]{:T(128)S(6)} %select_n.73), kind=kLoop, calls=%fused_computation.6 | loop fusion | bytes 2097160 | tf_op jit(solution)/shard_map/reshape | solution.py:347
  27.7 1.7 %collective-permute-done.1.refs_0_ = bf16[2048,256]{1,0:T(8,128)(2,1)} collective-permute-done((bf16[2048,256]{1,0:T(8,128)(2,1)}, bf16[2048,256]{1,0:T(8,128)(2,1)}, u32[]{:S(2)}, u32[]{:S(2)}) %collective-permute-start.1) | collective-permute-done | bytes 1048608 | tf_op jit(solution)/shard_map/ppermute | solution.py:323
  29.4 0.0 collective-permute-done.2.refs_1_
  29.4 0.0 collective-permute-done.3.refs_2_
  29.5 1.7 %collective-permute-start.8 = (bf16[2048,256]{1,0:T(8,128)(2,1)}, bf16[2048,256]{1,0:T(8,128)(2,1)}, u32[]{:S(2)}, u32[]{:S(2)}) collective-permute-start(bf16[2048,256]{1,0:T(8,128)(2,1)} %get-tuple-element.31.refs_3_.refs_4_), channel_id=1, source_target_pairs={{0,8},{4,20},{8,0},{12,28},{16,24},{20,4},{24,16},{28,12},{1,9},{5... | collective-permute-start | bytes 3145736 | tf_op jit(solution)/shard_map/ppermute | solution.py:326
  31.2 1.3 collective-permute-start.7
  32.5 1.6 %collective-permute-start.5 = (bf16[2048,256]{1,0:T(8,128)(2,1)}, bf16[2048,256]{1,0:T(8,128)(2,1)}, u32[]{:S(2)}, u32[]{:S(2)}) collective-permute-start(bf16[2048,256]{1,0:T(8,128)(2,1)} %get-tuple-element.31.refs_3_.refs_4_), channel_id=1, source_target_pairs={{0,16},{4,12},{8,24},{12,4},{16,0},{20,28},{24,8},{28,20},{1,17},{... | collective-permute-start | bytes 3145736 | tf_op jit(solution)/shard_map/ppermute | solution.py:329
  34.0 1.7 %collective-permute-start.4 = (bf16[2048,256]{1,0:T(8,128)(2,1)}, bf16[2048,256]{1,0:T(8,128)(2,1)}, u32[]{:S(2)}, u32[]{:S(2)}) collective-permute-start(bf16[2048,256]{1,0:T(8,128)(2,1)} %get-tuple-element.31.refs_3_.refs_4_), channel_id=1, source_target_pairs={{1,2},{2,1},{5,6},{6,5},{9,10},{10,9},{13,14},{14,13},{17,18},{18,... | collective-permute-start | bytes 3145736 | tf_op jit(solution)/shard_map/ppermute | solution.py:323
  35.7 0.0 collective-permute-start.6
  35.7 15.3 %shard_map.69.refs_1_.refs_10_ = bf16[1024,2048]{1,0:T(8,128)(2,1)} custom-call(s32[11]{0:T(128)} %copy-done, bf16[1024,2048]{1,0:T(8,128)(2,1)} %refs_0_.11, f32[1024,128]{1,0:T(8,128)} %get-tuple-element.30.refs_3_.refs_1_.refs_2_, bf16[4,2048,512]{2,1,0:T(8,128)(2,1)} %refs_2_.1, bf16[2048,256]{1,0:T(8,128)(2,1)} %get-tuple-element.31.refs_3_.refs_4_), custom_call_target="tpu_custom_call" | custom-call | flops 1 | bytes 1 | tf_op jit(solution)/shard_map/pallas_call | solution.py:188
  51.1 3.3 %collective-permute-done.8.refs_0_ = bf16[2048,256]{1,0:T(8,128)(2,1)} collective-permute-done((bf16[2048,256]{1,0:T(8,128)(2,1)}, bf16[2048,256]{1,0:T(8,128)(2,1)}, u32[]{:S(2)}, u32[]{:S(2)}) %collective-permute-start.8) | collective-permute-done | bytes 1048608 | tf_op jit(solution)/shard_map/ppermute | solution.py:326
  54.3 5.7 %collective-permute-done.7.refs_0_ = bf16[2048,256]{1,0:T(8,128)(2,1)} collective-permute-done((bf16[2048,256]{1,0:T(8,128)(2,1)}, bf16[2048,256]{1,0:T(8,128)(2,1)}, u32[]{:S(2)}, u32[]{:S(2)}) %collective-permute-start.7) | collective-permute-done | bytes 1048608 | tf_op jit(solution)/shard_map/ppermute | solution.py:323
  60.0 0.0 collective-permute-done.6.refs_1_
  60.0 0.0 collective-permute-done.5.refs_0_
  60.0 0.0 collective-permute-done.4.refs_0_
  60.1 1.5 collective-permute-start.9
  61.5 2.3 %broadcast_select_fusion.1.refs_7_.refs_4_ = bf16[2048,256]{1,0:T(8,128)(2,1)} fusion(bf16[2048,256]{1,0:T(8,128)(2,1)} %shard_map.71.refs_2_, bf16[2048,256]{1,0:T(8,128)(2,1)} %get-tuple-element.32, pred[]{:T(512)S(6)} %or.3), kind=kLoop, calls=%fused_computation.9 | loop fusion | flops 524288 | bytes 3145729 | tf_op jit(solution)/shard_map/jit(_where)/select_n | solution.py:369
  63.8 0.5 collective-permute-start.13
  64.4 1.5 collective-permute-start.14
  65.8 12.3 %shard_map.74 = (bf16[1024,256]{1,0:T(8,128)(2,1)}, bf16[1024,256]{1,0:T(8,128)(2,1)}) custom-call(s32[11]{0:T(128)} %copy-done, bf16[1024,2048]{1,0:T(8,128)(2,1)} %refs_0_.11, bf16[1024,2048]{1,0:T(8,128)(2,1)} %get-tuple-element.34.refs_1_, f32[1024,128]{1,0:T(8,128)} %get-tuple-element.30.refs_3_.refs_1_.refs_2_, f32[1024,128]{1,0:T(8,128)} %get-tuple-element.35.refs_3_, ...), custom_call_target="tpu_custom_call" | custom-call | flops 1 | bytes 1 | tf_op jit(solution)/shard_map/pallas_call | solution.py:188
  78.1 10.9 %collective-permute-done.9.refs_0_ = bf16[2048,256]{1,0:T(8,128)(2,1)} collective-permute-done((bf16[2048,256]{1,0:T(8,128)(2,1)}, bf16[2048,256]{1,0:T(8,128)(2,1)}, u32[]{:S(2)}, u32[]{:S(2)}) %collective-permute-start.9) | collective-permute-done | bytes 1048608 | tf_op jit(solution)/shard_map/ppermute | solution.py:323
  89.0 0.0 collective-permute-start.12
  89.0 1.2 collective-permute-done.13.refs_0_
  90.2 0.0 collective-permute-done.14.refs_1_
  90.2 0.4 collective-permute-start.15
  90.5 2.3 %broadcast_select_fusion.refs_7_.refs_8_ = bf16[2048,256]{1,0:T(8,128)(2,1)} fusion(bf16[2048,256]{1,0:T(8,128)(2,1)} %shard_map.75.refs_1_, bf16[2048,256]{1,0:T(8,128)(2,1)} %shard_map.73, pred[]{:T(512)S(6)} %or.3), kind=kLoop, calls=%fused_computation.8 | loop fusion | flops 524288 | bytes 3145729 | tf_op jit(solution)/shard_map/jit(_where)/select_n | solution.py:380
  92.9 0.3 collective-permute-start.10
  93.2 1.7 %collective-permute-start.11 = (bf16[2048,256]{1,0:T(8,128)(2,1)}, bf16[2048,256]{1,0:T(8,128)(2,1)}, u32[]{:S(2)}, u32[]{:S(2)}) collective-permute-start(bf16[2048,256]{1,0:T(8,128)(2,1)} %broadcast_select_fusion.refs_7_.refs_8_), channel_id=1, source_target_pairs={{0,8},{4,20},{8,0},{12,28},{16,24},{20,4},{24,16},{28,12},{1,9},{5... | collective-permute-start | bytes 3145736 | tf_op jit(solution)/shard_map/ppermute | solution.py:326
  94.9 15.2 %shard_map.78 = (bf16[1024,256]{1,0:T(8,128)(2,1)}, bf16[1024,256]{1,0:T(8,128)(2,1)}, bf16[1024,256]{1,0:T(8,128)(2,1)}, bf16[1024,256]{1,0:T(8,128)(2,1)}) custom-call(s32[11]{0:T(128)} %copy-done, bf16[1024,2048]{1,0:T(8,128)(2,1)} %refs_0_.11, bf16[1024,2048]{1,0:T(8,128)(2,1)} %get-tuple-element.34.refs_1_, ...), custom_call_target="tpu_custom_call" | custom-call | flops 1 | bytes 1 | tf_op jit(solution)/shard_map/pallas_call | solution.py:188
  110.1 4.8 %collective-permute-done.15.refs_1_ = bf16[2048,256]{1,0:T(8,128)(2,1)} collective-permute-done((bf16[2048,256]{1,0:T(8,128)(2,1)}, bf16[2048,256]{1,0:T(8,128)(2,1)}, u32[]{:S(2)}, u32[]{:S(2)}) %collective-permute-start.15) | collective-permute-done | bytes 1048608 | tf_op jit(solution)/shard_map/ppermute | solution.py:326
  115.0 0.0 collective-permute-done.12.refs_0_
  115.0 10.5 %shard_map.80 = (bf16[1024,2048]{1,0:T(8,128)(2,1)}, bf16[1024,256]{1,0:T(8,128)(2,1)}, bf16[16,256]{1,0:T(8,128)(2,1)}, bf16[1024,256]{1,0:T(8,128)(2,1)}) custom-call(s32[11]{0:T(128)} %copy-done, bf16[1024,2048]{1,0:T(8,128)(2,1)} %refs_0_.11, bf16[1024,2048]{1,0:T(8,128)(2,1)} %get-tuple-element.34.refs_1_, ...), custom_call_target="tpu_custom_call", output_to_operand_aliasing={{0}: (11, {})} | custom-call | flops 1 | bytes 1 | tf_op jit(solution)/shard_map/pallas_call | solution.py:188
  125.4 0.0 collective-permute-done.10.refs_0_
  125.4 2.3 %collective-permute-done.11.refs_1_ = bf16[2048,256]{1,0:T(8,128)(2,1)} collective-permute-done((bf16[2048,256]{1,0:T(8,128)(2,1)}, bf16[2048,256]{1,0:T(8,128)(2,1)}, u32[]{:S(2)}, u32[]{:S(2)}) %collective-permute-start.11) | collective-permute-done | bytes 1048608 | tf_op jit(solution)/shard_map/ppermute | solution.py:326
  127.7 0.4 collective-permute-start.16
  128.1 0.0 collective-permute-start.17
  128.1 0.5 collective-permute-start.18
  128.6 9.9 %shard_map.82 = (bf16[1024,256]{1,0:T(8,128)(2,1)}, bf16[1024,256]{1,0:T(8,128)(2,1)}) custom-call(s32[11]{0:T(128)} %copy-done, bf16[1024,2048]{1,0:T(8,128)(2,1)} %refs_0_.11, bf16[1024,2048]{1,0:T(8,128)(2,1)} %get-tuple-element.34.refs_1_, f32[1024,128]{1,0:T(8,128)} %get-tuple-element.30.refs_3_.refs_1_.refs_2_, f32[1024,128]{1,0:T(8,128)} %get-tuple-element.35.refs_3_, ...), custom_call_target="tpu_custom_call" | custom-call | flops 1 | bytes 1 | tf_op jit(solution)/shard_map/pallas_call | solution.py:188
  138.6 0.0 collective-permute-done.17.refs_0_
  138.6 0.0 collective-permute-done.18.refs_1_
  138.6 2.6 %shard_map.83.refs_1_.refs_6_ = bf16[1024,2048]{1,0:T(8,128)(2,1)} custom-call(s32[11]{0:T(128)} %copy-done, bf16[1024,256]{1,0:T(8,128)(2,1)} %collective-permute-done.17.refs_0_, bf16[1024,256]{1,0:T(8,128)(2,1)} %collective-permute-done.18.refs_1_, bf16[1024,2048]{1,0:T(8,128)(2,1)} %get-tuple-element.45.refs_2_, ...), custom_call_target="tpu_custom_call", output_to_operand_aliasing={{}: (3, {})} | custom-call | flops 1 | bytes 1 | tf_op jit(solution)/shard_map/pallas_call | solution.py:238
  141.3 1.6 %collective-permute-done.16.refs_0_ = bf16[2048,256]{1,0:T(8,128)(2,1)} collective-permute-done((bf16[2048,256]{1,0:T(8,128)(2,1)}, bf16[2048,256]{1,0:T(8,128)(2,1)}, u32[]{:S(2)}, u32[]{:S(2)}) %collective-permute-start.16) | collective-permute-done | bytes 1048608 | tf_op jit(solution)/shard_map/ppermute | solution.py:326
  142.9 0.5 collective-permute-start.20
  143.4 3.2 %collective-permute-done.20.refs_5_ = bf16[1024,256]{1,0:T(8,128)(2,1)} collective-permute-done((bf16[1024,256]{1,0:T(8,128)(2,1)}, bf16[1024,256]{1,0:T(8,128)(2,1)}, u32[]{:S(2)}, u32[]{:S(2)}) %collective-permute-start.20) | collective-permute-done | bytes 524320 | tf_op jit(solution)/shard_map/ppermute | solution.py:332
  146.6 7.3 %shard_map.85 = (bf16[1024,2048]{1,0:T(8,128)(2,1)}, bf16[16,256]{1,0:T(8,128)(2,1)}) custom-call(s32[11]{0:T(128)} %copy-done, bf16[1024,2048]{1,0:T(8,128)(2,1)} %refs_0_.11, f32[1024,128]{1,0:T(8,128)} %get-tuple-element.30.refs_3_.refs_1_.refs_2_, bf16[2048,256]{1,0:T(8,128)(2,1)} %shard_map.84.refs_2_, ...), custom_call_target="tpu_custom_call", output_to_operand_aliasing={{0}: (7, {})} | custom-call | flops 1 | bytes 1 | tf_op jit(solution)/shard_map/pallas_call | solution.py:188
  (26 shorter events, 0.0 us)
Async XLA Ops:
  0.0 9.2 %copy-start.2 = (s32[1024]{0:T(1024)S(1)}, s32[1024]{0:T(1024)}, u32[]{:S(2)}) copy-start(s32[1024]{0:T(1024)} %param.9) | copy-start | bytes 12292
  0.0 20.1 %copy-start.3 = (s32[1024]{0:T(1024)S(1)}, s32[1024]{0:T(1024)}, u32[]{:S(2)}) copy-start(s32[1024]{0:T(1024)} %param.8) | copy-start | bytes 12292
  0.0 29.4 %collective-permute-start.3 = (bf16[1024,2048]{1,0:T(8,128)(2,1)}, bf16[1024,2048]{1,0:T(8,128)(2,1)}, u32[]{:S(2)}, u32[]{:S(2)}) collective-permute-start(bf16[1024,2048]{1,0:T(8,128)(2,1)} %refs_0_.11), channel_id=1, source_target_pairs={{0,4},{4,0},{8,12},{12,8},{16,20},{20,16},{24,28},{28,24},{1,5},{5... | collective-permute-start | bytes 12582920 | tf_op jit(solution)/shard_map/ppermute | solution.py:332
  2.7 26.7 %collective-permute-start.1 = (bf16[2048,256]{1,0:T(8,128)(2,1)}, bf16[2048,256]{1,0:T(8,128)(2,1)}, u32[]{:S(2)}, u32[]{:S(2)}) collective-permute-start(bf16[2048,256]{1,0:T(8,128)(2,1)} %shard_map.64.refs_2_), channel_id=1, source_target_pairs={{0,1},{1,0},{2,3},{3,2},{4,5},{5,4},{6,7},{7,6},{8,9},{9,8},{10,11... | collective-permute-start | bytes 3145736 | tf_op jit(solution)/shard_map/ppermute | solution.py:323
  5.3 24.1 %collective-permute-start.2 = (bf16[2048,256]{1,0:T(8,128)(2,1)}, bf16[2048,256]{1,0:T(8,128)(2,1)}, u32[]{:S(2)}, u32[]{:S(2)}) collective-permute-start(bf16[2048,256]{1,0:T(8,128)(2,1)} %shard_map.64.refs_2_), channel_id=1, source_target_pairs={{1,2},{2,1},{5,6},{6,5},{9,10},{10,9},{13,14},{14,13},{17,18},{18,... | collective-permute-start | bytes 3145736 | tf_op jit(solution)/shard_map/ppermute | solution.py:323
  7.7 3.4 %collective-permute-start = (bf16[16,256]{1,0:T(8,128)(2,1)S(1)}, bf16[16,256]{1,0:T(8,128)(2,1)S(1)}, u32[]{:S(2)}, u32[]{:S(2)}) collective-permute-start(bf16[16,256]{1,0:T(8,128)(2,1)S(1)} %slice.18), channel_id=1, source_target_pairs={{0,4},{4,0},{8,12},{12,8},{16,20},{20,16},{24,28},{28,24},{1,5},{5... | collective-permute-start | bytes 24584 | tf_op jit(solution)/shard_map/ppermute | solution.py:332
  11.1 0.6 copy-start.1
  11.7 8.4 %all-to-all-start = ((f32[8,2,128]{2,1,0:T(2,128)}), f32[8,2,128]{2,1,0:T(2,128)S(1)}, u32[]{:S(2)}, u32[]{:S(2)}) async-start(f32[8,2,128]{2,1,0:T(2,128)} %shard_map.65), calls=%async_computation | async-start | bytes 16384 | tf_op jit(solution)/shard_map/all_to_all | solution.py:271
  15.5 13.9 %copy-start = (s32[11]{0:T(128)}, s32[11]{0:T(128)S(1)}, u32[]{:S(2)}) copy-start(s32[11]{0:T(128)S(1)} %stack.56.scalars.table_ref) | copy-start | bytes 136
  29.5 24.9 %collective-permute-start.8 = (bf16[2048,256]{1,0:T(8,128)(2,1)}, bf16[2048,256]{1,0:T(8,128)(2,1)}, u32[]{:S(2)}, u32[]{:S(2)}) collective-permute-start(bf16[2048,256]{1,0:T(8,128)(2,1)} %get-tuple-element.31.refs_3_.refs_4_), channel_id=1, source_target_pairs={{0,8},{4,20},{8,0},{12,28},{16,24},{20,4},{24,16},{28,12},{1,9},{5... | collective-permute-start | bytes 3145736 | tf_op jit(solution)/shard_map/ppermute | solution.py:326
  31.2 28.9 %collective-permute-start.7 = (bf16[2048,256]{1,0:T(8,128)(2,1)}, bf16[2048,256]{1,0:T(8,128)(2,1)}, u32[]{:S(2)}, u32[]{:S(2)}) collective-permute-start(bf16[2048,256]{1,0:T(8,128)(2,1)} %get-tuple-element.32), channel_id=1, source_target_pairs={{1,0},{2,3},{5,4},{6,7},{9,8},{10,11},{13,12},{14,15},{17,16},{18,... | collective-permute-start | bytes 3145736 | tf_op jit(solution)/shard_map/ppermute | solution.py:323
  32.5 27.6 %collective-permute-start.5 = (bf16[2048,256]{1,0:T(8,128)(2,1)}, bf16[2048,256]{1,0:T(8,128)(2,1)}, u32[]{:S(2)}, u32[]{:S(2)}) collective-permute-start(bf16[2048,256]{1,0:T(8,128)(2,1)} %get-tuple-element.31.refs_3_.refs_4_), channel_id=1, source_target_pairs={{0,16},{4,12},{8,24},{12,4},{16,0},{20,28},{24,8},{28,20},{1,17},{... | collective-permute-start | bytes 3145736 | tf_op jit(solution)/shard_map/ppermute | solution.py:329
  34.0 26.0 %collective-permute-start.4 = (bf16[2048,256]{1,0:T(8,128)(2,1)}, bf16[2048,256]{1,0:T(8,128)(2,1)}, u32[]{:S(2)}, u32[]{:S(2)}) collective-permute-start(bf16[2048,256]{1,0:T(8,128)(2,1)} %get-tuple-element.31.refs_3_.refs_4_), channel_id=1, source_target_pairs={{1,2},{2,1},{5,6},{6,5},{9,10},{10,9},{13,14},{14,13},{17,18},{18,... | collective-permute-start | bytes 3145736 | tf_op jit(solution)/shard_map/ppermute | solution.py:323
  35.7 24.3 %collective-permute-start.6 = (f32[1024,128]{1,0:T(8,128)}, f32[1024,128]{1,0:T(8,128)}, u32[]{:S(2)}, u32[]{:S(2)}) collective-permute-start(f32[1024,128]{1,0:T(8,128)} %get-tuple-element.30.refs_3_.refs_1_.refs_2_), channel_id=1, source_target_pairs={{0,4},{4,0},{8,12},{12,8},{16,20},{20,16},{24,28},{28,24},{1,5},{5... | collective-permute-start | bytes 1572872 | tf_op jit(solution)/shard_map/ppermute | solution.py:332
  60.1 28.9 %collective-permute-start.9 = (bf16[2048,256]{1,0:T(8,128)(2,1)}, bf16[2048,256]{1,0:T(8,128)(2,1)}, u32[]{:S(2)}, u32[]{:S(2)}) collective-permute-start(bf16[2048,256]{1,0:T(8,128)(2,1)} %shard_map.73), channel_id=1, source_target_pairs={{1,0},{2,3},{5,4},{6,7},{9,8},{10,11},{13,12},{14,15},{17,16},{18,... | collective-permute-start | bytes 3145736 | tf_op jit(solution)/shard_map/ppermute | solution.py:323
  63.8 26.3 %collective-permute-start.13 = (bf16[2048,256]{1,0:T(8,128)(2,1)}, bf16[2048,256]{1,0:T(8,128)(2,1)}, u32[]{:S(2)}, u32[]{:S(2)}) collective-permute-start(bf16[2048,256]{1,0:T(8,128)(2,1)} %broadcast_select_fusion.1.refs_7_.refs_4_), channel_id=1, source_target_pairs={{0,16},{4,12},{8,24},{12,4},{16,0},{20,28},{24,8},{28,20},{1,17},{... | collective-permute-start | bytes 3145736 | tf_op jit(solution)/shard_map/ppermute | solution.py:329
  64.4 25.8 %collective-permute-start.14 = (bf16[2048,256]{1,0:T(8,128)(2,1)}, bf16[2048,256]{1,0:T(8,128)(2,1)}, u32[]{:S(2)}, u32[]{:S(2)}) collective-permute-start(bf16[2048,256]{1,0:T(8,128)(2,1)} %broadcast_select_fusion.1.refs_7_.refs_4_), channel_id=1, source_target_pairs={{0,8},{4,20},{8,0},{12,28},{16,24},{20,4},{24,16},{28,12},{1,9},{5... | collective-permute-start | bytes 3145736 | tf_op jit(solution)/shard_map/ppermute | solution.py:326
  89.0 26.0 %collective-permute-start.12 = (bf16[2048,256]{1,0:T(8,128)(2,1)}, bf16[2048,256]{1,0:T(8,128)(2,1)}, u32[]{:S(2)}, u32[]{:S(2)}) collective-permute-start(bf16[2048,256]{1,0:T(8,128)(2,1)} %shard_map.76.refs_2_), channel_id=1, source_target_pairs={{0,1},{1,0},{2,3},{3,2},{4,5},{5,4},{6,7},{7,6},{8,9},{9,8},{10,11... | collective-permute-start | bytes 3145736 | tf_op jit(solution)/shard_map/ppermute | solution.py:323
  90.2 24.8 %collective-permute-start.15 = (bf16[2048,256]{1,0:T(8,128)(2,1)}, bf16[2048,256]{1,0:T(8,128)(2,1)}, u32[]{:S(2)}, u32[]{:S(2)}) collective-permute-start(bf16[2048,256]{1,0:T(8,128)(2,1)} %get-tuple-element.38.refs_6_), channel_id=1, source_target_pairs={{0,8},{4,20},{8,0},{12,28},{16,24},{20,4},{24,16},{28,12},{1,9},{5... | collective-permute-start | bytes 3145736 | tf_op jit(solution)/shard_map/ppermute | solution.py:326
  92.9 32.6 %collective-permute-start.10 = (bf16[2048,256]{1,0:T(8,128)(2,1)}, bf16[2048,256]{1,0:T(8,128)(2,1)}, u32[]{:S(2)}, u32[]{:S(2)}) collective-permute-start(bf16[2048,256]{1,0:T(8,128)(2,1)} %broadcast_select_fusion.refs_7_.refs_8_), channel_id=1, source_target_pairs={{0,16},{4,12},{8,24},{12,4},{16,0},{20,28},{24,8},{28,20},{1,17},{... | collective-permute-start | bytes 3145736 | tf_op jit(solution)/shard_map/ppermute | solution.py:329
  93.2 34.6 %collective-permute-start.11 = (bf16[2048,256]{1,0:T(8,128)(2,1)}, bf16[2048,256]{1,0:T(8,128)(2,1)}, u32[]{:S(2)}, u32[]{:S(2)}) collective-permute-start(bf16[2048,256]{1,0:T(8,128)(2,1)} %broadcast_select_fusion.refs_7_.refs_8_), channel_id=1, source_target_pairs={{0,8},{4,20},{8,0},{12,28},{16,24},{20,4},{24,16},{28,12},{1,9},{5... | collective-permute-start | bytes 3145736 | tf_op jit(solution)/shard_map/ppermute | solution.py:326
  127.7 15.1 %collective-permute-start.16 = (bf16[2048,256]{1,0:T(8,128)(2,1)}, bf16[2048,256]{1,0:T(8,128)(2,1)}, u32[]{:S(2)}, u32[]{:S(2)}) collective-permute-start(bf16[2048,256]{1,0:T(8,128)(2,1)} %get-tuple-element.46.refs_5_), channel_id=1, source_target_pairs={{0,8},{4,20},{8,0},{12,28},{16,24},{20,4},{24,16},{28,12},{1,9},{5... | collective-permute-start | bytes 3145736 | tf_op jit(solution)/shard_map/ppermute | solution.py:326
  128.1 10.5 %collective-permute-start.17 = (bf16[1024,256]{1,0:T(8,128)(2,1)}, bf16[1024,256]{1,0:T(8,128)(2,1)}, u32[]{:S(2)}, u32[]{:S(2)}) collective-permute-start(bf16[1024,256]{1,0:T(8,128)(2,1)} %get-tuple-element.47), channel_id=1, source_target_pairs={{0,4},{4,0},{8,12},{12,8},{16,20},{20,16},{24,28},{28,24},{1,5},{5... | collective-permute-start | bytes 1572872 | tf_op jit(solution)/shard_map/ppermute | solution.py:332
  128.1 10.5 %collective-permute-start.18 = (bf16[1024,256]{1,0:T(8,128)(2,1)}, bf16[1024,256]{1,0:T(8,128)(2,1)}, u32[]{:S(2)}, u32[]{:S(2)}) collective-permute-start(bf16[1024,256]{1,0:T(8,128)(2,1)} %get-tuple-element.48), channel_id=1, source_target_pairs={{0,4},{4,0},{8,12},{12,8},{16,20},{20,16},{24,28},{28,24},{1,5},{5... | collective-permute-start | bytes 1572872 | tf_op jit(solution)/shard_map/ppermute | solution.py:332
  142.9 3.8 %collective-permute-start.19 = (bf16[2048,256]{1,0:T(8,128)(2,1)}, bf16[2048,256]{1,0:T(8,128)(2,1)}, u32[]{:S(2)}, u32[]{:S(2)}) collective-permute-start(bf16[2048,256]{1,0:T(8,128)(2,1)} %shard_map.84.refs_2_), channel_id=1, source_target_pairs={{0,4},{4,0},{8,12},{12,8},{16,20},{20,16},{24,28},{28,24},{1,5},{5... | collective-permute-start | bytes 3145736 | tf_op jit(solution)/shard_map/ppermute | solution.py:332
  142.9 3.7 %collective-permute-start.20 = (bf16[1024,256]{1,0:T(8,128)(2,1)}, bf16[1024,256]{1,0:T(8,128)(2,1)}, u32[]{:S(2)}, u32[]{:S(2)}) collective-permute-start(bf16[1024,256]{1,0:T(8,128)(2,1)} %get-tuple-element.53), channel_id=1, source_target_pairs={{0,4},{4,0},{8,12},{12,8},{16,20},{20,16},{24,28},{28,24},{1,5},{5... | collective-permute-start | bytes 1572872 | tf_op jit(solution)/shard_map/ppermute | solution.py:332

commit v5 on v4

--- a/solution.py
+++ b/solution.py
@@ -355,28 +355,29 @@
     extra = own_rows(later[3])
     meta, extra = after([meta, extra], [own])
 
-    p1, p2, other_t = after([p1, p2, other_t], [meta])
+    (p1,) = after([p1], [meta])
+    p2, other_t = after([p2, other_t], [p1])
     p3, near1, far1, p4 = step(p2, outwards), by_near(p1), by_far(p1), step(p1, middle)
     other_meta = sib(meta)
     local = Group([(channel, interaction) for channel in range(channels)], column=own_column)
     ((out,),) = products(table, [t_pp], [meta], [local], [p1], result=shape)
 
     (near1,) = after([near1], [out])
-    (p3,) = after([p3], [near1])
-    far1, other_meta = after([far1, other_meta], [p3])
-    (p4,) = after([p4], [far1])
-    p5 = step(p4, outwards)
+    far1, other_meta = after([far1, other_meta], [near1])
+    (p3,) = after([p3], [far1])
     s2 = jnp.where(end, p3, p2)
     far2, near2 = by_far(s2), by_near(s2)
+    (p4,) = after([p4], [s2])
+    p5 = step(p4, outwards)
     t_rows = [t_pp, other_t]
     metas = [meta, other_meta]
-    (sum1,) = products(table, t_rows, metas, [Group([quarter(0, p1), quarter(1, near1), quarter(2, far1)])], [s2])
-
-    (p5,) = after([p5], [sum1[0]])
+    (sum1,) = products(table, t_rows, metas, [Group([quarter(0, p1), quarter(1, near1), quarter(2, far1)])], [p4])
+
+    far2, near2 = after([far2, near2], [sum1[0]])
+    across2 = by_near(far2)
+    (p5,) = after([p5], [far2])
     (extra,) = after([extra], [p5])
     e = step(extra, outer)
-    far2, near2 = after([far2, near2], [extra])
-    across2 = by_near(far2)
     s3 = jnp.where(end, p5, p4)
     far3, near3 = by_far(s3), by_near(s3)
     sum2, sum3 = products(

time: 156 us -> 153 us (0.981)
  waiting for transfers between devices: 38.7 us -> 37 us
    ppermute x3, waiting for transfers between devices: 1.18 us -> 8.81 us  [by_far(): return lax.ppermute(x, 'chan', far_pairs)]
    ppermute x5, waiting for transfers between devices: 12 us -> 6.03 us  [by_near(): return lax.ppermute(x, 'chan', near_pairs)]
    ppermute x6, waiting for transfers between devices: 18.3 us -> 14.8 us  [step(): return lax.ppermute(x, axes, pairs)]
  transfers between devices with their start and end apart: 22 -> 22, of which waited for: 10 -> 9; matrix products, arithmetic and copies ran while one was open for 11% -> 11% of each run, Pallas kernels for 43% -> 43%
where the time goes in v5:
time: 153 us; the launch traced here: 152 us
  Pallas kernels  73.2 us (48%)
  waiting for transfers between devices  37 us (24%)
  starting transfers between devices  22.1 us (14%)
  other arithmetic  9.59 us (6%)
  local copies, waits for them, and re-layouts  8.37 us (5%)
  between operations  2.07 us (1%)
    pallas_call x6, Pallas kernels, products(): pl.pallas_call(functools.partial(products_body, plan), in_specs=[IN_SMEM]...  70.5 us
    ppermute x6, waiting for transfers between devices, step(): return lax.ppermute(x, axes, pairs)  14.8 us
    ppermute x3, waiting for transfers between devices, by_far(): return lax.ppermute(x, 'chan', far_pairs)  8.81 us
    ppermute x6, starting transfers between devices, step(): return lax.ppermute(x, axes, pairs)  8.78 us
    ppermute x5, waiting for transfers between devices, by_near(): return lax.ppermute(x, 'chan', near_pairs)  6.03 us
    reshape x2, local copies, waits for them, and re-layouts, own_rows(): return rows.reshape(depth, part)  4.58 us
    ppermute x5, starting transfers between devices, by_near(): return lax.ppermute(x, 'chan', near_pairs)  4.56 us
    all_to_all x1, waiting for transfers between devices, meta_over(): return lax.all_to_all(back, 'chan', split_axis=0, concat_axis=0, tiled=True)  4.05 us
  transfers between devices with their start and end apart: 22, of which 9 were waited for; matrix products, arithmetic and copies ran while one was open for 11% of the time, Pallas kernels for 43%

profile of v5, /device:TPU:0, one launch (start us, length us, event | category | flops | bytes accessed | tf_op | source)
XLA Modules:
  0.0 152.3 jit_solution(7277824457241961413)
XLA Ops:
  0.0 0.5 collective-permute-start.4
  0.5 2.3 %dynamic-slice_bitcast_fusion.1.refs_0_ = bf16[2048,256]{1,0:T(8,128)(2,1)} fusion(bf16[4,2048,512]{2,1,0:T(8,128)(2,1)} %refs_2_.1, s32[]{:T(128)S(6)} %select_n.72, s32[]{:T(128)S(6)} %select_n.73), kind=kLoop, calls=%fused_computation.7 | loop fusion | bytes 2097160 | tf_op jit(solution)/shard_map/reshape | solution.py:347
  2.7 2.6 %collective-permute-start.1 = (bf16[2048,256]{1,0:T(8,128)(2,1)}, bf16[2048,256]{1,0:T(8,128)(2,1)}, u32[]{:S(2)}, u32[]{:S(2)}) collective-permute-start(bf16[2048,256]{1,0:T(8,128)(2,1)} %shard_map.64.refs_2_), channel_id=1, source_target_pairs={{0,1},{1,0},{2,3},{3,2},{4,5},{5,4},{6,7},{7,6},{8,9},{9,8},{10,11... | collective-permute-start | bytes 3145736 | tf_op jit(solution)/shard_map/ppermute | solution.py:323
  5.3 1.7 %collective-permute-start.3 = (bf16[2048,256]{1,0:T(8,128)(2,1)}, bf16[2048,256]{1,0:T(8,128)(2,1)}, u32[]{:S(2)}, u32[]{:S(2)}) collective-permute-start(bf16[2048,256]{1,0:T(8,128)(2,1)} %shard_map.64.refs_2_), channel_id=1, source_target_pairs={{1,2},{2,1},{5,6},{6,5},{9,10},{10,9},{13,14},{14,13},{17,18},{18,... | collective-permute-start | bytes 3145736 | tf_op jit(solution)/shard_map/ppermute | solution.py:323
  7.0 0.7 slice.18
  7.7 0.2 collective-permute-start
  7.9 0.7 dynamic_slice.13
  8.6 0.7 dynamic-slice_convert_fusion
  9.3 1.2 select_reduce_fusion.3
  10.5 0.6 maximum_bitcast_fusion.refs_0_
  11.1 0.0 collective-permute-done.refs_1_
  11.1 0.6 copy-done.1
  11.7 3.7 %all-to-all-start = ((f32[8,2,128]{2,1,0:T(2,128)}), f32[8,2,128]{2,1,0:T(2,128)S(1)}, u32[]{:S(2)}, u32[]{:S(2)}) async-start(f32[8,2,128]{2,1,0:T(2,128)} %shard_map.65), calls=%async_computation | async-start | bytes 16384 | tf_op jit(solution)/shard_map/all_to_all | solution.py:271
  15.5 0.1 stack.56.scalars.table_ref
  15.6 0.5 copy.34.refs_0_
  16.1 4.1 %all-to-all-done = f32[8,2,128]{2,1,0:T(2,128)S(1)} async-done(((f32[8,2,128]{2,1,0:T(2,128)}), f32[8,2,128]{2,1,0:T(2,128)S(1)}, u32[]{:S(2)}, u32[]{:S(2)}) %all-to-all-start) | async-done | bytes 8224 | tf_op jit(solution)/shard_map/all_to_all | solution.py:271
  20.2 1.2 select_reduce_fusion.1
  21.4 1.2 select_select_fusion.refs_1_.refs_0_
  22.6 1.2 slice.17
  25.4 2.3 %dynamic-slice_bitcast_fusion.refs_1_ = bf16[2048,256]{1,0:T(8,128)(2,1)} fusion(bf16[4,2048,512]{2,1,0:T(8,128)(2,1)} %refs_2_.1, s32[]{:T(128)S(6)} %select_n.78, s32[]{:T(128)S(6)} %select_n.73), kind=kLoop, calls=%fused_computation.6 | loop fusion | bytes 2097160 | tf_op jit(solution)/shard_map/reshape | solution.py:347
  27.8 1.7 %collective-permute-done.1.refs_0_ = bf16[2048,256]{1,0:T(8,128)(2,1)} collective-permute-done((bf16[2048,256]{1,0:T(8,128)(2,1)}, bf16[2048,256]{1,0:T(8,128)(2,1)}, u32[]{:S(2)}, u32[]{:S(2)}) %collective-permute-start.1) | collective-permute-done | bytes 1048608 | tf_op jit(solution)/shard_map/ppermute | solution.py:323
  29.4 1.7 %collective-permute-start.8 = (bf16[2048,256]{1,0:T(8,128)(2,1)}, bf16[2048,256]{1,0:T(8,128)(2,1)}, u32[]{:S(2)}, u32[]{:S(2)}) collective-permute-start(bf16[2048,256]{1,0:T(8,128)(2,1)} %shard_map.68.refs_2_.refs_3_.refs_4_), channel_id=1, source_target_pairs={{0,8},{4,20},{8,0},{12,28},{16,24},{20,4},{24,16},{28,12},{1,9},{5... | collective-permute-start | bytes 3145736 | tf_op jit(solution)/shard_map/ppermute | solution.py:326
  31.1 1.5 collective-permute-start.6
  32.6 0.0 collective-permute-done.3.refs_0_
  32.6 0.0 collective-permute-done.4.refs_1_
  32.6 1.3 collective-permute-start.5
  33.9 0.1 collective-permute-start.7
  34.0 1.7 %collective-permute-start.2 = (bf16[2048,256]{1,0:T(8,128)(2,1)}, bf16[2048,256]{1,0:T(8,128)(2,1)}, u32[]{:S(2)}, u32[]{:S(2)}) collective-permute-start(bf16[2048,256]{1,0:T(8,128)(2,1)} %shard_map.68.refs_2_.refs_3_.refs_4_), channel_id=1, source_target_pairs={{1,2},{2,1},{5,6},{6,5},{9,10},{10,9},{13,14},{14,13},{17,18},{18,... | collective-permute-start | bytes 3145736 | tf_op jit(solution)/shard_map/ppermute | solution.py:323
  35.7 15.3 %shard_map.70.refs_1_.refs_10_ = bf16[1024,2048]{1,0:T(8,128)(2,1)} custom-call(s32[11]{0:T(128)} %copy-done, bf16[1024,2048]{1,0:T(8,128)(2,1)} %refs_0_.11, f32[1024,128]{1,0:T(8,128)} %get-tuple-element.29.refs_1_.refs_2_, bf16[4,2048,512]{2,1,0:T(8,128)(2,1)} %refs_2_.1, bf16[2048,256]{1,0:T(8,128)(2,1)} %shard_map.68.refs_2_.refs_3_.refs_4_), custom_call_target="tpu_custom_call" | custom-call | flops 1 | bytes 1 | tf_op jit(solution)/shard_map/pallas_call | solution.py:188
  51.1 4.6 %collective-permute-done.8.refs_0_ = bf16[2048,256]{1,0:T(8,128)(2,1)} collective-permute-done((bf16[2048,256]{1,0:T(8,128)(2,1)}, bf16[2048,256]{1,0:T(8,128)(2,1)}, u32[]{:S(2)}, u32[]{:S(2)}) %collective-permute-start.8) | collective-permute-done | bytes 1048608 | tf_op jit(solution)/shard_map/ppermute | solution.py:326
  55.7 0.0 collective-permute-done.7.refs_1_
  55.7 0.0 collective-permute-done.6.refs_0_
  55.7 3.3 %collective-permute-done.5.refs_0_ = bf16[2048,256]{1,0:T(8,128)(2,1)} collective-permute-done((bf16[2048,256]{1,0:T(8,128)(2,1)}, bf16[2048,256]{1,0:T(8,128)(2,1)}, u32[]{:S(2)}, u32[]{:S(2)}) %collective-permute-start.5) | collective-permute-done | bytes 1048608 | tf_op jit(solution)/shard_map/ppermute | solution.py:323
  59.0 2.3 %broadcast_select_fusion.1.refs_1_.refs_4_ = bf16[2048,256]{1,0:T(8,128)(2,1)} fusion(bf16[2048,256]{1,0:T(8,128)(2,1)} %shard_map.73, bf16[2048,256]{1,0:T(8,128)(2,1)} %get-tuple-element.30, pred[]{:T(512)S(6)} %or.3), kind=kLoop, calls=%fused_computation.9 | loop fusion | flops 524288 | bytes 3145729 | tf_op jit(solution)/shard_map/jit(_where)/select_n | solution.py:368
  61.3 1.3 collective-permute-start.10
  62.6 1.5 collective-permute-start.11
  64.1 0.0 collective-permute-done.2.refs_0_
  64.1 1.5 collective-permute-start.9
  65.6 12.3 %shard_map.75 = (bf16[1024,256]{1,0:T(8,128)(2,1)}, bf16[1024,256]{1,0:T(8,128)(2,1)}) custom-call(s32[11]{0:T(128)} %copy-done, bf16[1024,2048]{1,0:T(8,128)(2,1)} %refs_0_.11, bf16[1024,2048]{1,0:T(8,128)(2,1)} %get-tuple-element.32.refs_1_, f32[1024,128]{1,0:T(8,128)} %get-tuple-element.29.refs_1_.refs_2_, f32[1024,128]{1,0:T(8,128)} %get-tuple-element.33.refs_3_, ...), custom_call_target="tpu_custom_call" | custom-call | flops 1 | bytes 1 | tf_op jit(solution)/shard_map/pallas_call | solution.py:188
  77.8 8.8 %collective-permute-done.10.refs_0_ = bf16[2048,256]{1,0:T(8,128)(2,1)} collective-permute-done((bf16[2048,256]{1,0:T(8,128)(2,1)}, bf16[2048,256]{1,0:T(8,128)(2,1)}, u32[]{:S(2)}, u32[]{:S(2)}) %collective-permute-start.10) | collective-permute-done | bytes 1048608 | tf_op jit(solution)/shard_map/ppermute | solution.py:329
  86.6 0.0 collective-permute-done.11.refs_1_
  86.7 0.4 collective-permute-start.15
  87.1 4.1 %collective-permute-done.9.refs_0_ = bf16[2048,256]{1,0:T(8,128)(2,1)} collective-permute-done((bf16[2048,256]{1,0:T(8,128)(2,1)}, bf16[2048,256]{1,0:T(8,128)(2,1)}, u32[]{:S(2)}, u32[]{:S(2)}) %collective-permute-start.9) | collective-permute-done | bytes 1048608 | tf_op jit(solution)/shard_map/ppermute | solution.py:323
  91.1 0.0 collective-permute-start.14
  91.1 2.3 %broadcast_select_fusion.refs_7_.refs_8_ = bf16[2048,256]{1,0:T(8,128)(2,1)} fusion(bf16[2048,256]{1,0:T(8,128)(2,1)} %shard_map.77.refs_1_, bf16[2048,256]{1,0:T(8,128)(2,1)} %shard_map.74.refs_7_, pred[]{:T(512)S(6)} %or.3), kind=kLoop, calls=%fused_computation.8 | loop fusion | flops 524288 | bytes 3145729 | tf_op jit(solution)/shard_map/jit(_where)/select_n | solution.py:381
  93.5 0.5 collective-permute-start.12
  94.0 0.4 collective-permute-start.13
  94.4 15.2 %shard_map.79 = (bf16[1024,256]{1,0:T(8,128)(2,1)}, bf16[1024,256]{1,0:T(8,128)(2,1)}, bf16[1024,256]{1,0:T(8,128)(2,1)}, bf16[1024,256]{1,0:T(8,128)(2,1)}) custom-call(s32[11]{0:T(128)} %copy-done, bf16[1024,2048]{1,0:T(8,128)(2,1)} %refs_0_.11, bf16[1024,2048]{1,0:T(8,128)(2,1)} %get-tuple-element.32.refs_1_, ...), custom_call_target="tpu_custom_call" | custom-call | flops 1 | bytes 1 | tf_op jit(solution)/shard_map/pallas_call | solution.py:188
  109.6 5.8 %collective-permute-done.14.refs_0_ = bf16[2048,256]{1,0:T(8,128)(2,1)} collective-permute-done((bf16[2048,256]{1,0:T(8,128)(2,1)}, bf16[2048,256]{1,0:T(8,128)(2,1)}, u32[]{:S(2)}, u32[]{:S(2)}) %collective-permute-start.14) | collective-permute-done | bytes 1048608 | tf_op jit(solution)/shard_map/ppermute | solution.py:323
  115.4 0.0 collective-permute-done.15.refs_1_
  115.4 10.5 %shard_map.81 = (bf16[1024,2048]{1,0:T(8,128)(2,1)}, bf16[1024,256]{1,0:T(8,128)(2,1)}, bf16[16,256]{1,0:T(8,128)(2,1)}, bf16[1024,256]{1,0:T(8,128)(2,1)}) custom-call(s32[11]{0:T(128)} %copy-done, bf16[1024,2048]{1,0:T(8,128)(2,1)} %refs_0_.11, bf16[1024,2048]{1,0:T(8,128)(2,1)} %get-tuple-element.32.refs_1_, ...), custom_call_target="tpu_custom_call", output_to_operand_aliasing={{0}: (11, {})} | custom-call | flops 1 | bytes 1 | tf_op jit(solution)/shard_map/pallas_call | solution.py:188
  125.9 0.0 collective-permute-done.12.refs_0_
  125.9 0.0 collective-permute-done.13.refs_1_
  125.9 0.6 collective-permute-start.16
  126.5 0.0 collective-permute-start.17
  126.5 0.5 collective-permute-start.18
  127.0 9.9 %shard_map.83 = (bf16[1024,256]{1,0:T(8,128)(2,1)}, bf16[1024,256]{1,0:T(8,128)(2,1)}) custom-call(s32[11]{0:T(128)} %copy-done, bf16[1024,2048]{1,0:T(8,128)(2,1)} %refs_0_.11, bf16[1024,2048]{1,0:T(8,128)(2,1)} %get-tuple-element.32.refs_1_, f32[1024,128]{1,0:T(8,128)} %get-tuple-element.29.refs_1_.refs_2_, f32[1024,128]{1,0:T(8,128)} %get-tuple-element.33.refs_3_, ...), custom_call_target="tpu_custom_call" | custom-call | flops 1 | bytes 1 | tf_op jit(solution)/shard_map/pallas_call | solution.py:188
  137.0 0.0 collective-permute-done.17.refs_0_
  137.0 0.0 collective-permute-done.18.refs_1_
  137.0 2.6 %shard_map.84.refs_1_.refs_6_ = bf16[1024,2048]{1,0:T(8,128)(2,1)} custom-call(s32[11]{0:T(128)} %copy-done, bf16[1024,256]{1,0:T(8,128)(2,1)} %collective-permute-done.17.refs_0_, bf16[1024,256]{1,0:T(8,128)(2,1)} %collective-permute-done.18.refs_1_, bf16[1024,2048]{1,0:T(8,128)(2,1)} %get-tuple-element.43.refs_2_, ...), custom_call_target="tpu_custom_call", output_to_operand_aliasing={{}: (3, {})} | custom-call | flops 1 | bytes 1 | tf_op jit(solution)/shard_map/pallas_call | solution.py:238
  139.7 1.4 collective-permute-done.16.refs_0_
  141.1 0.5 collective-permute-start.20
  141.6 3.2 %collective-permute-done.20.refs_5_ = bf16[1024,256]{1,0:T(8,128)(2,1)} collective-permute-done((bf16[1024,256]{1,0:T(8,128)(2,1)}, bf16[1024,256]{1,0:T(8,128)(2,1)}, u32[]{:S(2)}, u32[]{:S(2)}) %collective-permute-start.20) | collective-permute-done | bytes 524320 | tf_op jit(solution)/shard_map/ppermute | solution.py:332
  144.9 7.3 %shard_map.86 = (bf16[1024,2048]{1,0:T(8,128)(2,1)}, bf16[16,256]{1,0:T(8,128)(2,1)}) custom-call(s32[11]{0:T(128)} %copy-done, bf16[1024,2048]{1,0:T(8,128)(2,1)} %refs_0_.11, f32[1024,128]{1,0:T(8,128)} %get-tuple-element.29.refs_1_.refs_2_, bf16[2048,256]{1,0:T(8,128)(2,1)} %shard_map.85.refs_2_, ...), custom_call_target="tpu_custom_call", output_to_operand_aliasing={{0}: (7, {})} | custom-call | flops 1 | bytes 1 | tf_op jit(solution)/shard_map/pallas_call | solution.py:188
  (27 shorter events, 0.0 us)
Async XLA Ops:
  0.0 9.3 %copy-start.2 = (s32[1024]{0:T(1024)S(1)}, s32[1024]{0:T(1024)}, u32[]{:S(2)}) copy-start(s32[1024]{0:T(1024)} %param.9) | copy-start | bytes 12292
  0.0 20.1 %copy-start.3 = (s32[1024]{0:T(1024)S(1)}, s32[1024]{0:T(1024)}, u32[]{:S(2)}) copy-start(s32[1024]{0:T(1024)} %param.8) | copy-start | bytes 12292
  0.0 32.6 %collective-permute-start.4 = (bf16[1024,2048]{1,0:T(8,128)(2,1)}, bf16[1024,2048]{1,0:T(8,128)(2,1)}, u32[]{:S(2)}, u32[]{:S(2)}) collective-permute-start(bf16[1024,2048]{1,0:T(8,128)(2,1)} %refs_0_.11), channel_id=1, source_target_pairs={{0,4},{4,0},{8,12},{12,8},{16,20},{20,16},{24,28},{28,24},{1,5},{5... | collective-permute-start | bytes 12582920 | tf_op jit(solution)/shard_map/ppermute | solution.py:332
  2.7 26.7 %collective-permute-start.1 = (bf16[2048,256]{1,0:T(8,128)(2,1)}, bf16[2048,256]{1,0:T(8,128)(2,1)}, u32[]{:S(2)}, u32[]{:S(2)}) collective-permute-start(bf16[2048,256]{1,0:T(8,128)(2,1)} %shard_map.64.refs_2_), channel_id=1, source_target_pairs={{0,1},{1,0},{2,3},{3,2},{4,5},{5,4},{6,7},{7,6},{8,9},{9,8},{10,11... | collective-permute-start | bytes 3145736 | tf_op jit(solution)/shard_map/ppermute | solution.py:323
  5.3 27.3 %collective-permute-start.3 = (bf16[2048,256]{1,0:T(8,128)(2,1)}, bf16[2048,256]{1,0:T(8,128)(2,1)}, u32[]{:S(2)}, u32[]{:S(2)}) collective-permute-start(bf16[2048,256]{1,0:T(8,128)(2,1)} %shard_map.64.refs_2_), channel_id=1, source_target_pairs={{1,2},{2,1},{5,6},{6,5},{9,10},{10,9},{13,14},{14,13},{17,18},{18,... | collective-permute-start | bytes 3145736 | tf_op jit(solution)/shard_map/ppermute | solution.py:323
  7.7 3.4 %collective-permute-start = (bf16[16,256]{1,0:T(8,128)(2,1)S(1)}, bf16[16,256]{1,0:T(8,128)(2,1)S(1)}, u32[]{:S(2)}, u32[]{:S(2)}) collective-permute-start(bf16[16,256]{1,0:T(8,128)(2,1)S(1)} %slice.18), channel_id=1, source_target_pairs={{0,4},{4,0},{8,12},{12,8},{16,20},{20,16},{24,28},{28,24},{1,5},{5... | collective-permute-start | bytes 24584 | tf_op jit(solution)/shard_map/ppermute | solution.py:332
  11.1 0.6 copy-start.1
  11.7 8.4 %all-to-all-start = ((f32[8,2,128]{2,1,0:T(2,128)}), f32[8,2,128]{2,1,0:T(2,128)S(1)}, u32[]{:S(2)}, u32[]{:S(2)}) async-start(f32[8,2,128]{2,1,0:T(2,128)} %shard_map.65), calls=%async_computation | async-start | bytes 16384 | tf_op jit(solution)/shard_map/all_to_all | solution.py:271
  15.6 13.9 %copy-start = (s32[11]{0:T(128)}, s32[11]{0:T(128)S(1)}, u32[]{:S(2)}) copy-start(s32[11]{0:T(128)S(1)} %stack.56.scalars.table_ref) | copy-start | bytes 136
  29.4 26.2 %collective-permute-start.8 = (bf16[2048,256]{1,0:T(8,128)(2,1)}, bf16[2048,256]{1,0:T(8,128)(2,1)}, u32[]{:S(2)}, u32[]{:S(2)}) collective-permute-start(bf16[2048,256]{1,0:T(8,128)(2,1)} %shard_map.68.refs_2_.refs_3_.refs_4_), channel_id=1, source_target_pairs={{0,8},{4,20},{8,0},{12,28},{16,24},{20,4},{24,16},{28,12},{1,9},{5... | collective-permute-start | bytes 3145736 | tf_op jit(solution)/shard_map/ppermute | solution.py:326
  31.1 24.6 %collective-permute-start.6 = (bf16[2048,256]{1,0:T(8,128)(2,1)}, bf16[2048,256]{1,0:T(8,128)(2,1)}, u32[]{:S(2)}, u32[]{:S(2)}) collective-permute-start(bf16[2048,256]{1,0:T(8,128)(2,1)} %shard_map.68.refs_2_.refs_3_.refs_4_), channel_id=1, source_target_pairs={{0,16},{4,12},{8,24},{12,4},{16,0},{20,28},{24,8},{28,20},{1,17},{... | collective-permute-start | bytes 3145736 | tf_op jit(solution)/shard_map/ppermute | solution.py:329
  32.6 26.4 %collective-permute-start.5 = (bf16[2048,256]{1,0:T(8,128)(2,1)}, bf16[2048,256]{1,0:T(8,128)(2,1)}, u32[]{:S(2)}, u32[]{:S(2)}) collective-permute-start(bf16[2048,256]{1,0:T(8,128)(2,1)} %get-tuple-element.30), channel_id=1, source_target_pairs={{1,0},{2,3},{5,4},{6,7},{9,8},{10,11},{13,12},{14,15},{17,16},{18,... | collective-permute-start | bytes 3145736 | tf_op jit(solution)/shard_map/ppermute | solution.py:323
  33.9 21.8 %collective-permute-start.7 = (f32[1024,128]{1,0:T(8,128)}, f32[1024,128]{1,0:T(8,128)}, u32[]{:S(2)}, u32[]{:S(2)}) collective-permute-start(f32[1024,128]{1,0:T(8,128)} %get-tuple-element.29.refs_1_.refs_2_), channel_id=1, source_target_pairs={{0,4},{4,0},{8,12},{12,8},{16,20},{20,16},{24,28},{28,24},{1,5},{5... | collective-permute-start | bytes 1572872 | tf_op jit(solution)/shard_map/ppermute | solution.py:332
  34.0 30.1 %collective-permute-start.2 = (bf16[2048,256]{1,0:T(8,128)(2,1)}, bf16[2048,256]{1,0:T(8,128)(2,1)}, u32[]{:S(2)}, u32[]{:S(2)}) collective-permute-start(bf16[2048,256]{1,0:T(8,128)(2,1)} %shard_map.68.refs_2_.refs_3_.refs_4_), channel_id=1, source_target_pairs={{1,2},{2,1},{5,6},{6,5},{9,10},{10,9},{13,14},{14,13},{17,18},{18,... | collective-permute-start | bytes 3145736 | tf_op jit(solution)/shard_map/ppermute | solution.py:323
  61.3 25.3 %collective-permute-start.10 = (bf16[2048,256]{1,0:T(8,128)(2,1)}, bf16[2048,256]{1,0:T(8,128)(2,1)}, u32[]{:S(2)}, u32[]{:S(2)}) collective-permute-start(bf16[2048,256]{1,0:T(8,128)(2,1)} %broadcast_select_fusion.1.refs_1_.refs_4_), channel_id=1, source_target_pairs={{0,16},{4,12},{8,24},{12,4},{16,0},{20,28},{24,8},{28,20},{1,17},{... | collective-permute-start | bytes 3145736 | tf_op jit(solution)/shard_map/ppermute | solution.py:329
  62.6 24.0 %collective-permute-start.11 = (bf16[2048,256]{1,0:T(8,128)(2,1)}, bf16[2048,256]{1,0:T(8,128)(2,1)}, u32[]{:S(2)}, u32[]{:S(2)}) collective-permute-start(bf16[2048,256]{1,0:T(8,128)(2,1)} %broadcast_select_fusion.1.refs_1_.refs_4_), channel_id=1, source_target_pairs={{0,8},{4,20},{8,0},{12,28},{16,24},{20,4},{24,16},{28,12},{1,9},{5... | collective-permute-start | bytes 3145736 | tf_op jit(solution)/shard_map/ppermute | solution.py:326
  64.1 27.0 %collective-permute-start.9 = (bf16[2048,256]{1,0:T(8,128)(2,1)}, bf16[2048,256]{1,0:T(8,128)(2,1)}, u32[]{:S(2)}, u32[]{:S(2)}) collective-permute-start(bf16[2048,256]{1,0:T(8,128)(2,1)} %shard_map.74.refs_7_), channel_id=1, source_target_pairs={{1,0},{2,3},{5,4},{6,7},{9,8},{10,11},{13,12},{14,15},{17,16},{18,... | collective-permute-start | bytes 3145736 | tf_op jit(solution)/shard_map/ppermute | solution.py:323
  86.7 28.8 %collective-permute-start.15 = (bf16[2048,256]{1,0:T(8,128)(2,1)}, bf16[2048,256]{1,0:T(8,128)(2,1)}, u32[]{:S(2)}, u32[]{:S(2)}) collective-permute-start(bf16[2048,256]{1,0:T(8,128)(2,1)} %get-tuple-element.35.refs_1_.refs_6_), channel_id=1, source_target_pairs={{0,8},{4,20},{8,0},{12,28},{16,24},{20,4},{24,16},{28,12},{1,9},{5... | collective-permute-start | bytes 3145736 | tf_op jit(solution)/shard_map/ppermute | solution.py:326
  91.1 24.3 %collective-permute-start.14 = (bf16[2048,256]{1,0:T(8,128)(2,1)}, bf16[2048,256]{1,0:T(8,128)(2,1)}, u32[]{:S(2)}, u32[]{:S(2)}) collective-permute-start(bf16[2048,256]{1,0:T(8,128)(2,1)} %shard_map.78), channel_id=1, source_target_pairs={{0,1},{1,0},{2,3},{3,2},{4,5},{5,4},{6,7},{7,6},{8,9},{9,8},{10,11... | collective-permute-start | bytes 3145736 | tf_op jit(solution)/shard_map/ppermute | solution.py:323
  93.5 32.4 %collective-permute-start.12 = (bf16[2048,256]{1,0:T(8,128)(2,1)}, bf16[2048,256]{1,0:T(8,128)(2,1)}, u32[]{:S(2)}, u32[]{:S(2)}) collective-permute-start(bf16[2048,256]{1,0:T(8,128)(2,1)} %broadcast_select_fusion.refs_7_.refs_8_), channel_id=1, source_target_pairs={{0,16},{4,12},{8,24},{12,4},{16,0},{20,28},{24,8},{28,20},{1,17},{... | collective-permute-start | bytes 3145736 | tf_op jit(solution)/shard_map/ppermute | solution.py:329
  94.0 31.9 %collective-permute-start.13 = (bf16[2048,256]{1,0:T(8,128)(2,1)}, bf16[2048,256]{1,0:T(8,128)(2,1)}, u32[]{:S(2)}, u32[]{:S(2)}) collective-permute-start(bf16[2048,256]{1,0:T(8,128)(2,1)} %broadcast_select_fusion.refs_7_.refs_8_), channel_id=1, source_target_pairs={{0,8},{4,20},{8,0},{12,28},{16,24},{20,4},{24,16},{28,12},{1,9},{5... | collective-permute-start | bytes 3145736 | tf_op jit(solution)/shard_map/ppermute | solution.py:326
  125.9 15.2 %collective-permute-start.16 = (bf16[2048,256]{1,0:T(8,128)(2,1)}, bf16[2048,256]{1,0:T(8,128)(2,1)}, u32[]{:S(2)}, u32[]{:S(2)}) collective-permute-start(bf16[2048,256]{1,0:T(8,128)(2,1)} %get-tuple-element.44.refs_5_), channel_id=1, source_target_pairs={{0,8},{4,20},{8,0},{12,28},{16,24},{20,4},{24,16},{28,12},{1,9},{5... | collective-permute-start | bytes 3145736 | tf_op jit(solution)/shard_map/ppermute | solution.py:326
  126.5 10.5 %collective-permute-start.17 = (bf16[1024,256]{1,0:T(8,128)(2,1)}, bf16[1024,256]{1,0:T(8,128)(2,1)}, u32[]{:S(2)}, u32[]{:S(2)}) collective-permute-start(bf16[1024,256]{1,0:T(8,128)(2,1)} %get-tuple-element.45), channel_id=1, source_target_pairs={{0,4},{4,0},{8,12},{12,8},{16,20},{20,16},{24,28},{28,24},{1,5},{5... | collective-permute-start | bytes 1572872 | tf_op jit(solution)/shard_map/ppermute | solution.py:332
  126.5 10.5 %collective-permute-start.18 = (bf16[1024,256]{1,0:T(8,128)(2,1)}, bf16[1024,256]{1,0:T(8,128)(2,1)}, u32[]{:S(2)}, u32[]{:S(2)}) collective-permute-start(bf16[1024,256]{1,0:T(8,128)(2,1)} %get-tuple-element.46), channel_id=1, source_target_pairs={{0,4},{4,0},{8,12},{12,8},{16,20},{20,16},{24,28},{28,24},{1,5},{5... | collective-permute-start | bytes 1572872 | tf_op jit(solution)/shard_map/ppermute | solution.py:332
  141.1 3.8 %collective-permute-start.19 = (bf16[2048,256]{1,0:T(8,128)(2,1)}, bf16[2048,256]{1,0:T(8,128)(2,1)}, u32[]{:S(2)}, u32[]{:S(2)}) collective-permute-start(bf16[2048,256]{1,0:T(8,128)(2,1)} %shard_map.85.refs_2_), channel_id=1, source_target_pairs={{0,4},{4,0},{8,12},{12,8},{16,20},{20,16},{24,28},{28,24},{1,5},{5... | collective-permute-start | bytes 3145736 | tf_op jit(solution)/shard_map/ppermute | solution.py:332
  141.1 3.7 %collective-permute-start.20 = (bf16[1024,256]{1,0:T(8,128)(2,1)}, bf16[1024,256]{1,0:T(8,128)(2,1)}, u32[]{:S(2)}, u32[]{:S(2)}) collective-permute-start(bf16[1024,256]{1,0:T(8,128)(2,1)} %get-tuple-element.51), channel_id=1, source_target_pairs={{0,4},{4,0},{8,12},{12,8},{16,20},{20,16},{24,28},{28,24},{1,5},{5... | collective-permute-start | bytes 1572872 | tf_op jit(solution)/shard_map/ppermute | solution.py:332

commit v6 on v5

--- a/solution.py
+++ b/solution.py
@@ -131,6 +131,9 @@
                     product = part if product is None else product + part
                     used += 1
                 total = scale * product if total is None else total + scale * product
+            if total is None:
+                staged[g, here, :] = before_ref[g, here, :]
+                continue
             if befores[g]:
                 total = total + before_ref[g, here, :].astype(jnp.float32)
             staged[g, here, :] = total.astype(staged.dtype)
@@ -351,29 +354,28 @@
     other_t = sib(t_pp)
     fence = sib(own[:16])
     meta = meta_got(meta_over(meta_sent(fence)))
-    (later,) = after([table], [meta])
-    extra = own_rows(later[3])
-    meta, extra = after([meta, extra], [own])
-
-    (p1,) = after([p1], [meta])
-    p2, other_t = after([p2, other_t], [p1])
+    (meta,) = after([meta], [own])
+
+    (p2,) = after([p2], [meta])
+    p1, other_t = after([p1, other_t], [p2])
     p3, near1, far1, p4 = step(p2, outwards), by_near(p1), by_far(p1), step(p1, middle)
     other_meta = sib(meta)
     local = Group([(channel, interaction) for channel in range(channels)], column=own_column)
     ((out,),) = products(table, [t_pp], [meta], [local], [p1], result=shape)
 
-    (near1,) = after([near1], [out])
-    far1, other_meta = after([far1, other_meta], [near1])
-    (p3,) = after([p3], [far1])
+    p3, other_meta = after([p3, other_meta], [out])
     s2 = jnp.where(end, p3, p2)
     far2, near2 = by_far(s2), by_near(s2)
-    (p4,) = after([p4], [s2])
+    near1, far1 = after([near1, far1], [s2])
+    (p4,) = after([p4], [far1])
     p5 = step(p4, outwards)
     t_rows = [t_pp, other_t]
     metas = [meta, other_meta]
     (sum1,) = products(table, t_rows, metas, [Group([quarter(0, p1), quarter(1, near1), quarter(2, far1)])], [p4])
 
-    far2, near2 = after([far2, near2], [sum1[0]])
+    (later,) = after([table], [sum1[0]])
+    (extra,) = after([own_rows(later[3])], [sum1[0]])
+    far2, near2 = after([far2, near2], [extra])
     across2 = by_near(far2)
     (p5,) = after([p5], [far2])
     (extra,) = after([extra], [p5])
@@ -385,31 +387,34 @@
         [Group([quarter(0, s2), quarter(1, near2), quarter(2, far2)]), Group([quarter(0, s3)])],
         [s3],
     )
-    e, across2 = after([e, across2], [sum2[0]])
-    (out, rest1), (_, rest2) = products(
+    (across2,) = after([across2], [sum2[0]])
+    ((out, rest2),) = products(
+        table, t_rows, metas, [Group([quarter(3, across2)], before=sum2, column=columns[1])],
+        [across2], out=out, result=shape,
+    )
+    (back2,) = after([sib(rest2)], [out])
+
+    far3, near3 = after([far3, near3], [back2])
+    across3 = by_near(far3)
+    (e,) = after([e], [near3])
+    sum3, (out, rest1) = products(
         table, t_rows, metas,
         [
+            Group([quarter(1, near3), quarter(2, far3)], before=sum3),
             Group([quarter(3, e)], before=sum1, column=columns[0]),
-            Group([quarter(3, across2)], before=sum2, column=columns[1]),
         ],
-        [across2], out=out, result=shape,
+        [e], out=out, result=shape,
     )
-    back1, back2 = sib(rest1), sib(rest2)
-
-    far3, near3 = after([far3, near3], [out])
-    across3 = by_near(far3)
-    (sum3,) = products(
-        table, t_rows, metas, [Group([quarter(1, near3), quarter(2, far3)], before=sum3)], [near3]
-    )
-    back3 = sib(sum3[1])
-    out = place(table, out, other_columns[:2], [back1, back2], [sum3[0]])
-
-    (across3,) = after([across3], [out])
+    back1, back3 = after([sib(rest1), sib(sum3[1])], [out])
+
+    (across3,) = after([across3], [back3])
     groups = [
         Group([quarter(3, across3)], before=[sum3[0]], column=columns[2]),
         Group([quarter(3, sib(across3))], before=[back3], column=other_columns[2]),
+        Group([], before=[back1], column=other_columns[0]),
+        Group([], before=[back2], column=other_columns[1]),
     ]
-    ((out,), _) = products(table, [t_pp], [meta], groups, [], out=out, result=shape)
+    ((out,), *_) = products(table, [t_pp], [meta], groups, [], out=out, result=shape)
     return out
 
 

time: 153 us -> 152 us (level)
  Pallas kernels: 73.2 us -> 71.4 us
  starting transfers between devices: 22.1 us -> 23.8 us
  waiting for transfers between devices: 37 us -> 35.4 us
    ppermute x3, waiting for transfers between devices: 8.81 us -> 3.26 us  [by_far(): return lax.ppermute(x, 'chan', far_pairs)]
    ppermute x7, waiting for transfers between devices: 3.26 us -> 7.6 us  [sib(): return lax.ppermute(x, 'chan', other)]
    pallas_call x1 -> x0, Pallas kernels: 2.65 us -> none  [place(): pl.pallas_call(body, in_specs=[IN_SMEM] + [IN_HBM] * (count + 1 + len(ear...]
    ppermute x6, starting transfers between devices: 8.78 us -> 10.6 us  [step(): return lax.ppermute(x, axes, pairs)]
  transfers between devices with their start and end apart: 22 -> 22, of which waited for: 9 -> 11; matrix products, arithmetic and copies ran while one was open for 11% -> 12% of each run, Pallas kernels for 43% -> 42%
where the time goes in v6:
time: 152 us; the launch traced here: 151 us
  Pallas kernels  71.4 us (47%)
  waiting for transfers between devices  35.4 us (23%)
  starting transfers between devices  23.8 us (16%)
  other arithmetic  9.59 us (6%)
  local copies, waits for them, and re-layouts  8.86 us (6%)
  between operations  2.04 us (1%)
    pallas_call x6, Pallas kernels, products(): pl.pallas_call(functools.partial(products_body, plan), in_specs=[IN_SMEM]...  71.3 us
    ppermute x6, waiting for transfers between devices, step(): return lax.ppermute(x, axes, pairs)  14.6 us
    ppermute x6, starting transfers between devices, step(): return lax.ppermute(x, axes, pairs)  10.6 us
    ppermute x7, waiting for transfers between devices, sib(): return lax.ppermute(x, 'chan', other)  7.6 us
    ppermute x5, waiting for transfers between devices, by_near(): return lax.ppermute(x, 'chan', near_pairs)  5.25 us
    all_to_all x1, waiting for transfers between devices, meta_over(): return lax.all_to_all(back, 'chan', split_axis=0, concat_axis=0, tiled=True)  4.69 us
    ppermute x5, starting transfers between devices, by_near(): return lax.ppermute(x, 'chan', near_pairs)  4.59 us
    reshape x2, local copies, waits for them, and re-layouts, own_rows(): return rows.reshape(depth, part)  4.54 us
  transfers between devices with their start and end apart: 22, of which 11 were waited for; matrix products, arithmetic and copies ran while one was open for 12% of the time, Pallas kernels for 42%

profile of v6, /device:TPU:0, one launch (start us, length us, event | category | flops | bytes accessed | tf_op | source)
XLA Modules:
  0.0 151.1 jit_solution(7573435289370863630)
XLA Ops:
  0.0 0.5 collective-permute-start.2
  0.5 2.3 %dynamic-slice_bitcast_fusion.1.refs_0_ = bf16[2048,256]{1,0:T(8,128)(2,1)} fusion(bf16[4,2048,512]{2,1,0:T(8,128)(2,1)} %refs_2_.1, s32[]{:T(128)S(6)} %select_n.72, s32[]{:T(128)S(6)} %select_n.73), kind=kLoop, calls=%fused_computation.7 | loop fusion | bytes 2097160 | tf_op jit(solution)/shard_map/reshape | solution.py:350
  2.7 1.7 %collective-permute-start.3 = (bf16[2048,256]{1,0:T(8,128)(2,1)}, bf16[2048,256]{1,0:T(8,128)(2,1)}, u32[]{:S(2)}, u32[]{:S(2)}) collective-permute-start(bf16[2048,256]{1,0:T(8,128)(2,1)} %shard_map.64.refs_1_), channel_id=1, source_target_pairs={{1,2},{2,1},{5,6},{6,5},{9,10},{10,9},{13,14},{14,13},{17,18},{18,... | collective-permute-start | bytes 3145736 | tf_op jit(solution)/shard_map/ppermute | solution.py:326
  4.4 4.5 %collective-permute-start.1 = (bf16[2048,256]{1,0:T(8,128)(2,1)}, bf16[2048,256]{1,0:T(8,128)(2,1)}, u32[]{:S(2)}, u32[]{:S(2)}) collective-permute-start(bf16[2048,256]{1,0:T(8,128)(2,1)} %shard_map.64.refs_1_), channel_id=1, source_target_pairs={{0,1},{1,0},{2,3},{3,2},{4,5},{5,4},{6,7},{7,6},{8,9},{9,8},{10,11... | collective-permute-start | bytes 3145736 | tf_op jit(solution)/shard_map/ppermute | solution.py:326
  8.9 0.7 slice.18
  9.6 0.0 collective-permute-start
  9.6 0.7 dynamic_slice.13
  10.3 0.7 dynamic-slice_convert_fusion
  11.0 1.2 select_reduce_fusion.3
  12.2 0.6 maximum_bitcast_fusion.refs_0_
  12.8 0.0 collective-permute-done.refs_1_
  12.9 0.6 copy-done.1
  13.5 3.8 %all-to-all-start = ((f32[8,2,128]{2,1,0:T(2,128)}), f32[8,2,128]{2,1,0:T(2,128)S(1)}, u32[]{:S(2)}, u32[]{:S(2)}) async-start(f32[8,2,128]{2,1,0:T(2,128)} %shard_map.65), calls=%async_computation | async-start | bytes 16384 | tf_op jit(solution)/shard_map/all_to_all | solution.py:274
  17.3 4.7 %all-to-all-done = f32[8,2,128]{2,1,0:T(2,128)S(1)} async-done(((f32[8,2,128]{2,1,0:T(2,128)}), f32[8,2,128]{2,1,0:T(2,128)S(1)}, u32[]{:S(2)}, u32[]{:S(2)}) %all-to-all-start) | async-done | bytes 8224 | tf_op jit(solution)/shard_map/all_to_all | solution.py:274
  22.0 1.2 select_reduce_fusion.1
  23.2 1.1 select_select_fusion.refs_0_
  24.4 0.0 collective-permute-done.3.refs_0_
  24.4 1.3 collective-permute-start.7
  25.7 0.1 collective-permute-start.8
  25.8 6.9 %collective-permute-done.1.refs_0_ = bf16[2048,256]{1,0:T(8,128)(2,1)} collective-permute-done((bf16[2048,256]{1,0:T(8,128)(2,1)}, bf16[2048,256]{1,0:T(8,128)(2,1)}, u32[]{:S(2)}, u32[]{:S(2)}) %collective-permute-start.1) | collective-permute-done | bytes 1048608 | tf_op jit(solution)/shard_map/ppermute | solution.py:326
  32.7 0.0 collective-permute-done.2.refs_1_
  32.7 1.5 collective-permute-start.5
  34.2 1.5 %collective-permute-start.6 = (bf16[2048,256]{1,0:T(8,128)(2,1)}, bf16[2048,256]{1,0:T(8,128)(2,1)}, u32[]{:S(2)}, u32[]{:S(2)}) collective-permute-start(bf16[2048,256]{1,0:T(8,128)(2,1)} %get-tuple-element.30.refs_3_.refs_4_), channel_id=1, source_target_pairs={{0,16},{4,12},{8,24},{12,4},{16,0},{20,28},{24,8},{28,20},{1,17},{... | collective-permute-start | bytes 3145736 | tf_op jit(solution)/shard_map/ppermute | solution.py:332
  35.7 1.6 %collective-permute-start.4 = (bf16[2048,256]{1,0:T(8,128)(2,1)}, bf16[2048,256]{1,0:T(8,128)(2,1)}, u32[]{:S(2)}, u32[]{:S(2)}) collective-permute-start(bf16[2048,256]{1,0:T(8,128)(2,1)} %get-tuple-element.30.refs_3_.refs_4_), channel_id=1, source_target_pairs={{1,2},{2,1},{5,6},{6,5},{9,10},{10,9},{13,14},{14,13},{17,18},{18,... | collective-permute-start | bytes 3145736 | tf_op jit(solution)/shard_map/ppermute | solution.py:326
  37.4 0.6 stack.56.scalars
  38.0 15.3 %shard_map.69.refs_2_.refs_7_ = bf16[1024,2048]{1,0:T(8,128)(2,1)} custom-call(s32[11]{0:T(128)} %stack.56.scalars, bf16[1024,2048]{1,0:T(8,128)(2,1)} %refs_0_.11, f32[1024,128]{1,0:T(8,128)} %shard_map.66.refs_1_.refs_2_, bf16[4,2048,512]{2,1,0:T(8,128)(2,1)} %refs_2_.1, bf16[2048,256]{1,0:T(8,128)(2,1)} %get-tuple-element.30.refs_3_.refs_4_), custom_call_target="tpu_custom_call" | custom-call | flops 1 | bytes 1 | tf_op jit(solution)/shard_map/pallas_call | solution.py:191
  53.3 0.0 collective-permute-done.8.refs_1_
  53.3 4.3 %collective-permute-done.7.refs_0_ = bf16[2048,256]{1,0:T(8,128)(2,1)} collective-permute-done((bf16[2048,256]{1,0:T(8,128)(2,1)}, bf16[2048,256]{1,0:T(8,128)(2,1)}, u32[]{:S(2)}, u32[]{:S(2)}) %collective-permute-start.7) | collective-permute-done | bytes 1048608 | tf_op jit(solution)/shard_map/ppermute | solution.py:326
  57.6 2.3 %broadcast_select_fusion.1.refs_2_.refs_4_ = bf16[2048,256]{1,0:T(8,128)(2,1)} fusion(bf16[2048,256]{1,0:T(8,128)(2,1)} %get-tuple-element.31, bf16[2048,256]{1,0:T(8,128)(2,1)} %shard_map.67.refs_2_, pred[]{:T(512)S(6)} %or.3), kind=kLoop, calls=%fused_computation.9 | loop fusion | flops 524288 | bytes 3145729 | tf_op jit(solution)/shard_map/jit(_where)/select_n | solution.py:367
  60.0 1.5 %collective-permute-start.10 = (bf16[2048,256]{1,0:T(8,128)(2,1)}, bf16[2048,256]{1,0:T(8,128)(2,1)}, u32[]{:S(2)}, u32[]{:S(2)}) collective-permute-start(bf16[2048,256]{1,0:T(8,128)(2,1)} %broadcast_select_fusion.1.refs_2_.refs_4_), channel_id=1, source_target_pairs={{0,16},{4,12},{8,24},{12,4},{16,0},{20,28},{24,8},{28,20},{1,17},{... | collective-permute-start | bytes 3145736 | tf_op jit(solution)/shard_map/ppermute | solution.py:332
  61.5 1.5 collective-permute-start.11
  63.0 0.0 collective-permute-done.5.refs_0_
  63.0 0.0 collective-permute-done.6.refs_1_
  63.0 0.0 collective-permute-done.4.refs_0_
  63.0 1.5 collective-permute-start.9
  64.5 0.5 copy.46.refs_0_
  65.0 12.3 %shard_map.73 = (bf16[1024,256]{1,0:T(8,128)(2,1)}, bf16[1024,256]{1,0:T(8,128)(2,1)}) custom-call(s32[11]{0:T(128)} %stack.56.scalars, bf16[1024,2048]{1,0:T(8,128)(2,1)} %refs_0_.11, bf16[1024,2048]{1,0:T(8,128)(2,1)} %get-tuple-element.33.refs_1_, f32[1024,128]{1,0:T(8,128)} %shard_map.66.refs_1_.refs_2_, f32[1024,128]{1,0:T(8,128)} %get-tuple-element.34.refs_3_, ...), custom_call_target="tpu_custom_call" | custom-call | flops 1 | bytes 1 | tf_op jit(solution)/shard_map/pallas_call | solution.py:191
  77.3 1.2 slice.17
  80.2 2.3 %dynamic-slice_bitcast_fusion.refs_0_ = bf16[2048,256]{1,0:T(8,128)(2,1)} fusion(bf16[4,2048,512]{2,1,0:T(8,128)(2,1)} %refs_2_.1, s32[]{:T(128)S(6)} %select_n.80, s32[]{:T(128)S(6)} %select_n.73), kind=kLoop, calls=%fused_computation.6 | loop fusion | bytes 2097160 | tf_op jit(solution)/shard_map/reshape | solution.py:350
  82.4 3.2 %collective-permute-done.10.refs_0_ = bf16[2048,256]{1,0:T(8,128)(2,1)} collective-permute-done((bf16[2048,256]{1,0:T(8,128)(2,1)}, bf16[2048,256]{1,0:T(8,128)(2,1)}, u32[]{:S(2)}, u32[]{:S(2)}) %collective-permute-start.10) | collective-permute-done | bytes 1048608 | tf_op jit(solution)/shard_map/ppermute | solution.py:332
  85.7 0.0 collective-permute-done.11.refs_1_
  85.7 0.5 collective-permute-start.14
  86.2 3.3 %collective-permute-done.9.refs_0_ = bf16[2048,256]{1,0:T(8,128)(2,1)} collective-permute-done((bf16[2048,256]{1,0:T(8,128)(2,1)}, bf16[2048,256]{1,0:T(8,128)(2,1)}, u32[]{:S(2)}, u32[]{:S(2)}) %collective-permute-start.9) | collective-permute-done | bytes 1048608 | tf_op jit(solution)/shard_map/ppermute | solution.py:326
  89.5 2.3 %broadcast_select_fusion.refs_7_.refs_8_ = bf16[2048,256]{1,0:T(8,128)(2,1)} fusion(bf16[2048,256]{1,0:T(8,128)(2,1)} %shard_map.77.refs_1_, bf16[2048,256]{1,0:T(8,128)(2,1)} %shard_map.72.refs_7_, pred[]{:T(512)S(6)} %or.3), kind=kLoop, calls=%fused_computation.8 | loop fusion | flops 524288 | bytes 3145729 | tf_op jit(solution)/shard_map/jit(_where)/select_n | solution.py:383
  91.9 0.5 collective-permute-start.12
  92.4 0.5 collective-permute-start.13
  92.9 15.3 %shard_map.78 = (bf16[1024,256]{1,0:T(8,128)(2,1)}, bf16[1024,256]{1,0:T(8,128)(2,1)}, bf16[1024,256]{1,0:T(8,128)(2,1)}, bf16[1024,256]{1,0:T(8,128)(2,1)}) custom-call(s32[11]{0:T(128)} %stack.56.scalars, bf16[1024,2048]{1,0:T(8,128)(2,1)} %refs_0_.11, bf16[1024,2048]{1,0:T(8,128)(2,1)} %get-tuple-element.33.refs_1_, ...), custom_call_target="tpu_custom_call" | custom-call | flops 1 | bytes 1 | tf_op jit(solution)/shard_map/pallas_call | solution.py:191
  108.2 0.2 collective-permute-done.14.refs_0_
  108.4 7.5 %shard_map.80 = (bf16[1024,2048]{1,0:T(8,128)(2,1)}, bf16[1024,256]{1,0:T(8,128)(2,1)}) custom-call(s32[11]{0:T(128)} %stack.56.scalars, bf16[1024,2048]{1,0:T(8,128)(2,1)} %refs_0_.11, bf16[1024,2048]{1,0:T(8,128)(2,1)} %get-tuple-element.33.refs_1_, f32[1024,128]{1,0:T(8,128)} %shard_map.66.refs_1_.refs_2_, ...), custom_call_target="tpu_custom_call", output_to_operand_aliasing={{0}: (8, {})} | custom-call | flops 1 | bytes 1 | tf_op jit(solution)/shard_map/pallas_call | solution.py:191
  115.9 0.1 collective-permute-start.15
  116.0 2.2 %collective-permute-done.15.refs_0_ = bf16[1024,256]{1,0:T(8,128)(2,1)} collective-permute-done((bf16[1024,256]{1,0:T(8,128)(2,1)}, bf16[1024,256]{1,0:T(8,128)(2,1)}, u32[]{:S(2)}, u32[]{:S(2)}) %collective-permute-start.15) | collective-permute-done | bytes 524320 | tf_op jit(solution)/shard_map/ppermute | solution.py:335
  118.3 0.0 collective-permute-done.12.refs_0_
  118.3 5.0 %collective-permute-done.13.refs_1_ = bf16[2048,256]{1,0:T(8,128)(2,1)} collective-permute-done((bf16[2048,256]{1,0:T(8,128)(2,1)}, bf16[2048,256]{1,0:T(8,128)(2,1)}, u32[]{:S(2)}, u32[]{:S(2)}) %collective-permute-start.13) | collective-permute-done | bytes 1048608 | tf_op jit(solution)/shard_map/ppermute | solution.py:329
  123.3 0.5 collective-permute-start.16
  123.8 0.0 collective-permute-done.17.refs_0_
  123.8 13.0 %shard_map.85 = (bf16[1024,256]{1,0:T(8,128)(2,1)}, bf16[1024,256]{1,0:T(8,128)(2,1)}, bf16[1024,2048]{1,0:T(8,128)(2,1)}, bf16[1024,256]{1,0:T(8,128)(2,1)}) custom-call(s32[11]{0:T(128)} %stack.56.scalars, bf16[1024,2048]{1,0:T(8,128)(2,1)} %refs_0_.11, bf16[1024,2048]{1,0:T(8,128)(2,1)} %get-tuple-element.33.refs_1_, ...), custom_call_target="tpu_custom_call", output_to_operand_aliasing={{2}: (12, {})} | custom-call | flops 1 | bytes 1 | tf_op jit(solution)/shard_map/pallas_call | solution.py:191
  136.8 0.1 collective-permute-start.18
  136.9 0.5 collective-permute-start.19
  137.4 1.7 %collective-permute-done.18.refs_0_ = bf16[1024,256]{1,0:T(8,128)(2,1)} collective-permute-done((bf16[1024,256]{1,0:T(8,128)(2,1)}, bf16[1024,256]{1,0:T(8,128)(2,1)}, u32[]{:S(2)}, u32[]{:S(2)}) %collective-permute-start.18) | collective-permute-done | bytes 524320 | tf_op jit(solution)/shard_map/ppermute | solution.py:335
  139.1 0.7 collective-permute-done.19.refs_1_
  139.9 0.0 collective-permute-done.16.refs_0_
  139.9 0.1 collective-permute-start.20
  140.0 2.9 %collective-permute-done.20.refs_3_ = bf16[2048,256]{1,0:T(8,128)(2,1)} collective-permute-done((bf16[2048,256]{1,0:T(8,128)(2,1)}, bf16[2048,256]{1,0:T(8,128)(2,1)}, u32[]{:S(2)}, u32[]{:S(2)}) %collective-permute-start.20) | collective-permute-done | bytes 1048608 | tf_op jit(solution)/shard_map/ppermute | solution.py:335
  142.9 8.0 %shard_map.88 = (bf16[1024,2048]{1,0:T(8,128)(2,1)}, bf16[16,256]{1,0:T(8,128)(2,1)}, bf16[16,256]{1,0:T(8,128)(2,1)}, bf16[16,256]{1,0:T(8,128)(2,1)}) custom-call(s32[11]{0:T(128)} %stack.56.scalars, bf16[1024,2048]{1,0:T(8,128)(2,1)} %refs_0_.11, f32[1024,128]{1,0:T(8,128)} %shard_map.66.refs_1_.refs_2_, ...), custom_call_target="tpu_custom_call", output_to_operand_aliasing={{0}: (9, {})} | custom-call | flops 1 | bytes 1 | tf_op jit(solution)/shard_map/pallas_call | solution.py:191
  (29 shorter events, 0.0 us)
Async XLA Ops:
  0.0 11.0 %copy-start.2 = (s32[1024]{0:T(1024)S(1)}, s32[1024]{0:T(1024)}, u32[]{:S(2)}) copy-start(s32[1024]{0:T(1024)} %param.9) | copy-start | bytes 12292
  0.0 22.0 %copy-start.3 = (s32[1024]{0:T(1024)S(1)}, s32[1024]{0:T(1024)}, u32[]{:S(2)}) copy-start(s32[1024]{0:T(1024)} %param.8) | copy-start | bytes 12292
  0.0 32.7 %collective-permute-start.2 = (bf16[1024,2048]{1,0:T(8,128)(2,1)}, bf16[1024,2048]{1,0:T(8,128)(2,1)}, u32[]{:S(2)}, u32[]{:S(2)}) collective-permute-start(bf16[1024,2048]{1,0:T(8,128)(2,1)} %refs_0_.11), channel_id=1, source_target_pairs={{0,4},{4,0},{8,12},{12,8},{16,20},{20,16},{24,28},{28,24},{1,5},{5... | collective-permute-start | bytes 12582920 | tf_op jit(solution)/shard_map/ppermute | solution.py:335
  2.7 21.7 %collective-permute-start.3 = (bf16[2048,256]{1,0:T(8,128)(2,1)}, bf16[2048,256]{1,0:T(8,128)(2,1)}, u32[]{:S(2)}, u32[]{:S(2)}) collective-permute-start(bf16[2048,256]{1,0:T(8,128)(2,1)} %shard_map.64.refs_1_), channel_id=1, source_target_pairs={{1,2},{2,1},{5,6},{6,5},{9,10},{10,9},{13,14},{14,13},{17,18},{18,... | collective-permute-start | bytes 3145736 | tf_op jit(solution)/shard_map/ppermute | solution.py:326
  4.4 28.3 %collective-permute-start.1 = (bf16[2048,256]{1,0:T(8,128)(2,1)}, bf16[2048,256]{1,0:T(8,128)(2,1)}, u32[]{:S(2)}, u32[]{:S(2)}) collective-permute-start(bf16[2048,256]{1,0:T(8,128)(2,1)} %shard_map.64.refs_1_), channel_id=1, source_target_pairs={{0,1},{1,0},{2,3},{3,2},{4,5},{5,4},{6,7},{7,6},{8,9},{9,8},{10,11... | collective-permute-start | bytes 3145736 | tf_op jit(solution)/shard_map/ppermute | solution.py:326
  9.6 3.2 %collective-permute-start = (bf16[16,256]{1,0:T(8,128)(2,1)S(1)}, bf16[16,256]{1,0:T(8,128)(2,1)S(1)}, u32[]{:S(2)}, u32[]{:S(2)}) collective-permute-start(bf16[16,256]{1,0:T(8,128)(2,1)S(1)} %slice.18), channel_id=1, source_target_pairs={{0,4},{4,0},{8,12},{12,8},{16,20},{20,16},{24,28},{28,24},{1,5},{5... | collective-permute-start | bytes 24584 | tf_op jit(solution)/shard_map/ppermute | solution.py:335
  12.9 0.6 copy-start.1
  13.5 8.5 %all-to-all-start = ((f32[8,2,128]{2,1,0:T(2,128)}), f32[8,2,128]{2,1,0:T(2,128)S(1)}, u32[]{:S(2)}, u32[]{:S(2)}) async-start(f32[8,2,128]{2,1,0:T(2,128)} %shard_map.65), calls=%async_computation | async-start | bytes 16384 | tf_op jit(solution)/shard_map/all_to_all | solution.py:274
  24.4 33.2 %collective-permute-start.7 = (bf16[2048,256]{1,0:T(8,128)(2,1)}, bf16[2048,256]{1,0:T(8,128)(2,1)}, u32[]{:S(2)}, u32[]{:S(2)}) collective-permute-start(bf16[2048,256]{1,0:T(8,128)(2,1)} %shard_map.67.refs_2_), channel_id=1, source_target_pairs={{1,0},{2,3},{5,4},{6,7},{9,8},{10,11},{13,12},{14,15},{17,16},{18,... | collective-permute-start | bytes 3145736 | tf_op jit(solution)/shard_map/ppermute | solution.py:326
  25.7 27.6 %collective-permute-start.8 = (f32[1024,128]{1,0:T(8,128)}, f32[1024,128]{1,0:T(8,128)}, u32[]{:S(2)}, u32[]{:S(2)}) collective-permute-start(f32[1024,128]{1,0:T(8,128)} %shard_map.66.refs_1_.refs_2_), channel_id=1, source_target_pairs={{0,4},{4,0},{8,12},{12,8},{16,20},{20,16},{24,28},{28,24},{1,5},{5... | collective-permute-start | bytes 1572872 | tf_op jit(solution)/shard_map/ppermute | solution.py:335
  32.7 30.3 %collective-permute-start.5 = (bf16[2048,256]{1,0:T(8,128)(2,1)}, bf16[2048,256]{1,0:T(8,128)(2,1)}, u32[]{:S(2)}, u32[]{:S(2)}) collective-permute-start(bf16[2048,256]{1,0:T(8,128)(2,1)} %get-tuple-element.30.refs_3_.refs_4_), channel_id=1, source_target_pairs={{0,8},{4,20},{8,0},{12,28},{16,24},{20,4},{24,16},{28,12},{1,9},{5... | collective-permute-start | bytes 3145736 | tf_op jit(solution)/shard_map/ppermute | solution.py:329
  34.2 28.8 %collective-permute-start.6 = (bf16[2048,256]{1,0:T(8,128)(2,1)}, bf16[2048,256]{1,0:T(8,128)(2,1)}, u32[]{:S(2)}, u32[]{:S(2)}) collective-permute-start(bf16[2048,256]{1,0:T(8,128)(2,1)} %get-tuple-element.30.refs_3_.refs_4_), channel_id=1, source_target_pairs={{0,16},{4,12},{8,24},{12,4},{16,0},{20,28},{24,8},{28,20},{1,17},{... | collective-permute-start | bytes 3145736 | tf_op jit(solution)/shard_map/ppermute | solution.py:332
  35.7 27.3 %collective-permute-start.4 = (bf16[2048,256]{1,0:T(8,128)(2,1)}, bf16[2048,256]{1,0:T(8,128)(2,1)}, u32[]{:S(2)}, u32[]{:S(2)}) collective-permute-start(bf16[2048,256]{1,0:T(8,128)(2,1)} %get-tuple-element.30.refs_3_.refs_4_), channel_id=1, source_target_pairs={{1,2},{2,1},{5,6},{6,5},{9,10},{10,9},{13,14},{14,13},{17,18},{18,... | collective-permute-start | bytes 3145736 | tf_op jit(solution)/shard_map/ppermute | solution.py:326
  57.6 6.9 %copy-start = (s32[11]{0:T(128)S(1)}, s32[11]{0:T(128)}, u32[]{:S(2)}) copy-start(s32[11]{0:T(128)} %stack.56.scalars) | copy-start | bytes 136
  60.0 25.7 %collective-permute-start.10 = (bf16[2048,256]{1,0:T(8,128)(2,1)}, bf16[2048,256]{1,0:T(8,128)(2,1)}, u32[]{:S(2)}, u32[]{:S(2)}) collective-permute-start(bf16[2048,256]{1,0:T(8,128)(2,1)} %broadcast_select_fusion.1.refs_2_.refs_4_), channel_id=1, source_target_pairs={{0,16},{4,12},{8,24},{12,4},{16,0},{20,28},{24,8},{28,20},{1,17},{... | collective-permute-start | bytes 3145736 | tf_op jit(solution)/shard_map/ppermute | solution.py:332
  61.5 24.2 %collective-permute-start.11 = (bf16[2048,256]{1,0:T(8,128)(2,1)}, bf16[2048,256]{1,0:T(8,128)(2,1)}, u32[]{:S(2)}, u32[]{:S(2)}) collective-permute-start(bf16[2048,256]{1,0:T(8,128)(2,1)} %broadcast_select_fusion.1.refs_2_.refs_4_), channel_id=1, source_target_pairs={{0,8},{4,20},{8,0},{12,28},{16,24},{20,4},{24,16},{28,12},{1,9},{5... | collective-permute-start | bytes 3145736 | tf_op jit(solution)/shard_map/ppermute | solution.py:329
  63.0 26.5 %collective-permute-start.9 = (bf16[2048,256]{1,0:T(8,128)(2,1)}, bf16[2048,256]{1,0:T(8,128)(2,1)}, u32[]{:S(2)}, u32[]{:S(2)}) collective-permute-start(bf16[2048,256]{1,0:T(8,128)(2,1)} %shard_map.72.refs_7_), channel_id=1, source_target_pairs={{1,0},{2,3},{5,4},{6,7},{9,8},{10,11},{13,12},{14,15},{17,16},{18,... | collective-permute-start | bytes 3145736 | tf_op jit(solution)/shard_map/ppermute | solution.py:326
  85.7 22.7 %collective-permute-start.14 = (bf16[2048,256]{1,0:T(8,128)(2,1)}, bf16[2048,256]{1,0:T(8,128)(2,1)}, u32[]{:S(2)}, u32[]{:S(2)}) collective-permute-start(bf16[2048,256]{1,0:T(8,128)(2,1)} %get-tuple-element.37.refs_1_.refs_6_), channel_id=1, source_target_pairs={{0,8},{4,20},{8,0},{12,28},{16,24},{20,4},{24,16},{28,12},{1,9},{5... | collective-permute-start | bytes 3145736 | tf_op jit(solution)/shard_map/ppermute | solution.py:329
  91.9 26.4 %collective-permute-start.12 = (bf16[2048,256]{1,0:T(8,128)(2,1)}, bf16[2048,256]{1,0:T(8,128)(2,1)}, u32[]{:S(2)}, u32[]{:S(2)}) collective-permute-start(bf16[2048,256]{1,0:T(8,128)(2,1)} %broadcast_select_fusion.refs_7_.refs_8_), channel_id=1, source_target_pairs={{0,16},{4,12},{8,24},{12,4},{16,0},{20,28},{24,8},{28,20},{1,17},{... | collective-permute-start | bytes 3145736 | tf_op jit(solution)/shard_map/ppermute | solution.py:332
  92.4 30.9 %collective-permute-start.13 = (bf16[2048,256]{1,0:T(8,128)(2,1)}, bf16[2048,256]{1,0:T(8,128)(2,1)}, u32[]{:S(2)}, u32[]{:S(2)}) collective-permute-start(bf16[2048,256]{1,0:T(8,128)(2,1)} %broadcast_select_fusion.refs_7_.refs_8_), channel_id=1, source_target_pairs={{0,8},{4,20},{8,0},{12,28},{16,24},{20,4},{24,16},{28,12},{1,9},{5... | collective-permute-start | bytes 3145736 | tf_op jit(solution)/shard_map/ppermute | solution.py:329
  92.9 30.9 %collective-permute-start.17 = (bf16[2048,256]{1,0:T(8,128)(2,1)}, bf16[2048,256]{1,0:T(8,128)(2,1)}, u32[]{:S(2)}, u32[]{:S(2)}) collective-permute-start(bf16[2048,256]{1,0:T(8,128)(2,1)} %shard_map.83), channel_id=1, source_target_pairs={{0,1},{1,0},{2,3},{3,2},{4,5},{5,4},{6,7},{7,6},{8,9},{9,8},{10,11... | collective-permute-start | bytes 3145736 | tf_op jit(solution)/shard_map/ppermute | solution.py:326
  115.9 2.3 %collective-permute-start.15 = (bf16[1024,256]{1,0:T(8,128)(2,1)}, bf16[1024,256]{1,0:T(8,128)(2,1)}, u32[]{:S(2)}, u32[]{:S(2)}) collective-permute-start(bf16[1024,256]{1,0:T(8,128)(2,1)} %get-tuple-element.41), channel_id=1, source_target_pairs={{0,4},{4,0},{8,12},{12,8},{16,20},{20,16},{24,28},{28,24},{1,5},{5... | collective-permute-start | bytes 1572872 | tf_op jit(solution)/shard_map/ppermute | solution.py:335
  123.3 16.6 %collective-permute-start.16 = (bf16[2048,256]{1,0:T(8,128)(2,1)}, bf16[2048,256]{1,0:T(8,128)(2,1)}, u32[]{:S(2)}, u32[]{:S(2)}) collective-permute-start(bf16[2048,256]{1,0:T(8,128)(2,1)} %get-tuple-element.43.refs_5_), channel_id=1, source_target_pairs={{0,8},{4,20},{8,0},{12,28},{16,24},{20,4},{24,16},{28,12},{1,9},{5... | collective-permute-start | bytes 3145736 | tf_op jit(solution)/shard_map/ppermute | solution.py:329
  136.8 2.3 %collective-permute-start.18 = (bf16[1024,256]{1,0:T(8,128)(2,1)}, bf16[1024,256]{1,0:T(8,128)(2,1)}, u32[]{:S(2)}, u32[]{:S(2)}) collective-permute-start(bf16[1024,256]{1,0:T(8,128)(2,1)} %get-tuple-element.48), channel_id=1, source_target_pairs={{0,4},{4,0},{8,12},{12,8},{16,20},{20,16},{24,28},{28,24},{1,5},{5... | collective-permute-start | bytes 1572872 | tf_op jit(solution)/shard_map/ppermute | solution.py:335
  136.9 3.0 %collective-permute-start.19 = (bf16[1024,256]{1,0:T(8,128)(2,1)}, bf16[1024,256]{1,0:T(8,128)(2,1)}, u32[]{:S(2)}, u32[]{:S(2)}) collective-permute-start(bf16[1024,256]{1,0:T(8,128)(2,1)} %get-tuple-element.49), channel_id=1, source_target_pairs={{0,4},{4,0},{8,12},{12,8},{16,20},{20,16},{24,28},{28,24},{1,5},{5... | collective-permute-start | bytes 1572872 | tf_op jit(solution)/shard_map/ppermute | solution.py:335
  139.9 3.0 %collective-permute-start.20 = (bf16[2048,256]{1,0:T(8,128)(2,1)}, bf16[2048,256]{1,0:T(8,128)(2,1)}, u32[]{:S(2)}, u32[]{:S(2)}) collective-permute-start(bf16[2048,256]{1,0:T(8,128)(2,1)} %shard_map.87.refs_2_), channel_id=1, source_target_pairs={{0,4},{4,0},{8,12},{12,8},{16,20},{20,16},{24,28},{28,24},{1,5},{5... | collective-permute-start | bytes 3145736 | tf_op jit(solution)/shard_map/ppermute | solution.py:335
